TPU v7x, 512 devices: a whole 4x8x8 slice. The times are simulated.
512 devices in a mesh: req: 32 (over y, x), hist: 16 (over z, core).
Axes of the slice: x: 4, y: 8, z: 8, core: 2. Of those that a mesh axis runs over, the one named last changes fastest.
Arguments:
- codes: int32 [2, 1024], P(None, 'req'), may hold values from 0 to 255
- parents: int32 [1024], P('req'), may hold values from 0 to 63
- lengths: int32 [16], replicated, may hold values from 1 to 32768, as said below
- holders: int32 [16, 32], replicated, may hold values from 0 to 31, each once within a row
- history_keys: bfloat16 [32, 16384, 1024], P('req', 'hist')
- history_values: bfloat16 [32, 16384, 1024], P('req', 'hist')
- query_table: bfloat16 [2, 256, 4096], P(None, None, 'hist')
- kv_table: bfloat16 [2, 256, 2048], P(None, None, 'hist')
- embed_table: bfloat16 [2, 256, 4096], P(None, None, 'hist'), may hold values from -3 to 3
- out_weight: bfloat16 [4096, 4096], P(None, 'hist'), may hold values from -0.375 to 0.375
Outputs:
- layer_out: bfloat16 [2, 1024, 4096], P(None, 'req', 'hist')
Inputs may be any that keep to these rules, and one draw needn't show every extreme that they name: `holders`: each row lists each of the 32 history devices of the request once. `lengths`: at least one request's history fills all 32768 positions.
All inputs are finite; a program needn't handle non-finite values.
Results may differ from a plain program's by a relative error of at most 0.0065.
Values may be sent and summed in bfloat16 or wider, within the bound.
No kernel may reach another device: no remote copies, remote signals or barrier semaphores. Data moves between devices by JAX's collectives and lax.ppermute only.
A program may use at most 128 MiB of HBM per device.

v0:
```python
import jax
import jax.numpy as jnp
from jax import lax
from jax.sharding import PartitionSpec as P

QUERY_HEADS = 32
KEY_HEADS = 8
HEAD_SIZE = 128
LEVEL_COUNT = 2


def partner(array, axis, bit):
    return lax.ppermute(array, axis, [(i, i ^ 1 << bit) for i in range(lax.axis_size(axis))])


def look_rows(table, picks):
    code_ids = jnp.arange(table.shape[0], dtype=jnp.int32)
    one_hot = (picks[:, None] == code_ids[None, :]).astype(jnp.bfloat16)
    return jnp.dot(one_hot, table, preferred_element_type=jnp.float32).astype(jnp.bfloat16)


def combine_parts(first, second):
    first_top, first_total, first_out = first
    second_top, second_total, second_out = second
    best = jnp.maximum(first_top, second_top)
    first_factor = jnp.exp(first_top - best)
    second_factor = jnp.exp(second_top - best)
    total = first_total * first_factor + second_total * second_factor
    merged_out = first_out * first_factor[..., None] + second_out * second_factor[..., None]
    return (best, total, merged_out)


def merge_blocks(stats):
    block_top, block_total, block_out = stats
    head_count = block_top.shape[0]
    best = lax.pmax(block_top, "hist")
    factor = jnp.exp(block_top - best)
    total, summed_out = lax.psum((block_total * factor, block_out * factor[..., None]), "hist")
    return ((best, total, summed_out), 0, head_count)


def split_beams(stats, beams_per_unit, first_half):
    lower_parts = tuple((lax.slice_in_dim(member, 0, beams_per_unit, axis=1) for member in stats))
    upper_parts = tuple(
        (lax.slice_in_dim(member, beams_per_unit, 2 * beams_per_unit, axis=1) for member in stats)
    )
    mine_part = tuple(
        (
            jnp.where(first_half, lower_part, upper_part)
            for lower_part, upper_part in zip(lower_parts, upper_parts)
        )
    )
    other_part = tuple(
        (
            jnp.where(first_half, upper_part, lower_part)
            for lower_part, upper_part in zip(lower_parts, upper_parts)
        )
    )
    return (mine_part, other_part)


def shards(
    codes,
    parents,
    lengths,
    holders,
    history_keys,
    history_values,
    query_table,
    kv_table,
    embed_table,
    out_weight,
):
    hist_count = lax.axis_size("hist")
    hist_index = lax.axis_index("hist")
    device_row = lax.axis_index("req")
    half_index = device_row % 2
    request = device_row // 2
    place = half_index * hist_count + hist_index
    span_count = 2 * hist_count
    beams_per_unit = parents.shape[0]
    every_beam = 2 * beams_per_unit
    slot_positions = history_keys.shape[1]
    key_feature_width = KEY_HEADS * HEAD_SIZE
    query_group_width = QUERY_HEADS // KEY_HEADS
    scale_factor = HEAD_SIZE ** (-0.5)
    request_ids = jnp.arange(lengths.shape[0], dtype=jnp.int32)
    length_here = jnp.sum(jnp.where(request_ids == request, lengths, 0))
    holder_row = jnp.sum(jnp.where(request_ids[:, None] == request, holders, 0), axis=0)
    block_ids = jnp.arange(span_count, dtype=jnp.int32)
    position = jnp.sum(jnp.where(holder_row == place, block_ids, 0))
    live_slots = (
        position * slot_positions + jnp.arange(slot_positions, dtype=jnp.int32) < length_here
    )
    block_key_rows = history_keys[0].reshape(slot_positions, KEY_HEADS, HEAD_SIZE)
    block_value_rows = history_values[0].reshape(slot_positions, KEY_HEADS, HEAD_SIZE)
    first_half = half_index == 0
    parent_hot = (parents[:, None] == jnp.arange(every_beam, dtype=jnp.int32)[None, :]).astype(
        jnp.bfloat16
    )
    results = []
    earlier_rows = None
    for level_index in range(LEVEL_COUNT):
        picks = codes[level_index]
        query_part = look_rows(query_table[level_index], picks)
        kv_part = look_rows(kv_table[level_index], picks)
        query_mine, kv_mine = (
            lax.all_gather(query_part, "hist", axis=1, tiled=True),
            lax.all_gather(kv_part, "hist", axis=1, tiled=True),
        )
        query_other, kv_other = partner((query_mine, kv_mine), "req", 0)
        complete_query = jnp.where(
            first_half,
            jnp.concatenate([query_mine, query_other], 0),
            jnp.concatenate([query_other, query_mine], 0),
        )
        kv_full = jnp.where(
            first_half,
            jnp.concatenate([kv_mine, kv_other], 0),
            jnp.concatenate([kv_other, kv_mine], 0),
        )
        query_vectors = complete_query.reshape(every_beam, KEY_HEADS, query_group_width, HEAD_SIZE)
        scores = (
            jnp.einsum(
                "bgrd,tgd->grbt", query_vectors, block_key_rows, preferred_element_type=jnp.float32
            )
            * scale_factor
        )
        block_top = jnp.max(jnp.where(live_slots, scores, -1e30), axis=-1)
        weights = jnp.where(live_slots, jnp.exp(scores - block_top[..., None]), 0.0).astype(
            jnp.bfloat16
        )
        block_total = jnp.sum(weights, axis=-1, dtype=jnp.float32)
        block_out = jnp.einsum(
            "grbt,tgd->grbd", weights, block_value_rows, preferred_element_type=jnp.float32
        )
        stats = (
            block_top.reshape(QUERY_HEADS, every_beam),
            block_total.reshape(QUERY_HEADS, every_beam),
            block_out.reshape(QUERY_HEADS, every_beam, HEAD_SIZE),
        )
        merged, head_start, heads_here = merge_blocks(stats)
        mine_part, other_part = split_beams(merged, beams_per_unit, first_half)
        arrived = partner(other_part, "req", 0)
        final = combine_parts(mine_part, arrived)
        if level_index == 0:
            gen_rows = [kv_mine]
        else:
            parent_rows = jnp.dot(
                parent_hot, earlier_rows, preferred_element_type=jnp.float32
            ).astype(jnp.bfloat16)
            gen_rows = [parent_rows, kv_mine]
        earlier_rows = kv_full
        final_top, final_total, final_out = final
        query_heads = query_mine.reshape(beams_per_unit, QUERY_HEADS, HEAD_SIZE)
        overall = final_top
        gen_parts = []
        for generated_row in gen_rows:
            generated_keys = jnp.repeat(
                generated_row[:, :key_feature_width].reshape(beams_per_unit, KEY_HEADS, HEAD_SIZE),
                query_group_width,
                axis=1,
            )
            generated_values = jnp.repeat(
                generated_row[:, key_feature_width:].reshape(beams_per_unit, KEY_HEADS, HEAD_SIZE),
                query_group_width,
                axis=1,
            )
            gen_score = (
                jnp.einsum(
                    "bhd,bhd->hb", query_heads, generated_keys, preferred_element_type=jnp.float32
                )
                * scale_factor
            )
            overall = jnp.maximum(overall, gen_score)
            gen_parts.append((gen_score, generated_values))
        block_factor = jnp.exp(final_top - overall)
        denominator = final_total * block_factor
        numerator = final_out * block_factor[..., None]
        for gen_score, generated_values in gen_parts:
            gen_weight = jnp.exp(gen_score - overall)
            denominator = denominator + gen_weight
            numerator = numerator + gen_weight[..., None] * jnp.transpose(
                generated_values, (1, 0, 2)
            ).astype(jnp.float32)
        attention_part = (
            jnp.transpose(numerator / denominator[..., None], (1, 0, 2))
            .reshape(beams_per_unit, heads_here * HEAD_SIZE)
            .astype(jnp.bfloat16)
        )
        projected = jnp.dot(attention_part, out_weight, preferred_element_type=jnp.float32)
        residual_rows = look_rows(embed_table[level_index], picks).astype(jnp.float32)
        results.append((residual_rows + projected).astype(jnp.bfloat16))
    return jnp.stack(results)


def solution(mesh):
    in_specs = (
        P(None, "req"),
        P("req"),
        P(),
        P(),
        P("req", "hist", None),
        P("req", "hist", None),
        P(None, None, "hist"),
        P(None, None, "hist"),
        P(None, None, "hist"),
        P(None, "hist"),
    )
    out_specs = P(None, "req", "hist")
    return jax.shard_map(shards, mesh=mesh, in_specs=in_specs, out_specs=out_specs, check_vma=False)
```

profile of v0, /device:TPU:57, one launch (start us, length us, event | category | flops | bytes accessed | tf_op | source)
XLA Modules:
  0.0 346.6 jit_solution(7371107341267039184)
XLA Ops:
  6.5 0.8 slice_bitcast_fusion.4
  7.4 1.1 convolution_convert_fusion.1
  8.5 24.4 %all_gather.14 = bf16[32,4096]{1,0:T(8,128)(2,1)S(1)} all-gather(bf16[32,256]{1,0:T(8,128)(2,1)S(1)} %convolution_convert_fusion.1), channel_id=1, replica_groups=mesh['req'=32,'hist'=16] {'hist'}, dimensions={1}, use_global_device_ids=true | all-gather | bytes 278528 | tf_op jit(solution)/shard_map/all_gather | solution.py:108
  32.8 3.1 collective-permute-start.4
  36.0 1.1 convolution_convert_fusion.3
  37.0 15.2 %all_gather.12 = bf16[32,4096]{1,0:T(8,128)(2,1)S(1)} all-gather(bf16[32,256]{1,0:T(8,128)(2,1)S(1)} %convolution_convert_fusion.3), channel_id=1, replica_groups=mesh['req'=32,'hist'=16] {'hist'}, dimensions={1}, use_global_device_ids=true | all-gather | bytes 278528 | tf_op jit(solution)/shard_map/all_gather | solution.py:108
  52.2 2.2 collective-permute-start
  54.4 1.0 convolution_convert_fusion.6
  55.4 18.1 %all_gather.13 = bf16[32,2048]{1,0:T(8,128)(2,1)} all-gather(bf16[32,128]{1,0:T(8,128)(2,1)S(1)} %convolution_convert_fusion.6), channel_id=1, replica_groups=mesh['req'=32,'hist'=16] {'hist'}, dimensions={1}, use_global_device_ids=true | all-gather | bytes 139264 | tf_op jit(solution)/shard_map/all_gather | solution.py:109
  73.5 3.1 collective-permute-start.7
  76.6 0.9 slice_bitcast_fusion.2
  77.5 1.0 convolution_convert_fusion.5
  78.5 1.7 fusion.17
  80.3 1.7 fusion.16
  82.0 1.4 select_reduce_fusion.1
  83.4 14.8 %all_gather.15 = bf16[32,2048]{1,0:T(8,128)(2,1)S(1)} all-gather(bf16[32,128]{1,0:T(8,128)(2,1)S(1)} %convolution_convert_fusion.5), channel_id=1, replica_groups=mesh['req'=32,'hist'=16] {'hist'}, dimensions={1}, use_global_device_ids=true | all-gather | bytes 139264 | tf_op jit(solution)/shard_map/all_gather | solution.py:109
  98.2 0.7 slice_bitcast_fusion
  98.9 0.8 select_reduce_fusion
  101.1 3.6 %copy.107 = bf16[128,8,8,128]{3,2,1,0:T(8,128)(2,1)} copy(bf16[128,8,8,128]{3,1,2,0:T(8,128)(2,1)} %bitcast.136) | data formatting | bytes 4194304
  104.7 0.8 copy.44
  106.2 3.5 %copy.108 = bf16[128,8,8,128]{3,2,1,0:T(8,128)(2,1)} copy(bf16[128,8,8,128]{3,1,2,0:T(8,128)(2,1)} %bitcast.137) | data formatting | bytes 4194304
  109.7 0.7 copy.111
  111.8 0.7 add_compare_fusion
  112.5 1.3 convolution_convert_fusion
  115.1 1.1 concatenate.35
  116.4 1.1 concatenate.31
  117.6 3.0 fusion.12
  120.6 3.6 %fusion.4 = (f32[8,4,64]{2,1,0:T(4,128)S(1)}, f32[8,4,64]{2,1,0:T(4,128)S(1)}, f32[8,64,4,1024]{3,1,2,0:T(8,128)S(1)}) fusion(pred[1024]{0:T(1024)(128)(4,1)S(1)} %add_compare_fusion, f32[8,64,4,1024]{3,1,2,0:T(8,128)S(1)} %fusion.12, bf16[1024,8,128,1]{2,1,0,3:T(8,128)(2,1)S(1)} %bitcast.131, bf16[32,8,4,128]{3,0,2,1:T(8,128)(2,1)S(1)} %copy.45, ...), kind=kOutput, calls=%fused_computation.8 | convolution fusion | flops 551809024 | bytes 19416064 | tf_op jit(solution)/shard_map/bgrd,tgd->grbt/dot_general | solution.py:124
  124.3 3.8 %convert_reduce_fusion.1 = (f32[8,4,64]{2,1,0:T(4,128)S(1)}, f32[8,4,64]{2,1,0:T(4,128)S(1)}) fusion(f32[8,4,64]{2,1,0:T(4,128)S(1)} %get-tuple-element.9, f32[8,64,4,1024]{3,1,2,0:T(8,128)S(1)} %get-tuple-element.44, pred[1024]{0:T(1024)(128)(4,1)S(1)} %add_compare_fusion, f32[8,4,64]{2,1,0:T(4,128)S(1)} %get-tuple-element.10, f32[8,64,4,1024]{3,1,2,0:T(8,128)S(1)} %fusion.12), kind=kLoop, calls=%fused_computation.13 | loop fusion | flops 25161728 | bytes 16811008 | tf_op jit(solution)/shard_map/reduce_sum | solution.py:133
  128.1 3.0 fusion.10
  131.1 3.0 fusion.8
  134.1 44.2 %all-reduce.2 = (f32[32,64]{1,0:T(8,128)S(1)}, f32[32,64]{1,0:T(8,128)S(1)}) all-reduce(f32[32,64]{1,0:T(8,128)S(1)} %bitcast.158, f32[32,64]{1,0:T(8,128)S(1)} %bitcast.156), channel_id=1, replica_groups=mesh['req'=32,'hist'=16] {'hist'}, use_global_device_ids=true, to_apply=%region_9.10 | all-reduce | flops 4096 | bytes 32768 | tf_op jit(solution)/shard_map/pmax | solution.py:36
  178.5 2.9 copy_multiply_fusion.1
  181.4 2.9 copy_multiply_fusion
  185.6 0.7 copy.95
  186.3 45.7 %all-reduce = (f32[32,64]{1,0:T(8,128)S(1)}, f32[32,64]{1,0:T(8,128)S(1)}) all-reduce(f32[32,64]{1,0:T(8,128)S(1)} %get-tuple-element.45, f32[32,64]{1,0:T(8,128)S(1)} %get-tuple-element.28), channel_id=1, replica_groups=mesh['req'=32,'hist'=16] {'hist'}, use_global_device_ids=true, to_apply=%region_12.13 | all-reduce | flops 4096 | bytes 32768 | tf_op jit(solution)/shard_map/psum | solution.py:38
  232.0 0.7 slice_select_fusion.5
  232.7 2.2 collective-permute-start.3
  234.8 0.7 slice_select_fusion.6
  235.5 3.1 collective-permute-start.1
  239.3 2.2 collective-permute-start.8
  241.5 0.7 slice_select_fusion.3
  242.2 3.1 collective-permute-start.5
  245.3 60.5 %all-reduce.5.cloned.1.call-done = (f32[32,64,128]{2,0,1:T(8,128)}, f32[32,64,128]{2,0,1:T(8,128)}) async-done(((f32[32,64,128]{2,0,1:T(8,128)}, f32[32,64,128]{2,0,1:T(8,128)}), (f32[32,64,128]{2,0,1:T(8,128)}, f32[32,64,128]{2,0,1:T(8,128)})) %all-reduce.5.cloned.1.call-update) | async-done | bytes 2097168 | tf_op jit(solution)/shard_map/psum | solution.py:38
  305.8 2.2 slice_select_fusion.1
  308.0 3.1 collective-permute-start.2
  311.1 1.5 add_add_fusion
  312.6 2.1 slice_select_fusion
  314.7 2.2 collective-permute-start.6
  316.9 1.5 multiply_add_fusion
  318.4 1.4 copy.52
  319.7 1.4 copy.53
  321.1 1.4 copy.54
  322.5 1.4 copy.55
  323.9 1.4 copy.56
  325.3 0.8 copy.65
  326.1 1.4 copy.66
  327.5 1.4 copy.67
  328.9 1.4 copy.68
  330.3 1.4 copy.69
  331.7 1.4 copy.70
  333.2 2.0 divide_convert_fusion.1
  335.3 1.1 fusion.21
  336.7 2.0 divide_convert_fusion
  (68 shorter events, 7.9 us)
Async XLA Ops:
  6.5 328.7 %copy-start = (bf16[4096,256]{1,0:T(8,128)(2,1)S(1)}, bf16[4096,256]{1,0:T(8,128)(2,1)}, u32[]{:S(2)}) copy-start(bf16[4096,256]{1,0:T(8,128)(2,1)} %param.19) | copy-start | bytes 6291460
  6.5 299.3 %all-reduce.5.cloned.1.call-start = ((), (), s32[]{:S(2)}) async-start(), calls=%async_computation | async-start | bytes 4194304 | tf_op jit(solution)/shard_map/psum | solution.py:38
  32.8 82.3 %collective-permute-start.4 = (bf16[32,4096]{1,0:T(8,128)(2,1)S(1)}, bf16[32,4096]{1,0:T(8,128)(2,1)}, u32[]{:S(2)}, u32[]{:S(2)}) collective-permute-start(bf16[32,4096]{1,0:T(8,128)(2,1)S(1)} %all_gather.14), channel_id=1, source_target_pairs={{0,16},{16,0},{32,48},{48,32},{64,80},{80,64},{96,112},{112,96},{1... | collective-permute-start | bytes 786440 | tf_op jit(solution)/shard_map/ppermute | solution.py:13
  52.2 64.1 %collective-permute-start = (bf16[32,4096]{1,0:T(8,128)(2,1)S(1)}, bf16[32,4096]{1,0:T(8,128)(2,1)}, u32[]{:S(2)}, u32[]{:S(2)}) collective-permute-start(bf16[32,4096]{1,0:T(8,128)(2,1)S(1)} %all_gather.12), channel_id=1, source_target_pairs={{0,16},{16,0},{32,48},{48,32},{64,80},{80,64},{96,112},{112,96},{1... | collective-permute-start | bytes 786440 | tf_op jit(solution)/shard_map/ppermute | solution.py:13
  73.5 39.0 %collective-permute-start.7 = (bf16[32,2048]{1,0:T(8,128)(2,1)}, bf16[32,2048]{1,0:T(8,128)(2,1)}, u32[]{:S(2)}, u32[]{:S(2)}) collective-permute-start(bf16[32,2048]{1,0:T(8,128)(2,1)} %all_gather.13), channel_id=1, source_target_pairs={{0,16},{16,0},{32,48},{48,32},{64,80},{80,64},{96,112},{112,96},{1... | collective-permute-start | bytes 393224 | tf_op jit(solution)/shard_map/ppermute | solution.py:13
  101.1 9.4 %copy-start.9 = (bf16[4,8,8,128]{3,1,2,0:T(8,128)(2,1)S(1)}, bf16[4,8,8,128]{3,1,2,0:T(8,128)(2,1)}, u32[]{:S(2)}) copy-start(bf16[4,8,8,128]{3,1,2,0:T(8,128)(2,1)} %get-tuple-element.34) | copy-start | bytes 196612
  101.1 10.0 %copy-start.6 = (f32[4,8,8,128]{3,1,2,0:T(8,128)S(1)}, f32[4,8,8,128]{3,1,2,0:T(8,128)}, u32[]{:S(2)}) copy-start(f32[4,8,8,128]{3,1,2,0:T(8,128)} %get-tuple-element.35) | copy-start | bytes 393220
  101.1 11.3 %copy-start.12 = (s32[32]{0:T(128)S(1)}, s32[32]{0:T(128)}, u32[]{:S(2)}) copy-start(s32[32]{0:T(128)} %param.11) | copy-start | bytes 388
  117.5 3.1 copy-start.1
  124.2 3.8 %copy-start.3 = (bf16[128,8,8,128]{3,2,1,0:T(8,128)(2,1)S(1)}, bf16[128,8,8,128]{3,2,1,0:T(8,128)(2,1)}, u32[]{:S(2)}) copy-start(bf16[128,8,8,128]{3,2,1,0:T(8,128)(2,1)} %copy.108) | copy-start | bytes 6291460
  131.1 53.3 %copy-start.8 = (bf16[4,8,8,128]{3,2,1,0:T(8,128)(2,1)S(1)}, bf16[4,8,8,128]{3,2,1,0:T(8,128)(2,1)}, u32[]{:S(2)}) copy-start(bf16[4,8,8,128]{3,2,1,0:T(8,128)(2,1)} %copy.114) | copy-start | bytes 196612
  131.1 53.3 %copy-start.7 = (bf16[4,8,8,128]{3,2,1,0:T(8,128)(2,1)S(1)}, bf16[4,8,8,128]{3,2,1,0:T(8,128)(2,1)}, u32[]{:S(2)}) copy-start(bf16[4,8,8,128]{3,2,1,0:T(8,128)(2,1)} %copy.115) | copy-start | bytes 196612
  131.1 55.1 %copy-start.5 = (f32[4,8,8,128]{3,1,2,0:T(8,128)S(1)}, f32[4,8,8,128]{3,1,2,0:T(8,128)}, u32[]{:S(2)}) copy-start(f32[4,8,8,128]{3,1,2,0:T(8,128)} %get-tuple-element.37) | copy-start | bytes 393220
  134.1 198.9 %copy-start.4 = (f32[4,8,8,128]{3,2,1,0:T(8,128)S(1)}, f32[4,8,8,128]{3,2,1,0:T(8,128)}, u32[]{:S(2)}) copy-start(f32[4,8,8,128]{3,2,1,0:T(8,128)} %copy.111) | copy-start | bytes 393220
  232.0 13.3 %copy-start.10 = (f32[32,64]{1,0:T(8,128)}, f32[32,64]{1,0:T(8,128)S(1)}, u32[]{:S(2)}) copy-start(f32[32,64]{1,0:T(8,128)S(1)} %get-tuple-element.11) | copy-start | bytes 24580
  232.7 84.2 %collective-permute-start.3 = (f32[32,32]{1,0:T(8,128)}, f32[32,32]{1,0:T(8,128)}, u32[]{:S(2)}, u32[]{:S(2)}) collective-permute-start(f32[32,32]{1,0:T(8,128)} %slice_select_fusion.5), channel_id=1, source_target_pairs={{0,16},{16,0},{32,48},{48,32},{64,80},{80,64},{96,112},{112,96},{1... | collective-permute-start | bytes 12296 | tf_op jit(solution)/shard_map/ppermute | solution.py:13
  235.5 81.3 %collective-permute-start.1 = (f32[32,32]{1,0:T(8,128)}, f32[32,32]{1,0:T(8,128)}, u32[]{:S(2)}, u32[]{:S(2)}) collective-permute-start(f32[32,32]{1,0:T(8,128)} %get-tuple-element.38), channel_id=1, source_target_pairs={{0,16},{16,0},{32,48},{48,32},{64,80},{80,64},{96,112},{112,96},{1... | collective-permute-start | bytes 12296 | tf_op jit(solution)/shard_map/ppermute | solution.py:13
  239.3 71.8 %collective-permute-start.8 = (f32[32,32]{1,0:T(8,128)}, f32[32,32]{1,0:T(8,128)}, u32[]{:S(2)}, u32[]{:S(2)}) collective-permute-start(f32[32,32]{1,0:T(8,128)} %slice_select_fusion.2), channel_id=1, source_target_pairs={{0,16},{16,0},{32,48},{48,32},{64,80},{80,64},{96,112},{112,96},{1... | collective-permute-start | bytes 12296 | tf_op jit(solution)/shard_map/ppermute | solution.py:13
  242.2 68.9 %collective-permute-start.5 = (f32[32,32]{1,0:T(8,128)}, f32[32,32]{1,0:T(8,128)}, u32[]{:S(2)}, u32[]{:S(2)}) collective-permute-start(f32[32,32]{1,0:T(8,128)} %get-tuple-element.40), channel_id=1, source_target_pairs={{0,16},{16,0},{32,48},{48,32},{64,80},{80,64},{96,112},{112,96},{1... | collective-permute-start | bytes 12296 | tf_op jit(solution)/shard_map/ppermute | solution.py:13
  305.8 30.9 %copy-start.2 = (f32[32,64,128]{2,0,1:T(8,128)S(1)}, f32[32,64,128]{2,0,1:T(8,128)}, u32[]{:S(2)}) copy-start(f32[32,64,128]{2,0,1:T(8,128)} %get-tuple-element.13) | copy-start | bytes 3145732
  308.0 25.1 %collective-permute-start.2 = (f32[32,32,128]{2,0,1:T(8,128)}, f32[32,32,128]{2,0,1:T(8,128)}, u32[]{:S(2)}, u32[]{:S(2)}) collective-permute-start(f32[32,32,128]{2,0,1:T(8,128)} %slice_select_fusion.1), channel_id=1, source_target_pairs={{0,16},{16,0},{32,48},{48,32},{64,80},{80,64},{96,112},{112,96},{1... | collective-permute-start | bytes 1572872 | tf_op jit(solution)/shard_map/ppermute | solution.py:13
  314.7 21.7 %collective-permute-start.6 = (f32[32,32,128]{2,0,1:T(8,128)}, f32[32,32,128]{2,0,1:T(8,128)}, u32[]{:S(2)}, u32[]{:S(2)}) collective-permute-start(f32[32,32,128]{2,0,1:T(8,128)} %slice_select_fusion), channel_id=1, source_target_pairs={{0,16},{16,0},{32,48},{48,32},{64,80},{80,64},{96,112},{112,96},{1... | collective-permute-start | bytes 1572872 | tf_op jit(solution)/shard_map/ppermute | solution.py:13
  333.0 5.7 %copy-start.11 = (f32[32,256]{1,0:T(8,128)S(1)}, f32[32,256]{1,0:T(8,128)}, u32[]{:S(2)}) copy-start(f32[32,256]{1,0:T(8,128)} %fusion.16) | copy-start | bytes 98308
Sparse Core Ops, SparseCore 0:
  184.5 121.3 all-reduce.4
where the time goes:
time: 350 us; the launch traced here: 347 us
  blocking collectives  162 us (46%)
  waiting for transfers between devices  60.6 us (17%)
  local copies, waits for them, and re-layouts  31.3 us (9%)
  other arithmetic  30.5 us (9%)
  starting transfers between devices  24.2 us (7%)
  matrix products  23.2 us (7%)
  between operations  14.5 us (4%)
    psum x1, waiting for transfers between devices, merge_blocks(): lax.psum((block_total * factor, block_out * factor[..., None]), 'hist')  60.5 us
    psum x1, blocking collectives, merge_blocks(): lax.psum((block_total * factor, block_out * factor[..., None]), 'hist')  45.7 us
    pmax x1, blocking collectives, merge_blocks(): best = lax.pmax(block_top, 'hist')  44.2 us
    all_gather x2, blocking collectives, shards(): lax.all_gather(query_part, 'hist', axis=1, tiled=True)  39.5 us
    all_gather x2, blocking collectives, shards(): lax.all_gather(kv_part, 'hist', axis=1, tiled=True)  32.9 us
    ppermute x9, starting transfers between devices, partner(): lax.ppermute(array, axis, [(i, i ^ 1 << bit) for i in range(lax.axis_size...  24.2 us
    unnamed x36, local copies, waits for them, and re-layouts  9.32 us
    dot_general x6, matrix products, look_rows(): jnp.dot(one_hot, table, preferred_element_type=jnp.float32)  7.65 us
  transfers between devices with their start and end apart: 10, of which 1 were waited for; matrix products, arithmetic and copies ran while one was open for 16% of the time, Pallas kernels for 0%

commit v1 on v0

v1 whole, which is shorter than its diff:
```python
import functools
import math

import jax
import jax.numpy as jnp
from jax import lax
from jax.experimental import pallas as pl
from jax.experimental.pallas import tpu as pltpu
from jax.sharding import Mesh, PartitionSpec as P

KEY_HEADS = 8
HEAD = 128
STAT = 16
CHUNK = HEAD + STAT
DEAD = -1e30
EXP2_SCALE = HEAD ** (-0.5) * math.log2(math.e)
VMEM_LIMIT = 48 * 1024 * 1024


def params():
    return pltpu.CompilerParams(vmem_limit_bytes=VMEM_LIMIT)


def one_hot_rows(index_row, count):
    rows = index_row.shape[1]
    tall = jnp.transpose(jnp.broadcast_to(index_row, (128, rows)))
    parts = []
    for start in range(0, count, 128):
        lane = lax.broadcasted_iota(jnp.int32, (rows, 128), 1) + start
        parts.append((tall == lane).astype(jnp.float32).astype(jnp.bfloat16))
    return jnp.concatenate(parts, axis=1)


def look_kernel(index_ref, query_ref, kv_ref, query_out, kv_out):
    hot = one_hot_rows(index_ref[...], query_ref.shape[0])
    query_out[...] = jnp.dot(hot, query_ref[...], preferred_element_type=jnp.float32).astype(jnp.bfloat16)
    kv_out[...] = jnp.dot(hot, kv_ref[...], preferred_element_type=jnp.float32).astype(jnp.bfloat16)


def residual_kernel(index_ref, embed_ref, out_ref):
    hot = one_hot_rows(index_ref[...], embed_ref.shape[0])
    out_ref[...] = jnp.dot(hot, embed_ref[...], preferred_element_type=jnp.float32)[: out_ref.shape[0]]


def split3(value):
    high = value.astype(jnp.bfloat16).astype(jnp.float32)
    rest = value - high
    middle = rest.astype(jnp.bfloat16).astype(jnp.float32)
    return high, middle, rest - middle


def stat_rows(top, total):
    row = lax.broadcasted_iota(jnp.int32, (STAT, top.shape[1]), 0)
    out = jnp.zeros((STAT, top.shape[1]), jnp.float32)
    for at, piece in enumerate(split3(top) + split3(total)):
        out = jnp.where(row == at, piece, out)
    return out.astype(jnp.bfloat16)


def read_stats(rows):
    wide = rows.astype(jnp.float32)
    return wide[0:1] + wide[1:2] + wide[2:3], wide[3:4] + wide[4:5] + wide[5:6]


def attend_kernel(
    meta_ref, lengths_ref, holders_ref, query_ref, key_ref, value_ref, gen_key_ref, gen_value_ref, parent_ref,
    keep_ref, send_ref, live_ref, sums_ref, top_ref,
):
    group = pl.program_id(0)
    slots = key_ref.shape[0]
    request, place, core, gen_head = meta_ref[0], meta_ref[1], meta_ref[2], meta_ref[3]
    half = query_ref.shape[1] // 2

    @pl.when(group == 0)
    def _():
        position = jnp.int32(0)
        for block in range(holders_ref.shape[1]):
            position = jnp.where(holders_ref[request, block] == place, block, position)
        live_ref[0] = jnp.clip(lengths_ref[request] - position * slots, 0, slots)

    live = live_ref[0]

    def queries(local):
        pair = query_ref[2 * group + jnp.bitwise_xor(core, local)]
        return jnp.concatenate(
            [pair[x * half : (x + 1) * half, h * HEAD : (h + 1) * HEAD] for x in range(2) for h in range(2)], axis=0
        )

    def extended(values):
        return jnp.concatenate([jnp.transpose(values), jnp.ones((STAT, values.shape[0]), jnp.bfloat16)], axis=0)

    def scores_of(keys, rows):
        return lax.dot_general(keys, rows, (((1,), (1,)), ((), ())), preferred_element_type=jnp.float32)

    def attend(masked):
        keys = key_ref[...]
        values = extended(value_ref[...])
        width = 4 * half
        for local in range(2):
            lanes = slice(local * width, (local + 1) * width)
            scores = scores_of(keys, queries(local))
            if masked:
                slot = lax.broadcasted_iota(jnp.int32, (slots, 1), 0)
                scores = jnp.where(slot < live, scores, DEAD)
            top = jnp.max(scores, axis=0, keepdims=True)
            weights = jnp.exp2((scores - top) * EXP2_SCALE).astype(jnp.bfloat16)
            sums_ref[:, lanes] = jnp.dot(values, weights, preferred_element_type=jnp.float32)
            top_ref[:, lanes] = jnp.broadcast_to(top, (8, width))

    @pl.when(live == slots)
    def _():
        attend(False)

    @pl.when((live > 0) & (live < slots))
    def _():
        attend(True)

    @pl.when(live == 0)
    def _():
        sums_ref[...] = jnp.zeros(sums_ref.shape, jnp.float32)
        top_ref[...] = jnp.full(top_ref.shape, DEAD, jnp.float32)

    @pl.when(group == gen_head)
    def _():
        keys = gen_key_ref[...]
        values = extended(gen_value_ref[...])
        width = 4 * half
        row = lax.broadcasted_iota(jnp.int32, (2 * half, width), 0)
        lane = lax.broadcasted_iota(jnp.int32, (2 * half, width), 1)
        own = (lane // (2 * half)) * half + lane % half
        allowed = (row == own) | (row == parent_ref[...])
        for local in range(2):
            lanes = slice(local * width, (local + 1) * width)
            scores = jnp.where(allowed, scores_of(keys, queries(local)), DEAD)
            before = top_ref[0:1, lanes]
            top = jnp.maximum(before, jnp.max(scores, axis=0, keepdims=True))
            weights = jnp.where(allowed, jnp.exp2((scores - top) * EXP2_SCALE), 0.0)
            high = weights.astype(jnp.bfloat16)
            low = (weights - high.astype(jnp.float32)).astype(jnp.bfloat16)
            added = jnp.dot(values, high, preferred_element_type=jnp.float32)
            added = added + jnp.dot(values, low, preferred_element_type=jnp.float32)
            sums_ref[:, lanes] = sums_ref[:, lanes] * jnp.exp2((before - top) * EXP2_SCALE) + added
            top_ref[:, lanes] = jnp.broadcast_to(top, (8, width))

    for local, out_ref in enumerate((keep_ref, send_ref)):
        for x in range(2):
            lanes = slice(local * 4 * half + x * 2 * half, local * 4 * half + (x + 1) * 2 * half)
            out_ref[x, 0, 0:HEAD] = sums_ref[0:HEAD, lanes].astype(jnp.bfloat16)
            out_ref[x, 0, HEAD:CHUNK] = stat_rows(top_ref[0:1, lanes], sums_ref[HEAD : HEAD + 1, lanes])


def merge_kernel(mine_ref, other_ref, out_ref):
    for chunk in range(mine_ref.shape[0]):
        tops, totals = zip(*(read_stats(ref[chunk, HEAD:CHUNK]) for ref in (mine_ref, other_ref)))
        top = jnp.maximum(*tops)
        factors = [jnp.exp2((each - top) * EXP2_SCALE) for each in tops]
        total = totals[0] * factors[0] + totals[1] * factors[1]
        sums = (
            mine_ref[chunk, 0:HEAD].astype(jnp.float32) * factors[0]
            + other_ref[chunk, 0:HEAD].astype(jnp.float32) * factors[1]
        )
        out_ref[chunk, 0:HEAD] = sums.astype(jnp.bfloat16)
        out_ref[chunk, HEAD:CHUNK] = stat_rows(top, total)


def combine_kernel(parts_ref, out_ref):
    count = parts_ref.shape[0]
    stats = [read_stats(parts_ref[part, HEAD:CHUNK]) for part in range(count)]
    top = functools.reduce(jnp.maximum, [each for each, _ in stats])
    total = jnp.zeros_like(top)
    sums = jnp.zeros((HEAD, parts_ref.shape[2]), jnp.float32)
    for part in range(count):
        factor = jnp.exp2((stats[part][0] - top) * EXP2_SCALE)
        total = total + stats[part][1] * factor
        sums = sums + parts_ref[part, 0:HEAD].astype(jnp.float32) * factor
    tall = jnp.transpose(sums / total)
    rows = out_ref.shape[0]
    out_ref[...] = jnp.concatenate([tall[0:rows], tall[rows : 2 * rows]], axis=1).astype(jnp.bfloat16)


def project_kernel(rows_ref, weight_ref, residual_ref, out_ref):
    total = residual_ref[...]
    width = rows_ref.shape[2]
    for part in range(rows_ref.shape[0]):
        total = total + jnp.dot(
            rows_ref[part], weight_ref[part * width : (part + 1) * width], preferred_element_type=jnp.float32
        )
    out_ref[...] = total.astype(jnp.bfloat16)


def shards(
    codes, parents, lengths, holders, history_keys, history_values, query_table, kv_table, embed_table, out_weight
):
    beams = parents.shape[0]
    levels, code_count, width = query_table.shape
    half = levels * beams
    rows = 2 * half
    slots = history_keys.shape[1]
    z_count = lax.axis_size("z")
    pair, z, core = lax.axis_index("pair"), lax.axis_index("z"), lax.axis_index("core")
    hist = 2 * z + core
    first = pair == 0
    bf16, f32 = jnp.bfloat16, jnp.float32

    own_index = (codes + code_count * jnp.arange(levels, dtype=jnp.int32)[:, None]).reshape(half)
    mine = jnp.concatenate([own_index, parents])
    other = lax.ppermute(mine, "pair", [(0, 1), (1, 0)])
    residual = pl.pallas_call(
        residual_kernel,
        out_shape=jax.ShapeDtypeStruct((half, width), f32),
        compiler_params=params(),
        name="residual",
    )(jnp.concatenate([own_index, own_index]).reshape(1, rows), embed_table.reshape(levels * code_count, width))

    lower = jnp.where(first, mine, other)
    upper = jnp.where(first, other, mine)
    index = jnp.concatenate([lower[:half], upper[:half]]).reshape(1, rows)
    query_rows, kv_rows = pl.pallas_call(
        look_kernel,
        out_shape=(
            jax.ShapeDtypeStruct((rows, width), bf16),
            jax.ShapeDtypeStruct((rows, HEAD), bf16),
        ),
        compiler_params=params(),
        name="look",
    )(index, query_table.reshape(levels * code_count, width), kv_table.reshape(levels * code_count, HEAD))
    gen_values = lax.ppermute(kv_rows, "z", [(i + z_count // 2, i) for i in range(z_count // 2)])
    queries = lax.all_gather(query_rows, ("z", "core"), axis=0)

    both = jnp.stack([lower[half:], upper[half:]])
    parent_rows = (both // beams) * half + both % beams
    parent_lanes = jnp.concatenate([jnp.full((2, beams), -1, jnp.int32), parent_rows], axis=1)
    parent_lanes = jnp.broadcast_to(parent_lanes[:, None, :], (2, 2, half)).reshape(1, 2 * rows)

    gen_head = jnp.where(first & (z < z_count // 2), hist, -1)
    meta = jnp.stack([lax.axis_index("grp"), pair * 2 * z_count + hist, core, gen_head]).astype(jnp.int32)
    partial_shape = jax.ShapeDtypeStruct((2, z_count, CHUNK, 2 * half), bf16)
    whole = lambda *shape: pl.BlockSpec(shape, lambda g, *_: (0,) * len(shape))
    keep, send = pl.pallas_call(
        attend_kernel,
        out_shape=(partial_shape, partial_shape),
        grid_spec=pltpu.PrefetchScalarGridSpec(
            num_scalar_prefetch=3,
            grid=(KEY_HEADS,),
            in_specs=[
                whole(2 * z_count, rows, width),
                pl.BlockSpec((slots, HEAD), lambda g, *_: (0, g)),
                pl.BlockSpec((slots, HEAD), lambda g, *_: (0, g)),
                whole(rows, HEAD),
                whole(rows, HEAD),
                whole(1, 2 * rows),
            ],
            out_specs=[pl.BlockSpec((2, 1, CHUNK, 2 * half), lambda g, *_: (0, g, 0, 0))] * 2,
            scratch_shapes=[
                pltpu.SMEM((1,), jnp.int32),
                pltpu.VMEM((CHUNK, 4 * rows), f32),
                pltpu.VMEM((8, 4 * rows), f32),
            ],
        ),
        compiler_params=params(),
        cost_estimate=pl.CostEstimate(
            flops=4 * 4 * rows * KEY_HEADS * slots * HEAD,
            bytes_accessed=4 * slots * KEY_HEADS * HEAD,
            transcendentals=4 * rows * KEY_HEADS * slots,
        ),
        name="attend",
    )(meta, lengths, holders, queries, history_keys[0], history_values[0], kv_rows, gen_values, parent_lanes)

    shape = (2 * z_count, CHUNK, 2 * half)
    arrived = lax.ppermute(send, "core", [(0, 1), (1, 0)])
    merged = pl.pallas_call(
        merge_kernel, out_shape=jax.ShapeDtypeStruct(shape, bf16), compiler_params=params(), name="merge"
    )(keep.reshape(shape), arrived.reshape(shape))
    parts = lax.all_to_all(merged, ("pair", "z"), split_axis=0, concat_axis=0, tiled=True)
    attention = pl.pallas_call(
        combine_kernel,
        out_shape=jax.ShapeDtypeStruct((half, width), bf16),
        compiler_params=params(),
        name="combine",
    )(parts)
    gathered = lax.all_gather(attention, ("z", "core"), axis=0)
    out = pl.pallas_call(
        project_kernel,
        out_shape=jax.ShapeDtypeStruct((half, width), bf16),
        compiler_params=params(),
        name="project",
    )(gathered, out_weight, residual)
    return out.reshape(levels, beams, width)


def solution(mesh):
    split = Mesh(mesh.devices.reshape(16, 2, 8, 2), ("grp", "pair", "z", "core"))
    req, hist = ("grp", "pair"), ("z", "core")
    in_specs = (
        P(None, req),
        P(req),
        P(),
        P(),
        P(req, hist, None),
        P(req, hist, None),
        P(None, None, hist),
        P(None, None, hist),
        P(None, None, hist),
        P(None, hist),
    )
    return jax.shard_map(shards, mesh=split, in_specs=in_specs, out_specs=P(None, req, hist), check_vma=False)
```

time: 350 us -> 138 us (0.39)
  blocking collectives: 162 us -> 19.9 us
  other arithmetic: 30.5 us -> 2.46 us
  local copies, waits for them, and re-layouts: 31.3 us -> 6.35 us
  matrix products: 23.2 us -> 0 us
  Pallas kernels: 0 us -> 19 us
  starting transfers between devices: 24.2 us -> 11.1 us
  waiting for transfers between devices: 60.6 us -> 64.3 us
    psum x1 -> x0, waiting for transfers between devices: 60.5 us -> none  [merge_blocks(): lax.psum((block_total * factor, block_out * factor[..., None]), 'hist')]
    all_gather x4 -> x1, blocking collectives: 72.4 us -> 19.9 us  [shards(): gathered = lax.all_gather(attention, ('z', 'core'), axis=0)]
    psum x1 -> x0, blocking collectives: 45.7 us -> none  [merge_blocks(): lax.psum((block_total * factor, block_out * factor[..., None]), 'hist')]
    pmax x1 -> x0, blocking collectives: 44.2 us -> none  [merge_blocks(): best = lax.pmax(block_top, 'hist')]
    all_gather x0 -> x1, waiting for transfers between devices: none -> 36.3 us  [shards(): queries = lax.all_gather(query_rows, ('z', 'core'), axis=0)]
    dot_general x13 -> x0, matrix products: 23.2 us -> none  [the longest x6 7.65 us: look_rows(): jnp.dot(one_hot, table, preferred_element_type=jnp.float32)]
    pallas_call x0 -> x6, Pallas kernels: none -> 19 us  [the longest x1 15.5 us: shards(): pl.pallas_call(attend_kernel, out_shape=(partial_shape, partial_shape), g...]
    ppermute x9 -> x3, starting transfers between devices: 24.2 us -> 6.68 us  [the longest x1 3.11 us: shards(): other = lax.ppermute(mine, 'pair', [(0, 1), (1, 0)])]
  transfers between devices with their start and end apart: 10 -> 5, of which waited for: 1 -> 5; matrix products, arithmetic and copies ran while one was open for 16% -> 0% of each run, Pallas kernels for 0% -> 0%
where the time goes in v1:
time: 138 us; the launch traced here: 137 us
  waiting for transfers between devices  64.3 us (47%)
  blocking collectives  19.9 us (14%)
  Pallas kernels  19 us (14%)
  between operations  13.5 us (10%)
  starting transfers between devices  11.1 us (8%)
  local copies, waits for them, and re-layouts  6.35 us (5%)
  other arithmetic  2.46 us (2%)
    all_gather x1, waiting for transfers between devices, shards(): queries = lax.all_gather(query_rows, ('z', 'core'), axis=0)  36.3 us
    all_gather x1, blocking collectives, shards(): gathered = lax.all_gather(attention, ('z', 'core'), axis=0)  19.9 us
    pallas_call x1, Pallas kernels, shards(): pl.pallas_call(attend_kernel, out_shape=(partial_shape, partial_shape), g...  15.5 us
    all_to_all x1, waiting for transfers between devices, shards(): lax.all_to_all(merged, ('pair', 'z'), split_axis=0, concat_axis=0, tiled=...  15.4 us
    ppermute x1, waiting for transfers between devices, shards(): lax.ppermute(kv_rows, 'z', [(i + z_count // 2, i) for i in range(z_count...  9.78 us
    unnamed x16, local copies, waits for them, and re-layouts  6.03 us
    all_to_all x1, starting transfers between devices, shards(): lax.all_to_all(merged, ('pair', 'z'), split_axis=0, concat_axis=0, tiled=...  4.43 us
    ppermute x1, starting transfers between devices, shards(): other = lax.ppermute(mine, 'pair', [(0, 1), (1, 0)])  3.11 us
  transfers between devices with their start and end apart: 5, of which 5 were waited for; matrix products, arithmetic and copies ran while one was open for 0% of the time, Pallas kernels for 0%

profile of v1, /device:TPU:57, one launch (start us, length us, event | category | flops | bytes accessed | tf_op | source)
XLA Modules:
  0.0 136.6 jit_solution(7336279719409866482)
XLA Ops:
  6.5 0.0 all-gather.4.cloned.1.call-start
  6.5 0.7 broadcast_add_fusion
  7.3 0.1 reshape.36
  7.4 0.7 pad_add_fusion.2
  8.1 3.1 %collective-permute-start = (s32[96]{0:T(128)S(1)}, s32[96]{0:T(128)S(1)}, u32[]{:S(2)}, u32[]{:S(2)}) collective-permute-start(s32[96]{0:T(128)S(1)} %pad_add_fusion.2), channel_id=1, source_target_pairs={{0,16},{16,0},{1,17},{17,1},{2,18},{18,2},{3,19},{19,3},{4,20},{20... | collective-permute-start | bytes 1160 | tf_op jit(solution)/shard_map/ppermute | solution.py:207
  11.2 1.1 collective-permute-done
  12.4 0.7 broadcast_select_fusion.1
  13.1 0.1 add_bitcast_fusion.index_ref
  13.2 0.0 copy-start.2
  13.2 0.9 copy-done.2
  14.1 0.0 copy-start.3
  14.1 0.9 copy-done.3
  15.0 0.9 look.1
  15.9 0.0 all-gather.4.cloned.1.call-update
  16.0 0.1 pad_add_fusion.1.meta_ref
  16.1 1.3 collective-permute-start.1
  17.3 0.1 slice_bitcast_fusion
  17.4 0.1 concatenate.14
  17.5 0.1 reshape.40.parent_ref
  17.6 9.8 %collective-permute-done.1.gen_value_ref = bf16[128,128]{1,0:T(8,128)(2,1)S(1)} collective-permute-done((bf16[128,128]{1,0:T(8,128)(2,1)S(1)}, bf16[128,128]{1,0:T(8,128)(2,1)S(1)}, u32[]{:S(2)}, u32[]{:S(2)}) %collective-permute-start.1) | collective-permute-done | bytes 32800 | tf_op jit(solution)/shard_map/ppermute | solution.py:227
  27.4 36.3 %all-gather.4.cloned.1.call-done = bf16[2048,256]{1,0:T(8,128)(2,1)} async-done(((bf16[128,256]{1,0:T(8,128)(2,1)}), bf16[2048,256]{1,0:T(8,128)(2,1)}) %all-gather.4.cloned.1.call-update) | async-done | bytes 1048592 | tf_op jit(solution)/shard_map/all_gather | solution.py:228
  63.6 0.0 copy-start.4
  63.7 1.6 %copy-done.4 = bf16[1,1024,1024]{2,1,0:T(8,128)(2,1)S(1)} copy-done((bf16[1,1024,1024]{2,1,0:T(8,128)(2,1)S(1)}, bf16[1,1024,1024]{2,1,0:T(8,128)(2,1)}, u32[]{:S(2)}) %copy-start.4) | copy-done | bytes 2097176
  65.2 0.0 copy-start.5
  65.2 1.2 copy-done.5
  66.5 0.0 copy-start.6
  66.5 0.7 copy-done.6
  67.2 0.0 copy-start.7
  67.2 0.7 copy-done.7
  67.8 15.5 %attend.1 = (bf16[2,8,144,128]{3,2,1,0:T(8,128)(2,1)S(1)}, bf16[2,8,144,128]{3,2,1,0:T(8,128)(2,1)S(1)}) custom-call(s32[4]{0:T(128)S(1)} %pad_add_fusion.1.meta_ref, s32[16]{0:T(128)S(1)} %copy-done.7, s32[16,32]{1,0:T(8,128)S(1)} %copy-done.6, bf16[16,128,256]{2,1,0:T(8,128)(2,1)S(1)} %bitcast.31, bf16[1024,1024]{1,0:T(8,128)(2,1)S(1)} %bitcast.30, ...), custom_call_target="tpu_custom_call" | custom-call | flops 2147483648 | bytes 4194304 | tf_op jit(solution)/shard_map/attend/pallas_call | solution.py:239
  83.3 0.0 copy-start.1
  83.3 2.3 %collective-permute-start.2 = (bf16[2,8,144,128]{3,2,1,0:T(8,128)(2,1)S(1)}, bf16[2,8,144,128]{3,2,1,0:T(8,128)(2,1)S(1)}, u32[]{:S(2)}, u32[]{:S(2)}) collective-permute-start(bf16[2,8,144,128]{3,2,1,0:T(8,128)(2,1)S(1)} %get-tuple-element.12), channel_id=1, source_target_pairs={{0,1},{1,0},{2,3},{3,2},{4,5},{5,4},{6,7},{7,6},{8,9},{9,8},{10,11... | collective-permute-start | bytes 1769480 | tf_op jit(solution)/shard_map/ppermute | solution.py:270
  85.6 1.7 %collective-permute-done.2 = bf16[2,8,144,128]{3,2,1,0:T(8,128)(2,1)S(1)} collective-permute-done((bf16[2,8,144,128]{3,2,1,0:T(8,128)(2,1)S(1)}, bf16[2,8,144,128]{3,2,1,0:T(8,128)(2,1)S(1)}, u32[]{:S(2)}, u32[]{:S(2)}) %collective-permute-start.2) | collective-permute-done | bytes 589856 | tf_op jit(solution)/shard_map/ppermute | solution.py:270
  87.3 0.0 copy-start
  87.3 1.2 merge.1
  88.5 4.4 %all-to-all-start = ((bf16[16,144,128]{2,1,0:T(8,128)(2,1)}), bf16[16,144,128]{2,1,0:T(8,128)(2,1)S(1)}, u32[]{:S(2)}, u32[]{:S(2)}) async-start(bf16[16,144,128]{2,1,0:T(8,128)(2,1)} %merge.1), calls=%async_computation | async-start | bytes 1179648 | tf_op jit(solution)/shard_map/all_to_all | solution.py:274
  92.9 0.1 add_bitcast_fusion.1.index_ref
  93.0 0.0 copy-done.1
  93.0 0.2 residual.1.residual_ref
  93.2 15.4 %all-to-all-done.parts_ref = bf16[16,144,128]{2,1,0:T(8,128)(2,1)S(1)} async-done(((bf16[16,144,128]{2,1,0:T(8,128)(2,1)}), bf16[16,144,128]{2,1,0:T(8,128)(2,1)S(1)}, u32[]{:S(2)}, u32[]{:S(2)}) %all-to-all-start) | async-done | bytes 589856 | tf_op jit(solution)/shard_map/all_to_all | solution.py:274
  108.6 0.2 combine.1
  108.9 19.9 %all-gather.1 = bf16[1024,256]{1,0:T(8,128)(2,1)S(1)} all-gather(bf16[64,256]{1,0:T(8,128)(2,1)S(1)} %combine.1), channel_id=3, replica_groups=mesh['grp'=16,'pair'=2,'z'=8,'core'=2] {'z','core'}, dimensions={0}, use_global_device_ids=true | all-gather | bytes 557056 | tf_op jit(solution)/shard_map/all_gather | solution.py:281
  128.7 0.0 copy-done
  128.7 1.1 project.1
  (3 shorter events, 0.0 us)
Async XLA Ops:
  6.5 57.1 %all-gather.4.cloned.1.call-start = ((), (), s32[]{:S(2)}) async-start(), calls=%async_computation.1 | async-start | bytes 1114112 | tf_op jit(solution)/shard_map/all_gather | solution.py:228
  8.1 4.3 %collective-permute-start = (s32[96]{0:T(128)S(1)}, s32[96]{0:T(128)S(1)}, u32[]{:S(2)}, u32[]{:S(2)}) collective-permute-start(s32[96]{0:T(128)S(1)} %pad_add_fusion.2), channel_id=1, source_target_pairs={{0,16},{16,0},{1,17},{17,1},{2,18},{18,2},{3,19},{19,3},{4,20},{20... | collective-permute-start | bytes 1160 | tf_op jit(solution)/shard_map/ppermute | solution.py:207
  13.2 0.9 copy-start.2
  14.1 0.9 copy-start.3
  16.1 11.3 %collective-permute-start.1 = (bf16[128,128]{1,0:T(8,128)(2,1)S(1)}, bf16[128,128]{1,0:T(8,128)(2,1)S(1)}, u32[]{:S(2)}, u32[]{:S(2)}) collective-permute-start(bf16[128,128]{1,0:T(8,128)(2,1)S(1)} %get-tuple-element.10.gen_key_ref), channel_id=1, source_target_pairs={{8,0},{10,2},{12,4},{14,6},{9,1},{11,3},{13,5},{15,7},{24,16},{26,... | collective-permute-start | bytes 98312 | tf_op jit(solution)/shard_map/ppermute | solution.py:227
  63.6 1.6 %copy-start.4 = (bf16[1,1024,1024]{2,1,0:T(8,128)(2,1)S(1)}, bf16[1,1024,1024]{2,1,0:T(8,128)(2,1)}, u32[]{:S(2)}) copy-start(bf16[1,1024,1024]{2,1,0:T(8,128)(2,1)} %param.14) | copy-start | bytes 6291460
  65.2 1.2 copy-start.5
  66.5 0.7 copy-start.6
  67.2 0.7 copy-start.7
  83.3 9.7 %copy-start.1 = (bf16[2,256,256]{2,1,0:T(8,128)(2,1)S(1)}, bf16[2,256,256]{2,1,0:T(8,128)(2,1)}, u32[]{:S(2)}) copy-start(bf16[2,256,256]{2,1,0:T(8,128)(2,1)} %param.18) | copy-start | bytes 786436
  83.3 4.0 %collective-permute-start.2 = (bf16[2,8,144,128]{3,2,1,0:T(8,128)(2,1)S(1)}, bf16[2,8,144,128]{3,2,1,0:T(8,128)(2,1)S(1)}, u32[]{:S(2)}, u32[]{:S(2)}) collective-permute-start(bf16[2,8,144,128]{3,2,1,0:T(8,128)(2,1)S(1)} %get-tuple-element.12), channel_id=1, source_target_pairs={{0,1},{1,0},{2,3},{3,2},{4,5},{5,4},{6,7},{7,6},{8,9},{9,8},{10,11... | collective-permute-start | bytes 1769480 | tf_op jit(solution)/shard_map/ppermute | solution.py:270
  87.3 41.4 %copy-start = (bf16[4096,256]{1,0:T(8,128)(2,1)S(1)}, bf16[4096,256]{1,0:T(8,128)(2,1)}, u32[]{:S(2)}) copy-start(bf16[4096,256]{1,0:T(8,128)(2,1)} %weight_ref.1) | copy-start | bytes 6291460
  88.5 20.1 %all-to-all-start = ((bf16[16,144,128]{2,1,0:T(8,128)(2,1)}), bf16[16,144,128]{2,1,0:T(8,128)(2,1)S(1)}, u32[]{:S(2)}, u32[]{:S(2)}) async-start(bf16[16,144,128]{2,1,0:T(8,128)(2,1)} %merge.1), calls=%async_computation | async-start | bytes 1179648 | tf_op jit(solution)/shard_map/all_to_all | solution.py:274
Sparse Core Ops, SparseCore 0:
  16.1 47.5 all-gather.3

commit v2 on v1

v2 whole, which is shorter than its diff:
```python
import functools
import math

import jax
import jax.numpy as jnp
from jax import lax
from jax.experimental import pallas as pl
from jax.experimental.pallas import tpu as pltpu
from jax.sharding import Mesh, PartitionSpec as P

KEY_HEADS = 8
HEAD = 128
STAT = 16
CHUNK = HEAD + STAT
DEAD = -1e30
EXP2_SCALE = HEAD ** (-0.5) * math.log2(math.e)
VMEM_LIMIT = 32 * 1024 * 1024


def params():
    return pltpu.CompilerParams(vmem_limit_bytes=VMEM_LIMIT)


def one_hot_rows(index_row, count):
    rows = index_row.shape[1]
    tall = jnp.transpose(jnp.broadcast_to(index_row, (128, rows)))
    parts = []
    for start in range(0, count, 128):
        lane = lax.broadcasted_iota(jnp.int32, (rows, 128), 1) + start
        parts.append((tall == lane).astype(jnp.float32).astype(jnp.bfloat16))
    return jnp.concatenate(parts, axis=1)


def look(hot, table_ref):
    return jnp.dot(hot, table_ref[...], preferred_element_type=jnp.float32)


def own_kernel(index_ref, query_ref, kv_ref, embed_ref, query_out, kv_out, residual_out):
    rows = query_out.shape[0]
    hot = one_hot_rows(index_ref[...], query_ref.shape[0])
    query_out[...] = look(hot, query_ref)[:rows].astype(jnp.bfloat16)
    kv_out[...] = look(hot, kv_ref)[:rows].astype(jnp.bfloat16)
    residual_out[...] = look(hot, embed_ref)[:rows]


def both_kernel(pair_ref, index_ref, query_ref, kv_ref, own_query_ref, own_kv_ref, query_out, kv_out):
    rows = own_query_ref.shape[0]
    hot = one_hot_rows(index_ref[...], query_ref.shape[0])
    mine = pl.ds(pl.multiple_of(pair_ref[0] * rows, rows), rows)
    theirs = pl.ds(pl.multiple_of((1 - pair_ref[0]) * rows, rows), rows)
    query_out[mine] = own_query_ref[...]
    query_out[theirs] = look(hot, query_ref)[:rows].astype(jnp.bfloat16)
    kv_out[mine] = own_kv_ref[...]
    kv_out[theirs] = look(hot, kv_ref)[:rows].astype(jnp.bfloat16)


def stage_kernel(key_ref, value_ref, key_out, value_out):
    slots = key_ref.shape[0]
    for head in range(key_out.shape[0]):
        lanes = slice(head * HEAD, (head + 1) * HEAD)
        key_out[head] = key_ref[:, lanes]
        value_out[head, 0:HEAD] = jnp.transpose(value_ref[:, lanes])
        value_out[head, HEAD:CHUNK] = jnp.ones((STAT, slots), jnp.bfloat16)


def split3(value):
    high = value.astype(jnp.bfloat16).astype(jnp.float32)
    rest = value - high
    middle = rest.astype(jnp.bfloat16).astype(jnp.float32)
    return high, middle, rest - middle


def stat_rows(top, total):
    row = lax.broadcasted_iota(jnp.int32, (STAT, top.shape[1]), 0)
    out = jnp.zeros((STAT, top.shape[1]), jnp.float32)
    for at, piece in enumerate(split3(top) + split3(total)):
        out = jnp.where(row == at, piece, out)
    return out.astype(jnp.bfloat16)


def read_stats(rows):
    wide = rows.astype(jnp.float32)
    return wide[0:1] + wide[1:2] + wide[2:3], wide[3:4] + wide[4:5] + wide[5:6]


def scores_of(keys, rows):
    return lax.dot_general(keys, rows, (((1,), (1,)), ((), ())), preferred_element_type=jnp.float32)


def attend_kernel(
    meta_ref, lengths_ref, holders_ref, query_ref, key_ref, value_ref, gen_key_ref, gen_value_ref, parent_ref,
    out_ref, score_ref,
):
    heads, slots = key_ref.shape[0], key_ref.shape[1]
    half = query_ref.shape[1] // 2
    width = 4 * half
    request, place, gen_head = meta_ref[0], meta_ref[1], meta_ref[2]

    position = jnp.int32(0)
    for block in range(holders_ref.shape[1]):
        position = jnp.where(holders_ref[request, block] == place, block, position)
    live = jnp.clip(lengths_ref[request] - position * slots, 0, slots)

    def queries(head):
        pair = query_ref[head]
        return jnp.concatenate(
            [pair[x * half : (x + 1) * half, h * HEAD : (h + 1) * HEAD] for x in range(2) for h in range(2)], axis=0
        )

    def write(head, sums, total, top):
        for x in range(2):
            lanes = slice(x * 2 * half, (x + 1) * 2 * half)
            out_ref[x, head, 0:HEAD] = sums[:, lanes].astype(jnp.bfloat16)
            out_ref[x, head, HEAD:CHUNK] = stat_rows(top[:, lanes], total[:, lanes])

    def attend(masked):
        def score(head, slot):
            scores = scores_of(key_ref[head], queries(head))
            if masked:
                scores = jnp.where(lax.broadcasted_iota(jnp.int32, (slots, 1), 0) < live, scores, DEAD)
            score_ref[slot] = scores
            return jnp.max(scores, axis=0, keepdims=True)

        def finish(head, slot, top):
            weights = jnp.exp2((score_ref[slot] - top) * EXP2_SCALE).astype(jnp.bfloat16)
            sums = jnp.dot(value_ref[head], weights, preferred_element_type=jnp.float32)
            write(head, sums[0:HEAD], sums[HEAD : HEAD + 1], top)

        def step(i, top):
            later = score(2 * i + 1, 1)
            finish(2 * i, 0, top)
            top = score(jnp.minimum(2 * i + 2, heads - 1), 0)
            finish(2 * i + 1, 1, later)
            return top

        top = lax.fori_loop(0, heads // 2 - 1, step, score(0, 0))
        later = score(heads - 1, 1)
        finish(heads - 2, 0, top)
        finish(heads - 1, 1, later)

    @pl.when(live == slots)
    def _():
        attend(False)

    @pl.when((live > 0) & (live < slots))
    def _():
        attend(True)

    @pl.when(live == 0)
    def _():
        row = lax.broadcasted_iota(jnp.int32, (CHUNK, 2 * half), 0)
        tops = split3(jnp.full((CHUNK, 2 * half), DEAD, jnp.float32))
        dead = jnp.zeros((CHUNK, 2 * half), jnp.float32)
        for at, piece in enumerate(tops):
            dead = jnp.where(row == HEAD + at, piece, dead)
        dead = dead.astype(jnp.bfloat16)
        for x in range(2):
            for head in range(heads):
                out_ref[x, head] = dead

    @pl.when(gen_head >= 0)
    def _():
        values = jnp.concatenate(
            [jnp.transpose(gen_value_ref[...]), jnp.ones((STAT, 2 * half), jnp.bfloat16)], axis=0
        )
        row = lax.broadcasted_iota(jnp.int32, (2 * half, width), 0)
        lane = lax.broadcasted_iota(jnp.int32, (2 * half, width), 1)
        own = (lane // (2 * half)) * half + lane % half
        allowed = (row == own) | (row == parent_ref[...])
        scores = jnp.where(allowed, scores_of(gen_key_ref[...], queries(gen_head)), DEAD)
        before = jnp.concatenate([out_ref[x, gen_head] for x in range(2)], axis=1)
        old_top, old_total = read_stats(before[HEAD:CHUNK])
        top = jnp.maximum(old_top, jnp.max(scores, axis=0, keepdims=True))
        weights = jnp.where(allowed, jnp.exp2((scores - top) * EXP2_SCALE), 0.0)
        high = weights.astype(jnp.bfloat16)
        low = (weights - high.astype(jnp.float32)).astype(jnp.bfloat16)
        added = jnp.dot(values, high, preferred_element_type=jnp.float32)
        added = added + jnp.dot(values, low, preferred_element_type=jnp.float32)
        factor = jnp.exp2((old_top - top) * EXP2_SCALE)
        sums = before[0:HEAD].astype(jnp.float32) * factor + added[0:HEAD]
        write(gen_head, sums, old_total * factor + added[HEAD : HEAD + 1], top)


def merge_kernel(mine_ref, other_ref, out_ref):
    for chunk in range(mine_ref.shape[0]):
        tops, totals = zip(*(read_stats(ref[chunk, HEAD:CHUNK]) for ref in (mine_ref, other_ref)))
        top = jnp.maximum(*tops)
        factors = [jnp.exp2((each - top) * EXP2_SCALE) for each in tops]
        total = totals[0] * factors[0] + totals[1] * factors[1]
        sums = (
            mine_ref[chunk, 0:HEAD].astype(jnp.float32) * factors[0]
            + other_ref[chunk, 0:HEAD].astype(jnp.float32) * factors[1]
        )
        out_ref[chunk, 0:HEAD] = sums.astype(jnp.bfloat16)
        out_ref[chunk, HEAD:CHUNK] = stat_rows(top, total)


def combine_kernel(parts_ref, out_ref):
    count = parts_ref.shape[0]
    stats = [read_stats(parts_ref[part, HEAD:CHUNK]) for part in range(count)]
    top = functools.reduce(jnp.maximum, [each for each, _ in stats])
    total = jnp.zeros_like(top)
    sums = jnp.zeros((HEAD, parts_ref.shape[2]), jnp.float32)
    for part in range(count):
        factor = jnp.exp2((stats[part][0] - top) * EXP2_SCALE)
        total = total + stats[part][1] * factor
        sums = sums + parts_ref[part, 0:HEAD].astype(jnp.float32) * factor
    tall = jnp.transpose(sums / total)
    rows = out_ref.shape[0]
    out_ref[...] = jnp.concatenate([tall[0:rows], tall[rows : 2 * rows]], axis=1).astype(jnp.bfloat16)


def project_kernel(parity, core_ref, rows_ref, weight_ref, before_ref, out_ref):
    total = before_ref[...]
    at = jnp.bitwise_xor(core_ref[0], parity)
    for part in range(rows_ref.shape[0]):
        total = total + jnp.dot(rows_ref[part], weight_ref[part, at], preferred_element_type=jnp.float32)
    out_ref[...] = total.astype(out_ref.dtype)


def call(kernel, out_shape, scalars, name, **rest):
    specs = lambda count, space: [pl.BlockSpec(memory_space=space)] * count

    def run(*args):
        return pl.pallas_call(
            kernel,
            out_shape=out_shape,
            in_specs=specs(scalars, pltpu.SMEM) + specs(len(args) - scalars, pltpu.VMEM),
            out_specs=jax.tree.map(lambda _: pl.BlockSpec(memory_space=pltpu.VMEM), out_shape),
            compiler_params=params(),
            name=name,
            **rest,
        )(*args)

    return run


def shards(
    codes, parents, lengths, holders, history_keys, history_values, query_table, kv_table, embed_table, out_weight
):
    beams = parents.shape[0]
    levels, code_count, width = query_table.shape
    half = levels * beams
    rows = 2 * half
    slots = history_keys.shape[1]
    z_count = lax.axis_size("z")
    pair, z, core = lax.axis_index("pair"), lax.axis_index("z"), lax.axis_index("core")
    hist = 2 * z + core
    first = pair == 0
    bf16, f32 = jnp.bfloat16, jnp.float32
    array = jax.ShapeDtypeStruct
    swap = [(0, 1), (1, 0)]

    other_codes = lax.ppermute(codes, "pair", swap)
    other_parents = lax.ppermute(parents, "pair", swap)

    def index_of(picks):
        flat = (picks + code_count * jnp.arange(levels, dtype=jnp.int32)[:, None]).reshape(half)
        return jnp.concatenate([flat, flat]).reshape(1, rows)

    query_flat = query_table.reshape(levels * code_count, width)
    kv_flat = kv_table.reshape(levels * code_count, HEAD)
    embed_flat = embed_table.reshape(levels * code_count, width)
    own_query, own_kv, residual = call(
        own_kernel, (array((half, width), bf16), array((half, HEAD), bf16), array((half, width), f32)), 0, "own"
    )(index_of(codes), query_flat, kv_flat, embed_flat)
    staged_keys, staged_values = call(
        stage_kernel,
        (array((KEY_HEADS, slots, HEAD), bf16), array((KEY_HEADS, CHUNK, slots), bf16)),
        0,
        "stage",
    )(history_keys[0], history_values[0])

    query_rows, kv_rows = call(both_kernel, (array((rows, width), bf16), array((rows, HEAD), bf16)), 1, "both")(
        pair.reshape(1), index_of(other_codes), query_flat, kv_flat, own_query, own_kv
    )
    gen_values = lax.ppermute(kv_rows, "z", [(i + z_count // 2, i) for i in range(z_count // 2)])
    near_queries = lax.all_gather(query_rows, "z", axis=0)
    far_queries = lax.ppermute(near_queries, "core", swap)

    lower = jnp.where(first, parents, other_parents)
    upper = jnp.where(first, other_parents, parents)
    both = jnp.stack([lower, upper])
    parent_rows = (both // beams) * half + both % beams
    parent_lanes = jnp.concatenate([jnp.full((2, beams), -1, jnp.int32), parent_rows], axis=1)
    parent_lanes = jnp.broadcast_to(parent_lanes[:, None, :], (2, 2, half)).reshape(1, 2 * rows)

    gen_head = jnp.where(first & (z < z_count // 2), hist, -1)
    meta = jnp.stack([lax.axis_index("grp"), pair * 2 * z_count + hist, gen_head]).astype(jnp.int32)
    attend = call(
        attend_kernel,
        array((2, z_count, CHUNK, 2 * half), bf16),
        3,
        "attend",
        scratch_shapes=[pltpu.VMEM((2, slots, 2 * rows), f32)],
        cost_estimate=pl.CostEstimate(
            flops=2 * 4 * rows * KEY_HEADS * slots * HEAD,
            bytes_accessed=4 * slots * KEY_HEADS * HEAD,
            transcendentals=2 * rows * KEY_HEADS * slots,
        ),
    )
    rest = (staged_keys, staged_values, kv_rows, gen_values, parent_lanes)
    send = attend(meta, lengths, holders, near_queries, *rest)
    arrived = lax.ppermute(send, "core", swap)
    keep = attend(meta, lengths, holders, far_queries, *rest)

    shape = (2 * z_count, CHUNK, 2 * half)
    merged = call(merge_kernel, array(shape, bf16), 0, "merge")(keep.reshape(shape), arrived.reshape(shape))
    parts = lax.all_to_all(merged, ("pair", "z"), split_axis=0, concat_axis=0, tiled=True)
    attention = call(combine_kernel, array((half, width), bf16), 0, "combine")(parts)
    near_rows = lax.all_gather(attention, "z", axis=0)
    far_rows = lax.ppermute(near_rows, "core", swap)
    weight = out_weight.reshape(z_count, 2, width, width)
    place = core.reshape(1)
    begun = call(functools.partial(project_kernel, 1), array((half, width), f32), 1, "project_near")(
        place, near_rows, weight, residual
    )
    out = call(functools.partial(project_kernel, 0), array((half, width), bf16), 1, "project_far")(
        place, far_rows, weight, begun
    )
    return out.reshape(levels, beams, width)


def solution(mesh):
    split = Mesh(mesh.devices.reshape(16, 2, 8, 2), ("grp", "pair", "z", "core"))
    req, hist = ("grp", "pair"), ("z", "core")
    in_specs = (
        P(None, req),
        P(req),
        P(),
        P(),
        P(req, hist, None),
        P(req, hist, None),
        P(None, None, hist),
        P(None, None, hist),
        P(None, None, hist),
        P(None, hist),
    )
    return jax.shard_map(shards, mesh=split, in_specs=in_specs, out_specs=P(None, req, hist), check_vma=False)
```

time: 138 us -> 115 us (0.83)
  waiting for transfers between devices: 64.3 us -> 0.83 us
  blocking collectives: 19.9 us -> 66.3 us
  starting transfers between devices: 11.1 us -> 27.7 us
  between operations: 13.5 us -> 0.26 us
  Pallas kernels: 19 us -> 12.4 us
  other arithmetic: 2.46 us -> 0.33 us
    all_gather x1 -> x0, waiting for transfers between devices: 36.3 us -> none  [shards(): queries = lax.all_gather(query_rows, ('z', 'core'), axis=0)]
    all_gather x1 -> x2, blocking collectives: 19.9 us -> 45.2 us  [the longest x1 26.2 us: shards(): near_queries = lax.all_gather(query_rows, 'z', axis=0)]
    all_to_all x0 -> x1, blocking collectives: none -> 21.1 us  [shards(): lax.all_to_all(merged, ('pair', 'z'), split_axis=0, concat_axis=0, tiled=...]
    ppermute x2 -> x5, starting transfers between devices: 5.4 us -> 26.4 us  [the longest x1 10.3 us: shards(): far_rows = lax.ppermute(near_rows, 'core', swap)]
    all_to_all x1 -> x0, waiting for transfers between devices: 15.4 us -> none  [shards(): lax.all_to_all(merged, ('pair', 'z'), split_axis=0, concat_axis=0, tiled=...]
    ppermute x1, waiting for transfers between devices: 9.78 us -> 0.01 us  [shards(): lax.ppermute(kv_rows, 'z', [(i + z_count // 2, i) for i in range(z_count...]
    pallas_call x6 -> x9, Pallas kernels: 19 us -> 12.4 us  [run(): pl.pallas_call(kernel, out_shape=out_shape, in_specs=specs(scalars, pltpu...]
    all_to_all x1 -> x0, starting transfers between devices: 4.43 us -> none  [shards(): lax.all_to_all(merged, ('pair', 'z'), split_axis=0, concat_axis=0, tiled=...]
  transfers between devices with their start and end apart: 5 -> 6, of which waited for: 5 -> 1; matrix products, arithmetic and copies ran while one was open for 0% -> 0% of each run, Pallas kernels for 0% -> 9%
where the time goes in v2:
time: 115 us; the launch traced here: 114 us
  blocking collectives  66.3 us (58%)
  starting transfers between devices  27.7 us (24%)
  Pallas kernels  12.4 us (11%)
  local copies, waits for them, and re-layouts  6.46 us (6%)
    all_gather x1, blocking collectives, shards(): near_queries = lax.all_gather(query_rows, 'z', axis=0)  26.2 us
    all_to_all x1, blocking collectives, shards(): lax.all_to_all(merged, ('pair', 'z'), split_axis=0, concat_axis=0, tiled=...  21.1 us
    all_gather x1, blocking collectives, shards(): near_rows = lax.all_gather(attention, 'z', axis=0)  19 us
    pallas_call x9, Pallas kernels, run(): pl.pallas_call(kernel, out_shape=out_shape, in_specs=specs(scalars, pltpu...  12.4 us
    ppermute x1, starting transfers between devices, shards(): far_rows = lax.ppermute(near_rows, 'core', swap)  10.3 us
    ppermute x1, starting transfers between devices, shards(): far_queries = lax.ppermute(near_queries, 'core', swap)  8.87 us
    unnamed x24, local copies, waits for them, and re-layouts  6.13 us
    ppermute x1, starting transfers between devices, shards(): other_parents = lax.ppermute(parents, 'pair', swap)  3.11 us
  transfers between devices with their start and end apart: 6, of which 1 were waited for; matrix products, arithmetic and copies ran while one was open for 0% of the time, Pallas kernels for 9%

profile of v2, /device:TPU:57, one launch (start us, length us, event | category | flops | bytes accessed | tf_op | source)
XLA Modules:
  0.0 114.3 jit_solution(7436027400773533625)
XLA Ops:
  0.0 3.1 %collective-permute-start.3 = (s32[32]{0:T(128)}, s32[32]{0:T(128)S(1)}, u32[]{:S(2)}, u32[]{:S(2)}) collective-permute-start(s32[32]{0:T(128)} %param.11), channel_id=1, source_target_pairs={{0,16},{16,0},{1,17},{17,1},{2,18},{18,2},{3,19},{19,3},{4,20},{20... | collective-permute-start | bytes 392 | tf_op jit(solution)/shard_map/ppermute | solution.py:255
  3.1 2.2 %collective-permute-start = (s32[2,32]{1,0:T(2,128)}, s32[2,32]{1,0:T(2,128)S(1)}, u32[]{:S(2)}, u32[]{:S(2)}) collective-permute-start(s32[2,32]{1,0:T(2,128)} %param.10), channel_id=1, source_target_pairs={{0,16},{16,0},{1,17},{17,1},{2,18},{18,2},{3,19},{19,3},{4,20},{20... | collective-permute-start | bytes 776 | tf_op jit(solution)/shard_map/ppermute | solution.py:254
  5.3 0.1 pad_add_fusion.1.meta_ref
  5.4 0.0 copy-start.3
  5.4 1.6 %copy-done.3 = bf16[1,1024,1024]{2,1,0:T(8,128)(2,1)S(1)} copy-done((bf16[1,1024,1024]{2,1,0:T(8,128)(2,1)S(1)}, bf16[1,1024,1024]{2,1,0:T(8,128)(2,1)}, u32[]{:S(2)}) %copy-start.3) | copy-done | bytes 2097176
  7.0 0.0 copy-start.4
  7.0 1.6 %copy-done.4 = bf16[1,1024,1024]{2,1,0:T(8,128)(2,1)S(1)} copy-done((bf16[1,1024,1024]{2,1,0:T(8,128)(2,1)S(1)}, bf16[1,1024,1024]{2,1,0:T(8,128)(2,1)}, u32[]{:S(2)}) %copy-start.4) | copy-done | bytes 2097176
  8.6 0.0 copy-start.11
  8.6 0.0 copy-start.10
  8.6 0.0 copy-start.5
  8.6 0.0 copy-start.6
  8.6 0.0 copy-start.7
  8.6 0.0 copy-start.8
  8.6 0.0 copy-start.9
  8.6 0.9 stage.1
  9.6 0.0 copy-start.1
  9.6 1.3 %copy-done.1 = bf16[8,1024,128]{2,1,0:T(8,128)(2,1)} copy-done((bf16[8,1024,128]{2,1,0:T(8,128)(2,1)}, bf16[8,1024,128]{2,1,0:T(8,128)(2,1)S(1)}, u32[]{:S(2)}) %copy-start.1) | copy-done | bytes 2097176
  10.9 0.0 collective-permute-done.3
  10.9 0.0 copy-done.11
  10.9 0.1 concatenate.11
  11.0 0.1 reshape.57.parent_ref
  11.1 0.0 collective-permute-done
  11.1 0.0 copy-done.10
  11.1 0.1 broadcast_add_fusion
  11.2 0.1 reshape.54
  11.3 0.1 add_bitcast_fusion.1.index_ref
  11.4 0.1 reshape.50
  11.4 0.1 add_bitcast_fusion.index_ref
  11.5 0.0 copy-done.5
  11.5 0.0 copy-done.6
  11.5 0.0 copy-done.7
  11.5 0.3 own.1
  11.8 0.3 both.1
  12.1 1.3 %collective-permute-start.2 = (bf16[128,128]{1,0:T(8,128)(2,1)S(1)}, bf16[128,128]{1,0:T(8,128)(2,1)S(1)}, u32[]{:S(2)}, u32[]{:S(2)}) collective-permute-start(bf16[128,128]{1,0:T(8,128)(2,1)S(1)} %get-tuple-element.17.gen_key_ref), channel_id=1, source_target_pairs={{8,0},{10,2},{12,4},{14,6},{9,1},{11,3},{13,5},{15,7},{24,16},{26,... | collective-permute-start | bytes 98312 | tf_op jit(solution)/shard_map/ppermute | solution.py:277
  13.4 26.2 %all-gather = bf16[1024,256]{1,0:T(8,128)(2,1)S(1)} all-gather(bf16[128,256]{1,0:T(8,128)(2,1)S(1)} %get-tuple-element.14), channel_id=2, replica_groups=mesh['grp'=16,'pair'=2,'z'=8,'core'=2] {'z'}, dimensions={0}, use_global_device_ids=true | all-gather | bytes 589824 | tf_op jit(solution)/shard_map/all_gather | solution.py:278
  39.6 8.9 %collective-permute-start.1 = (bf16[8,128,256]{2,1,0:T(8,128)(2,1)S(1)}, bf16[8,128,256]{2,1,0:T(8,128)(2,1)S(1)}, u32[]{:S(2)}, u32[]{:S(2)}) collective-permute-start(bf16[8,128,256]{2,1,0:T(8,128)(2,1)S(1)} %bitcast.27), channel_id=1, source_target_pairs={{0,1},{1,0},{2,3},{3,2},{4,5},{5,4},{6,7},{7,6},{8,9},{9,8},{10,11... | collective-permute-start | bytes 1572872 | tf_op jit(solution)/shard_map/ppermute | solution.py:279
  48.5 0.0 collective-permute-done.2.gen_value_ref
  48.5 0.0 copy-done.8
  48.5 0.0 copy-done.9
  48.6 0.0 copy-start.2
  48.6 1.6 %copy-done.2 = bf16[8,1024,128]{2,1,0:T(8,128)(2,1)S(1)} copy-done((bf16[8,1024,128]{2,1,0:T(8,128)(2,1)S(1)}, bf16[8,1024,128]{2,1,0:T(8,128)(2,1)}, u32[]{:S(2)}) %copy-start.2) | copy-done | bytes 2097176
  50.2 4.6 %attend.3 = bf16[2,8,144,128]{3,2,1,0:T(8,128)(2,1)S(1)} custom-call(s32[3]{0:T(128)S(1)} %pad_add_fusion.1.meta_ref, s32[16]{0:T(128)S(1)} %copy-done.9, s32[16,32]{1,0:T(8,128)S(1)} %copy-done.8, bf16[8,128,256]{2,1,0:T(8,128)(2,1)S(1)} %bitcast.28, bf16[8,1024,128]{2,1,0:T(8,128)(2,1)S(1)} %copy-done.2, ...), custom_call_target="tpu_custom_call" | custom-call | flops 1073741824 | bytes 4194304 | tf_op jit(solution)/shard_map/attend/pallas_call | solution.py:225
  54.7 1.9 %collective-permute-start.4 = (bf16[2,8,144,128]{3,2,1,0:T(8,128)(2,1)S(1)}, bf16[2,8,144,128]{3,2,1,0:T(8,128)(2,1)S(1)}, u32[]{:S(2)}, u32[]{:S(2)}) collective-permute-start(bf16[2,8,144,128]{3,2,1,0:T(8,128)(2,1)S(1)} %attend.3), channel_id=1, source_target_pairs={{0,1},{1,0},{2,3},{3,2},{4,5},{5,4},{6,7},{7,6},{8,9},{9,8},{10,11... | collective-permute-start | bytes 1769480 | tf_op jit(solution)/shard_map/ppermute | solution.py:304
  56.6 0.0 collective-permute-done.1.query_ref
  56.7 4.6 %attend.2 = bf16[2,8,144,128]{3,2,1,0:T(8,128)(2,1)S(1)} custom-call(s32[3]{0:T(128)S(1)} %pad_add_fusion.1.meta_ref, s32[16]{0:T(128)S(1)} %copy-done.9, s32[16,32]{1,0:T(8,128)S(1)} %copy-done.8, bf16[8,128,256]{2,1,0:T(8,128)(2,1)S(1)} %collective-permute-done.1.query_ref, bf16[8,1024,128]{2,1,0:T(8,128)(2,1)S(1)} %copy-done.2, ...), custom_call_target="tpu_custom_call" | custom-call | flops 1073741824 | bytes 4194304 | tf_op jit(solution)/shard_map/attend/pallas_call | solution.py:225
  61.2 0.0 copy-start
  61.2 0.0 collective-permute-done.4
  61.3 0.3 merge.1
  61.6 21.1 %all_to_all.5.parts_ref = bf16[16,144,128]{2,1,0:T(8,128)(2,1)S(1)} all-to-all(bf16[16,144,128]{2,1,0:T(8,128)(2,1)S(1)} %merge.1), channel_id=1, replica_groups=mesh['grp'=16,'pair'=2,'z'=8,'core'=2] {'pair','z'}, dimensions={0} | all-to-all | bytes 1179648 | tf_op jit(solution)/shard_map/all_to_all | solution.py:309
  82.7 0.2 combine.1
  82.9 19.0 %all-gather.1 = bf16[512,256]{1,0:T(8,128)(2,1)S(1)} all-gather(bf16[64,256]{1,0:T(8,128)(2,1)S(1)} %combine.1), channel_id=3, replica_groups=mesh['grp'=16,'pair'=2,'z'=8,'core'=2] {'z'}, dimensions={0}, use_global_device_ids=true | all-gather | bytes 294912 | tf_op jit(solution)/shard_map/all_gather | solution.py:311
  101.9 10.3 %collective-permute-start.5 = (bf16[8,64,256]{2,1,0:T(8,128)(2,1)S(1)}, bf16[8,64,256]{2,1,0:T(8,128)(2,1)S(1)}, u32[]{:S(2)}, u32[]{:S(2)}) collective-permute-start(bf16[8,64,256]{2,1,0:T(8,128)(2,1)S(1)} %bitcast.33), channel_id=1, source_target_pairs={{0,1},{1,0},{2,3},{3,2},{4,5},{5,4},{6,7},{7,6},{8,9},{9,8},{10,11... | collective-permute-start | bytes 786440 | tf_op jit(solution)/shard_map/ppermute | solution.py:312
  112.3 0.0 copy-done
  112.3 0.3 project_near.1.before_ref
  112.6 0.8 collective-permute-done.5.rows_ref
  113.4 0.9 project_far.1
  (4 shorter events, 0.0 us)
Async XLA Ops:
  0.0 10.9 %collective-permute-start.3 = (s32[32]{0:T(128)}, s32[32]{0:T(128)S(1)}, u32[]{:S(2)}, u32[]{:S(2)}) collective-permute-start(s32[32]{0:T(128)} %param.11), channel_id=1, source_target_pairs={{0,16},{16,0},{1,17},{17,1},{2,18},{18,2},{3,19},{19,3},{4,20},{20... | collective-permute-start | bytes 392 | tf_op jit(solution)/shard_map/ppermute | solution.py:255
  3.1 8.0 %collective-permute-start = (s32[2,32]{1,0:T(2,128)}, s32[2,32]{1,0:T(2,128)S(1)}, u32[]{:S(2)}, u32[]{:S(2)}) collective-permute-start(s32[2,32]{1,0:T(2,128)} %param.10), channel_id=1, source_target_pairs={{0,16},{16,0},{1,17},{17,1},{2,18},{18,2},{3,19},{19,3},{4,20},{20... | collective-permute-start | bytes 776 | tf_op jit(solution)/shard_map/ppermute | solution.py:254
  5.4 1.6 %copy-start.3 = (bf16[1,1024,1024]{2,1,0:T(8,128)(2,1)S(1)}, bf16[1,1024,1024]{2,1,0:T(8,128)(2,1)}, u32[]{:S(2)}) copy-start(bf16[1,1024,1024]{2,1,0:T(8,128)(2,1)} %param.14) | copy-start | bytes 6291460
  7.0 1.6 %copy-start.4 = (bf16[1,1024,1024]{2,1,0:T(8,128)(2,1)S(1)}, bf16[1,1024,1024]{2,1,0:T(8,128)(2,1)}, u32[]{:S(2)}) copy-start(bf16[1,1024,1024]{2,1,0:T(8,128)(2,1)} %param.15) | copy-start | bytes 6291460
  8.6 2.3 %copy-start.11 = (s32[32]{0:T(128)S(1)}, s32[32]{0:T(128)}, u32[]{:S(2)}) copy-start(s32[32]{0:T(128)} %param.11) | copy-start | bytes 388
  8.6 2.5 %copy-start.10 = (s32[2,32]{1,0:T(2,128)S(1)}, s32[2,32]{1,0:T(2,128)}, u32[]{:S(2)}) copy-start(s32[2,32]{1,0:T(2,128)} %param.10) | copy-start | bytes 772
  8.6 2.9 %copy-start.5 = (bf16[2,256,256]{2,1,0:T(8,128)(2,1)S(1)}, bf16[2,256,256]{2,1,0:T(8,128)(2,1)}, u32[]{:S(2)}) copy-start(bf16[2,256,256]{2,1,0:T(8,128)(2,1)} %param.16) | copy-start | bytes 786436
  8.6 2.9 %copy-start.6 = (bf16[2,256,128]{2,1,0:T(8,128)(2,1)S(1)}, bf16[2,256,128]{2,1,0:T(8,128)(2,1)}, u32[]{:S(2)}) copy-start(bf16[2,256,128]{2,1,0:T(8,128)(2,1)} %param.17) | copy-start | bytes 393220
  8.6 2.9 %copy-start.7 = (bf16[2,256,256]{2,1,0:T(8,128)(2,1)S(1)}, bf16[2,256,256]{2,1,0:T(8,128)(2,1)}, u32[]{:S(2)}) copy-start(bf16[2,256,256]{2,1,0:T(8,128)(2,1)} %param.18) | copy-start | bytes 786436
  8.6 39.9 %copy-start.8 = (s32[16,32]{1,0:T(8,128)S(1)}, s32[16,32]{1,0:T(8,128)}, u32[]{:S(2)}) copy-start(s32[16,32]{1,0:T(8,128)} %holders_ref.3) | copy-start | bytes 6148
  8.6 39.9 %copy-start.9 = (s32[16]{0:T(128)S(1)}, s32[16]{0:T(128)}, u32[]{:S(2)}) copy-start(s32[16]{0:T(128)} %lengths_ref.3) | copy-start | bytes 196
  9.6 1.3 %copy-start.1 = (bf16[8,1024,128]{2,1,0:T(8,128)(2,1)}, bf16[8,1024,128]{2,1,0:T(8,128)(2,1)S(1)}, u32[]{:S(2)}) copy-start(bf16[8,1024,128]{2,1,0:T(8,128)(2,1)S(1)} %get-tuple-element.15.key_ref) | copy-start | bytes 6291460
  12.1 36.4 %collective-permute-start.2 = (bf16[128,128]{1,0:T(8,128)(2,1)S(1)}, bf16[128,128]{1,0:T(8,128)(2,1)S(1)}, u32[]{:S(2)}, u32[]{:S(2)}) collective-permute-start(bf16[128,128]{1,0:T(8,128)(2,1)S(1)} %get-tuple-element.17.gen_key_ref), channel_id=1, source_target_pairs={{8,0},{10,2},{12,4},{14,6},{9,1},{11,3},{13,5},{15,7},{24,16},{26,... | collective-permute-start | bytes 98312 | tf_op jit(solution)/shard_map/ppermute | solution.py:277
  39.6 17.0 %collective-permute-start.1 = (bf16[8,128,256]{2,1,0:T(8,128)(2,1)S(1)}, bf16[8,128,256]{2,1,0:T(8,128)(2,1)S(1)}, u32[]{:S(2)}, u32[]{:S(2)}) collective-permute-start(bf16[8,128,256]{2,1,0:T(8,128)(2,1)S(1)} %bitcast.27), channel_id=1, source_target_pairs={{0,1},{1,0},{2,3},{3,2},{4,5},{5,4},{6,7},{7,6},{8,9},{9,8},{10,11... | collective-permute-start | bytes 1572872 | tf_op jit(solution)/shard_map/ppermute | solution.py:279
  48.6 1.6 %copy-start.2 = (bf16[8,1024,128]{2,1,0:T(8,128)(2,1)S(1)}, bf16[8,1024,128]{2,1,0:T(8,128)(2,1)}, u32[]{:S(2)}) copy-start(bf16[8,1024,128]{2,1,0:T(8,128)(2,1)} %copy-done.1) | copy-start | bytes 6291460
  54.7 6.5 %collective-permute-start.4 = (bf16[2,8,144,128]{3,2,1,0:T(8,128)(2,1)S(1)}, bf16[2,8,144,128]{3,2,1,0:T(8,128)(2,1)S(1)}, u32[]{:S(2)}, u32[]{:S(2)}) collective-permute-start(bf16[2,8,144,128]{3,2,1,0:T(8,128)(2,1)S(1)} %attend.3), channel_id=1, source_target_pairs={{0,1},{1,0},{2,3},{3,2},{4,5},{5,4},{6,7},{7,6},{8,9},{9,8},{10,11... | collective-permute-start | bytes 1769480 | tf_op jit(solution)/shard_map/ppermute | solution.py:304
  61.2 51.0 %copy-start = (bf16[4096,256]{1,0:T(8,128)(2,1)S(1)}, bf16[4096,256]{1,0:T(8,128)(2,1)}, u32[]{:S(2)}) copy-start(bf16[4096,256]{1,0:T(8,128)(2,1)} %param.19) | copy-start | bytes 6291460
  101.9 11.5 %collective-permute-start.5 = (bf16[8,64,256]{2,1,0:T(8,128)(2,1)S(1)}, bf16[8,64,256]{2,1,0:T(8,128)(2,1)S(1)}, u32[]{:S(2)}, u32[]{:S(2)}) collective-permute-start(bf16[8,64,256]{2,1,0:T(8,128)(2,1)S(1)} %bitcast.33), channel_id=1, source_target_pairs={{0,1},{1,0},{2,3},{3,2},{4,5},{5,4},{6,7},{7,6},{8,9},{9,8},{10,11... | collective-permute-start | bytes 786440 | tf_op jit(solution)/shard_map/ppermute | solution.py:312

commit v3 on v2

--- a/solution.py
+++ b/solution.py
@@ -48,19 +48,25 @@
     hot = one_hot_rows(index_ref[...], query_ref.shape[0])
     mine = pl.ds(pl.multiple_of(pair_ref[0] * rows, rows), rows)
     theirs = pl.ds(pl.multiple_of((1 - pair_ref[0]) * rows, rows), rows)
-    query_out[mine] = own_query_ref[...]
-    query_out[theirs] = look(hot, query_ref)[:rows].astype(jnp.bfloat16)
+    found = look(hot, query_ref)[:rows].astype(jnp.bfloat16)
+    for copy in range(query_out.shape[0]):
+        query_out[copy, mine] = own_query_ref[...]
+        query_out[copy, theirs] = found
     kv_out[mine] = own_kv_ref[...]
     kv_out[theirs] = look(hot, kv_ref)[:rows].astype(jnp.bfloat16)
 
 
-def stage_kernel(key_ref, value_ref, key_out, value_out):
-    slots = key_ref.shape[0]
-    for head in range(key_out.shape[0]):
-        lanes = slice(head * HEAD, (head + 1) * HEAD)
-        key_out[head] = key_ref[:, lanes]
-        value_out[head, 0:HEAD] = jnp.transpose(value_ref[:, lanes])
-        value_out[head, HEAD:CHUNK] = jnp.ones((STAT, slots), jnp.bfloat16)
+def stage_kernel(*refs):
+    *blocks, key_out, value_out = refs
+    slots = blocks[0].shape[0]
+    for block in range(len(blocks) // 2):
+        key_ref, value_ref = blocks[2 * block : 2 * block + 2]
+        span = slice(block * slots, (block + 1) * slots)
+        for head in range(key_out.shape[0]):
+            lanes = slice(head * HEAD, (head + 1) * HEAD)
+            key_out[head, span] = key_ref[:, lanes]
+            value_out[head, 0:HEAD, span] = jnp.transpose(value_ref[:, lanes])
+            value_out[head, HEAD:CHUNK, span] = jnp.ones((STAT, slots), jnp.bfloat16)
 
 
 def split3(value):
@@ -96,10 +102,16 @@
     width = 4 * half
     request, place, gen_head = meta_ref[0], meta_ref[1], meta_ref[2]
 
-    position = jnp.int32(0)
+    block_slots = slots // 2
+    near, far = jnp.int32(0), jnp.int32(0)
     for block in range(holders_ref.shape[1]):
-        position = jnp.where(holders_ref[request, block] == place, block, position)
-    live = jnp.clip(lengths_ref[request] - position * slots, 0, slots)
+        holder = holders_ref[request, block]
+        near = jnp.where(holder == place, block, near)
+        far = jnp.where(holder == jnp.bitwise_xor(place, 1), block, far)
+    near_live, far_live = (
+        jnp.clip(lengths_ref[request] - each * block_slots, 0, block_slots) for each in (near, far)
+    )
+    live = near_live + far_live
 
     def queries(head):
         pair = query_ref[head]
@@ -114,15 +126,17 @@
             out_ref[x, head, HEAD:CHUNK] = stat_rows(top[:, lanes], total[:, lanes])
 
     def attend(masked):
-        def score(head, slot):
+        def score(head, at):
             scores = scores_of(key_ref[head], queries(head))
             if masked:
-                scores = jnp.where(lax.broadcasted_iota(jnp.int32, (slots, 1), 0) < live, scores, DEAD)
-            score_ref[slot] = scores
+                slot = lax.broadcasted_iota(jnp.int32, (slots, 1), 0)
+                allowed = (slot < near_live) | ((slot >= block_slots) & (slot < block_slots + far_live))
+                scores = jnp.where(allowed, scores, DEAD)
+            score_ref[at] = scores
             return jnp.max(scores, axis=0, keepdims=True)
 
-        def finish(head, slot, top):
-            weights = jnp.exp2((score_ref[slot] - top) * EXP2_SCALE).astype(jnp.bfloat16)
+        def finish(head, at, top):
+            weights = jnp.exp2((score_ref[at] - top) * EXP2_SCALE).astype(jnp.bfloat16)
             sums = jnp.dot(value_ref[head], weights, preferred_element_type=jnp.float32)
             write(head, sums[0:HEAD], sums[HEAD : HEAD + 1], top)
 
@@ -181,20 +195,6 @@
         write(gen_head, sums, old_total * factor + added[HEAD : HEAD + 1], top)
 
 
-def merge_kernel(mine_ref, other_ref, out_ref):
-    for chunk in range(mine_ref.shape[0]):
-        tops, totals = zip(*(read_stats(ref[chunk, HEAD:CHUNK]) for ref in (mine_ref, other_ref)))
-        top = jnp.maximum(*tops)
-        factors = [jnp.exp2((each - top) * EXP2_SCALE) for each in tops]
-        total = totals[0] * factors[0] + totals[1] * factors[1]
-        sums = (
-            mine_ref[chunk, 0:HEAD].astype(jnp.float32) * factors[0]
-            + other_ref[chunk, 0:HEAD].astype(jnp.float32) * factors[1]
-        )
-        out_ref[chunk, 0:HEAD] = sums.astype(jnp.bfloat16)
-        out_ref[chunk, HEAD:CHUNK] = stat_rows(top, total)
-
-
 def combine_kernel(parts_ref, out_ref):
     count = parts_ref.shape[0]
     stats = [read_stats(parts_ref[part, HEAD:CHUNK]) for part in range(count)]
@@ -210,11 +210,10 @@
     out_ref[...] = jnp.concatenate([tall[0:rows], tall[rows : 2 * rows]], axis=1).astype(jnp.bfloat16)
 
 
-def project_kernel(parity, core_ref, rows_ref, weight_ref, before_ref, out_ref):
-    total = before_ref[...]
-    at = jnp.bitwise_xor(core_ref[0], parity)
+def project_kernel(rows_ref, weight_ref, residual_ref, out_ref):
+    total = residual_ref[...]
     for part in range(rows_ref.shape[0]):
-        total = total + jnp.dot(rows_ref[part], weight_ref[part, at], preferred_element_type=jnp.float32)
+        total = total + jnp.dot(rows_ref[part], weight_ref[part], preferred_element_type=jnp.float32)
     out_ref[...] = total.astype(out_ref.dtype)
 
 
@@ -251,8 +250,12 @@
     array = jax.ShapeDtypeStruct
     swap = [(0, 1), (1, 0)]
 
-    other_codes = lax.ppermute(codes, "pair", swap)
-    other_parents = lax.ppermute(parents, "pair", swap)
+    mine = jnp.concatenate([codes, parents[None]])
+    other = lax.ppermute(mine, "pair", swap)
+    other_codes, other_parents = other[:levels], other[levels]
+    near_keys, near_values = history_keys[0], history_values[0]
+    far_keys = lax.ppermute(near_keys, "core", swap)
+    far_values = lax.ppermute(near_values, "core", swap)
 
     def index_of(picks):
         flat = (picks + code_count * jnp.arange(levels, dtype=jnp.int32)[:, None]).reshape(half)
@@ -264,19 +267,19 @@
     own_query, own_kv, residual = call(
         own_kernel, (array((half, width), bf16), array((half, HEAD), bf16), array((half, width), f32)), 0, "own"
     )(index_of(codes), query_flat, kv_flat, embed_flat)
+    query_rows, kv_rows = call(
+        both_kernel, (array((z_count, rows, width), bf16), array((rows, HEAD), bf16)), 1, "both"
+    )(pair.reshape(1), index_of(other_codes), query_flat, kv_flat, own_query, own_kv)
+    queries = lax.all_to_all(query_rows, "z", split_axis=0, concat_axis=0, tiled=True)
+    far_kv = lax.ppermute(kv_rows, "core", swap)
+    gen_keys = jnp.where(first, kv_rows, far_kv)
+    gen_values = lax.ppermute(gen_keys, "z", [(i + z_count // 2, i) for i in range(z_count // 2)])
     staged_keys, staged_values = call(
         stage_kernel,
-        (array((KEY_HEADS, slots, HEAD), bf16), array((KEY_HEADS, CHUNK, slots), bf16)),
+        (array((KEY_HEADS, 2 * slots, HEAD), bf16), array((KEY_HEADS, CHUNK, 2 * slots), bf16)),
         0,
         "stage",
-    )(history_keys[0], history_values[0])
-
-    query_rows, kv_rows = call(both_kernel, (array((rows, width), bf16), array((rows, HEAD), bf16)), 1, "both")(
-        pair.reshape(1), index_of(other_codes), query_flat, kv_flat, own_query, own_kv
-    )
-    gen_values = lax.ppermute(kv_rows, "z", [(i + z_count // 2, i) for i in range(z_count // 2)])
-    near_queries = lax.all_gather(query_rows, "z", axis=0)
-    far_queries = lax.ppermute(near_queries, "core", swap)
+    )(near_keys, near_values, far_keys, far_values)
 
     lower = jnp.where(first, parents, other_parents)
     upper = jnp.where(first, other_parents, parents)
@@ -285,38 +288,27 @@
     parent_lanes = jnp.concatenate([jnp.full((2, beams), -1, jnp.int32), parent_rows], axis=1)
     parent_lanes = jnp.broadcast_to(parent_lanes[:, None, :], (2, 2, half)).reshape(1, 2 * rows)
 
-    gen_head = jnp.where(first & (z < z_count // 2), hist, -1)
+    gen_head = jnp.where(z < z_count // 2, 2 * z + jnp.bitwise_xor(core, pair), -1)
     meta = jnp.stack([lax.axis_index("grp"), pair * 2 * z_count + hist, gen_head]).astype(jnp.int32)
-    attend = call(
+    partials = call(
         attend_kernel,
         array((2, z_count, CHUNK, 2 * half), bf16),
         3,
         "attend",
-        scratch_shapes=[pltpu.VMEM((2, slots, 2 * rows), f32)],
+        scratch_shapes=[pltpu.VMEM((2, 2 * slots, 2 * rows), f32)],
         cost_estimate=pl.CostEstimate(
-            flops=2 * 4 * rows * KEY_HEADS * slots * HEAD,
+            flops=4 * 4 * rows * KEY_HEADS * slots * HEAD,
             bytes_accessed=4 * slots * KEY_HEADS * HEAD,
-            transcendentals=2 * rows * KEY_HEADS * slots,
+            transcendentals=4 * rows * KEY_HEADS * slots,
         ),
-    )
-    rest = (staged_keys, staged_values, kv_rows, gen_values, parent_lanes)
-    send = attend(meta, lengths, holders, near_queries, *rest)
-    arrived = lax.ppermute(send, "core", swap)
-    keep = attend(meta, lengths, holders, far_queries, *rest)
+    )(meta, lengths, holders, queries, staged_keys, staged_values, gen_keys, gen_values, parent_lanes)
 
     shape = (2 * z_count, CHUNK, 2 * half)
-    merged = call(merge_kernel, array(shape, bf16), 0, "merge")(keep.reshape(shape), arrived.reshape(shape))
-    parts = lax.all_to_all(merged, ("pair", "z"), split_axis=0, concat_axis=0, tiled=True)
+    parts = lax.all_to_all(partials.reshape(shape), ("pair", "z"), split_axis=0, concat_axis=0, tiled=True)
     attention = call(combine_kernel, array((half, width), bf16), 0, "combine")(parts)
-    near_rows = lax.all_gather(attention, "z", axis=0)
-    far_rows = lax.ppermute(near_rows, "core", swap)
-    weight = out_weight.reshape(z_count, 2, width, width)
-    place = core.reshape(1)
-    begun = call(functools.partial(project_kernel, 1), array((half, width), f32), 1, "project_near")(
-        place, near_rows, weight, residual
-    )
-    out = call(functools.partial(project_kernel, 0), array((half, width), bf16), 1, "project_far")(
-        place, far_rows, weight, begun
+    gathered = lax.all_gather(attention, ("z", "core"), axis=0)
+    out = call(project_kernel, array((half, width), bf16), 0, "project")(
+        gathered, out_weight.reshape(2 * z_count, width, width), residual
     )
     return out.reshape(levels, beams, width)
 

time: 115 us -> 101 us (0.88)
  blocking collectives: 66.3 us -> 49.6 us
  local copies, waits for them, and re-layouts: 6.46 us -> 15.2 us
  starting transfers between devices: 27.7 us -> 22.9 us
  Pallas kernels: 12.4 us -> 8.14 us
  other arithmetic: 0.33 us -> 2.38 us
    all_gather x2 -> x1, blocking collectives: 45.2 us -> 19.2 us  [shards(): gathered = lax.all_gather(attention, ('z', 'core'), axis=0)]
    ppermute x6 -> x5, starting transfers between devices: 27.7 us -> 12.8 us  [the longest x1 3.82 us: shards(): far_kv = lax.ppermute(kv_rows, 'core', swap)]
    all_to_all x0 -> x1, starting transfers between devices: none -> 10 us  [shards(): lax.all_to_all(query_rows, 'z', split_axis=0, concat_axis=0, tiled=True)]
    all_to_all x1, blocking collectives: 21.1 us -> 30.4 us  [shards(): lax.all_to_all(partials.reshape(shape), ('pair', 'z'), split_axis=0, conc...]
    unnamed x24 -> x28, local copies, waits for them, and re-layouts: 6.13 us -> 14.9 us
    pallas_call x9 -> x6, Pallas kernels: 12.4 us -> 8.14 us  [run(): pl.pallas_call(kernel, out_shape=out_shape, in_specs=specs(scalars, pltpu...]
  transfers between devices with their start and end apart: 6 -> 6, of which waited for: 1 -> 3; matrix products, arithmetic and copies ran while one was open for 0% -> 3% of each run, Pallas kernels for 9% -> 6%
where the time goes in v3:
time: 101 us; the launch traced here: 100 us
  blocking collectives  49.6 us (49%)
  starting transfers between devices  22.9 us (23%)
  local copies, waits for them, and re-layouts  15.2 us (15%)
  Pallas kernels  8.14 us (8%)
  other arithmetic  2.38 us (2%)
  waiting for transfers between devices  1.89 us (2%)
    all_to_all x1, blocking collectives, shards(): lax.all_to_all(partials.reshape(shape), ('pair', 'z'), split_axis=0, conc...  30.4 us
    all_gather x1, blocking collectives, shards(): gathered = lax.all_gather(attention, ('z', 'core'), axis=0)  19.2 us
    unnamed x28, local copies, waits for them, and re-layouts  14.9 us
    all_to_all x1, starting transfers between devices, shards(): lax.all_to_all(query_rows, 'z', split_axis=0, concat_axis=0, tiled=True)  10 us
    pallas_call x6, Pallas kernels, run(): pl.pallas_call(kernel, out_shape=out_shape, in_specs=specs(scalars, pltpu...  8.14 us
    ppermute x1, starting transfers between devices, shards(): far_kv = lax.ppermute(kv_rows, 'core', swap)  3.82 us
    ppermute x1, starting transfers between devices, shards(): other = lax.ppermute(mine, 'pair', swap)  3.11 us
    ppermute x1, starting transfers between devices, shards(): far_keys = lax.ppermute(near_keys, 'core', swap)  2.7 us
  transfers between devices with their start and end apart: 6, of which 3 were waited for; matrix products, arithmetic and copies ran while one was open for 3% of the time, Pallas kernels for 6%

profile of v3, /device:TPU:57, one launch (start us, length us, event | category | flops | bytes accessed | tf_op | source)
XLA Modules:
  0.0 100.3 jit_solution(9542398188808563144)
XLA Ops:
  0.0 0.0 copy-start.5
  0.0 2.7 %collective-permute-start.1 = (bf16[1024,1024]{1,0:T(8,128)(2,1)}, bf16[1024,1024]{1,0:T(8,128)(2,1)}, u32[]{:S(2)}, u32[]{:S(2)}) collective-permute-start(bf16[1024,1024]{1,0:T(8,128)(2,1)} %bitcast.28), channel_id=1, source_target_pairs={{0,1},{1,0},{2,3},{3,2},{4,5},{5,4},{6,7},{7,6},{8,9},{9,8},{10,11... | collective-permute-start | bytes 6291464 | tf_op jit(solution)/shard_map/ppermute | solution.py:257
  2.7 1.9 %collective-permute-start.2 = (bf16[1024,1024]{1,0:T(8,128)(2,1)}, bf16[1024,1024]{1,0:T(8,128)(2,1)}, u32[]{:S(2)}, u32[]{:S(2)}) collective-permute-start(bf16[1024,1024]{1,0:T(8,128)(2,1)} %bitcast.30), channel_id=1, source_target_pairs={{0,1},{1,0},{2,3},{3,2},{4,5},{5,4},{6,7},{7,6},{8,9},{9,8},{10,11... | collective-permute-start | bytes 6291464 | tf_op jit(solution)/shard_map/ppermute | solution.py:258
  4.6 0.7 pad_add_fusion
  5.4 3.1 %collective-permute-start = (s32[3,32]{1,0:T(4,128)S(1)}, s32[3,32]{1,0:T(4,128)S(1)}, u32[]{:S(2)}, u32[]{:S(2)}) collective-permute-start(s32[3,32]{1,0:T(4,128)S(1)} %pad_add_fusion), channel_id=1, source_target_pairs={{0,16},{16,0},{1,17},{17,1},{2,18},{18,2},{3,19},{19,3},{4,20},{20... | collective-permute-start | bytes 1160 | tf_op jit(solution)/shard_map/ppermute | solution.py:254
  8.5 1.2 %collective-permute-done = s32[3,32]{1,0:T(4,128)S(1)} collective-permute-done((s32[3,32]{1,0:T(4,128)S(1)}, s32[3,32]{1,0:T(4,128)S(1)}, u32[]{:S(2)}, u32[]{:S(2)}) %collective-permute-start) | collective-permute-done | bytes 416 | tf_op jit(solution)/shard_map/ppermute | solution.py:254
  9.7 0.7 broadcast_add_fusion
  10.4 0.1 reshape.43
  10.5 0.1 reshape.47
  10.6 0.1 add_bitcast_fusion.1.index_ref
  10.7 0.0 copy-start.7
  10.7 0.9 copy-done.7
  11.6 0.0 copy-start.9
  11.6 0.9 copy-done.9
  12.5 0.0 copy-start.11
  12.5 0.9 copy-done.11
  13.5 0.3 own.1
  13.8 0.1 add_bitcast_fusion.index_ref
  13.9 0.0 copy-start.8
  13.9 1.0 copy-done.8
  14.8 0.0 copy-start.10
  14.8 0.9 copy-done.10
  15.7 1.1 %both.1 = (bf16[8,128,256]{2,1,0:T(8,128)(2,1)}, bf16[128,128]{1,0:T(8,128)(2,1)S(1)}) custom-call(s32[1]{0:T(128)} %bitcast.3.pair_ref, s32[1,128]{1,0:T(1,128)S(1)} %add_bitcast_fusion.index_ref, bf16[512,256]{1,0:T(8,128)(2,1)S(1)} %bitcast.33, bf16[512,128]{1,0:T(8,128)(2,1)S(1)} %bitcast.35, bf16[64,256]{1,0:T(8,128)(2,1)S(1)} %get-tuple-element.12.own_query_ref, ...), custom_call_target="tpu_custom_call" | custom-call | tf_op jit(solution)/shard_map/both/pallas_call | solution.py:224
  16.8 10.0 %all-to-all-start = ((bf16[8,128,256]{2,1,0:T(8,128)(2,1)}), bf16[8,128,256]{2,1,0:T(8,128)(2,1)S(1)}, u32[]{:S(2)}, u32[]{:S(2)}) async-start(bf16[8,128,256]{2,1,0:T(8,128)(2,1)} %get-tuple-element.14), calls=%async_computation | async-start | bytes 1048576 | tf_op jit(solution)/shard_map/all_to_all | solution.py:273
  26.9 0.1 pad_add_fusion.2.meta_ref
  26.9 3.8 %collective-permute-start.3 = (bf16[128,128]{1,0:T(8,128)(2,1)S(1)}, bf16[128,128]{1,0:T(8,128)(2,1)S(1)}, u32[]{:S(2)}, u32[]{:S(2)}) collective-permute-start(bf16[128,128]{1,0:T(8,128)(2,1)S(1)} %get-tuple-element.17), channel_id=1, source_target_pairs={{0,1},{1,0},{2,3},{3,2},{4,5},{5,4},{6,7},{7,6},{8,9},{9,8},{10,11... | collective-permute-start | bytes 98312 | tf_op jit(solution)/shard_map/ppermute | solution.py:274
  30.8 0.7 fusion.1
  31.4 0.2 collective-permute-done.3
  31.6 1.3 %collective-permute-start.4 = (bf16[128,128]{1,0:T(8,128)(2,1)S(1)}, bf16[128,128]{1,0:T(8,128)(2,1)S(1)}, u32[]{:S(2)}, u32[]{:S(2)}) collective-permute-start(bf16[128,128]{1,0:T(8,128)(2,1)S(1)} %broadcast_select_fusion.gen_key_ref), channel_id=1, source_target_pairs={{8,0},{10,2},{12,4},{14,6},{9,1},{11,3},{13,5},{15,7},{24,16},{26,... | collective-permute-start | bytes 98312 | tf_op jit(solution)/shard_map/ppermute | solution.py:276
  32.9 0.1 concatenate.15
  33.0 0.0 copy-start.13
  33.0 0.1 reshape.50.parent_ref
  33.1 0.0 collective-permute-done.1.refs_2_
  33.1 0.0 collective-permute-done.2.refs_3_
  33.1 0.0 copy-done.5
  33.1 0.0 copy-start.6
  33.1 1.6 %copy-done.6 = bf16[1,1024,1024]{2,1,0:T(8,128)(2,1)S(1)} copy-done((bf16[1,1024,1024]{2,1,0:T(8,128)(2,1)S(1)}, bf16[1,1024,1024]{2,1,0:T(8,128)(2,1)}, u32[]{:S(2)}) %copy-start.6) | copy-done | bytes 2097176
  34.7 0.0 copy-start.12
  34.7 4.2 %stage.1 = (bf16[8,2048,128]{2,1,0:T(8,128)(2,1)S(1)}, bf16[8,144,2048]{2,1,0:T(8,128)(2,1)S(1)}) custom-call(bf16[1024,1024]{1,0:T(8,128)(2,1)S(1)} %bitcast.29, bf16[1024,1024]{1,0:T(8,128)(2,1)S(1)} %bitcast.31, bf16[1024,1024]{1,0:T(8,128)(2,1)} %collective-permute-done.1.refs_2_, bf16[1024,1024]{1,0:T(8,128)(2,1)} %collective-permute-done.2.refs_3_), custom_call_target="tpu_custom_call" | custom-call | tf_op jit(solution)/shard_map/stage/pallas_call | solution.py:224
  38.9 0.0 copy-start
  38.9 2.1 %copy-done = bf16[8,144,2048]{2,1,0:T(8,128)(2,1)} copy-done((bf16[8,144,2048]{2,1,0:T(8,128)(2,1)}, bf16[8,144,2048]{2,1,0:T(8,128)(2,1)S(1)}, u32[]{:S(2)}) %copy-start) | copy-done | bytes 4718616
  41.0 0.0 copy-start.2
  41.0 2.0 %copy-done.2 = bf16[8,2048,128]{2,1,0:T(8,128)(2,1)} copy-done((bf16[8,2048,128]{2,1,0:T(8,128)(2,1)}, bf16[8,2048,128]{2,1,0:T(8,128)(2,1)S(1)}, u32[]{:S(2)}) %copy-start.2) | copy-done | bytes 4194328
  43.0 0.5 collective-permute-done.4.gen_value_ref
  43.5 0.0 all-to-all-done.query_ref
  43.5 0.0 copy-done.13
  43.5 0.0 copy-done.12
  43.6 0.0 copy-start.1
  43.6 2.3 %copy-done.1 = bf16[8,144,2048]{2,1,0:T(8,128)(2,1)S(1)} copy-done((bf16[8,144,2048]{2,1,0:T(8,128)(2,1)S(1)}, bf16[8,144,2048]{2,1,0:T(8,128)(2,1)}, u32[]{:S(2)}) %copy-start.1) | copy-done | bytes 4718616
  45.9 0.0 copy-start.3
  45.9 2.2 %copy-done.3 = bf16[8,2048,128]{2,1,0:T(8,128)(2,1)S(1)} copy-done((bf16[8,2048,128]{2,1,0:T(8,128)(2,1)S(1)}, bf16[8,2048,128]{2,1,0:T(8,128)(2,1)}, u32[]{:S(2)}) %copy-start.3) | copy-done | bytes 4194328
  48.1 1.3 %attend.1 = bf16[2,8,144,128]{3,2,1,0:T(8,128)(2,1)S(1)} custom-call(s32[3]{0:T(128)S(1)} %pad_add_fusion.2.meta_ref, s32[16]{0:T(128)S(1)} %copy-done.13, s32[16,32]{1,0:T(8,128)S(1)} %copy-done.12, bf16[8,128,256]{2,1,0:T(8,128)(2,1)S(1)} %all-to-all-done.query_ref, bf16[8,2048,128]{2,1,0:T(8,128)(2,1)S(1)} %copy-done.3, ...), custom_call_target="tpu_custom_call" | custom-call | flops 2147483648 | bytes 4194304 | tf_op jit(solution)/shard_map/attend/pallas_call | solution.py:224
  49.3 0.0 copy-start.4
  49.4 30.4 %all_to_all.10.parts_ref = bf16[16,144,128]{2,1,0:T(8,128)(2,1)S(1)} all-to-all(bf16[16,144,128]{2,1,0:T(8,128)(2,1)S(1)} %bitcast.25), channel_id=1, replica_groups=mesh['grp'=16,'pair'=2,'z'=8,'core'=2] {'pair','z'}, dimensions={0} | all-to-all | bytes 1179648 | tf_op jit(solution)/shard_map/all_to_all | solution.py:307
  79.7 0.2 combine.1
  79.9 19.2 %all-gather = bf16[1024,256]{1,0:T(8,128)(2,1)S(1)} all-gather(bf16[64,256]{1,0:T(8,128)(2,1)S(1)} %combine.1), channel_id=2, replica_groups=mesh['grp'=16,'pair'=2,'z'=8,'core'=2] {'z','core'}, dimensions={0}, use_global_device_ids=true | all-gather | bytes 557056 | tf_op jit(solution)/shard_map/all_gather | solution.py:309
  99.2 0.0 copy-done.4
  99.2 1.1 %project.1 = bf16[64,256]{1,0:T(8,128)(2,1)} custom-call(bf16[16,64,256]{2,1,0:T(8,128)(2,1)S(1)} %bitcast.27, bf16[16,256,256]{2,1,0:T(8,128)(2,1)S(1)} %bitcast.26, f32[64,256]{1,0:T(8,128)S(1)} %get-tuple-element.18.residual_ref), custom_call_target="tpu_custom_call" | custom-call | tf_op jit(solution)/shard_map/project/pallas_call | solution.py:224
  (4 shorter events, 0.0 us)
Async XLA Ops:
  0.0 33.1 %copy-start.5 = (bf16[1,1024,1024]{2,1,0:T(8,128)(2,1)S(1)}, bf16[1,1024,1024]{2,1,0:T(8,128)(2,1)}, u32[]{:S(2)}) copy-start(bf16[1,1024,1024]{2,1,0:T(8,128)(2,1)} %param.14) | copy-start | bytes 6291460
  0.0 33.1 %collective-permute-start.1 = (bf16[1024,1024]{1,0:T(8,128)(2,1)}, bf16[1024,1024]{1,0:T(8,128)(2,1)}, u32[]{:S(2)}, u32[]{:S(2)}) collective-permute-start(bf16[1024,1024]{1,0:T(8,128)(2,1)} %bitcast.28), channel_id=1, source_target_pairs={{0,1},{1,0},{2,3},{3,2},{4,5},{5,4},{6,7},{7,6},{8,9},{9,8},{10,11... | collective-permute-start | bytes 6291464 | tf_op jit(solution)/shard_map/ppermute | solution.py:257
  2.7 30.4 %collective-permute-start.2 = (bf16[1024,1024]{1,0:T(8,128)(2,1)}, bf16[1024,1024]{1,0:T(8,128)(2,1)}, u32[]{:S(2)}, u32[]{:S(2)}) collective-permute-start(bf16[1024,1024]{1,0:T(8,128)(2,1)} %bitcast.30), channel_id=1, source_target_pairs={{0,1},{1,0},{2,3},{3,2},{4,5},{5,4},{6,7},{7,6},{8,9},{9,8},{10,11... | collective-permute-start | bytes 6291464 | tf_op jit(solution)/shard_map/ppermute | solution.py:258
  5.4 4.3 %collective-permute-start = (s32[3,32]{1,0:T(4,128)S(1)}, s32[3,32]{1,0:T(4,128)S(1)}, u32[]{:S(2)}, u32[]{:S(2)}) collective-permute-start(s32[3,32]{1,0:T(4,128)S(1)} %pad_add_fusion), channel_id=1, source_target_pairs={{0,16},{16,0},{1,17},{17,1},{2,18},{18,2},{3,19},{19,3},{4,20},{20... | collective-permute-start | bytes 1160 | tf_op jit(solution)/shard_map/ppermute | solution.py:254
  10.7 0.9 copy-start.7
  11.6 0.9 copy-start.9
  12.5 0.9 copy-start.11
  13.9 1.0 copy-start.8
  14.8 0.9 copy-start.10
  16.8 26.7 %all-to-all-start = ((bf16[8,128,256]{2,1,0:T(8,128)(2,1)}), bf16[8,128,256]{2,1,0:T(8,128)(2,1)S(1)}, u32[]{:S(2)}, u32[]{:S(2)}) async-start(bf16[8,128,256]{2,1,0:T(8,128)(2,1)} %get-tuple-element.14), calls=%async_computation | async-start | bytes 1048576 | tf_op jit(solution)/shard_map/all_to_all | solution.py:273
  26.9 4.7 %collective-permute-start.3 = (bf16[128,128]{1,0:T(8,128)(2,1)S(1)}, bf16[128,128]{1,0:T(8,128)(2,1)S(1)}, u32[]{:S(2)}, u32[]{:S(2)}) collective-permute-start(bf16[128,128]{1,0:T(8,128)(2,1)S(1)} %get-tuple-element.17), channel_id=1, source_target_pairs={{0,1},{1,0},{2,3},{3,2},{4,5},{5,4},{6,7},{7,6},{8,9},{9,8},{10,11... | collective-permute-start | bytes 98312 | tf_op jit(solution)/shard_map/ppermute | solution.py:274
  31.6 11.9 %collective-permute-start.4 = (bf16[128,128]{1,0:T(8,128)(2,1)S(1)}, bf16[128,128]{1,0:T(8,128)(2,1)S(1)}, u32[]{:S(2)}, u32[]{:S(2)}) collective-permute-start(bf16[128,128]{1,0:T(8,128)(2,1)S(1)} %broadcast_select_fusion.gen_key_ref), channel_id=1, source_target_pairs={{8,0},{10,2},{12,4},{14,6},{9,1},{11,3},{13,5},{15,7},{24,16},{26,... | collective-permute-start | bytes 98312 | tf_op jit(solution)/shard_map/ppermute | solution.py:276
  33.0 10.6 %copy-start.13 = (s32[16]{0:T(128)S(1)}, s32[16]{0:T(128)}, u32[]{:S(2)}) copy-start(s32[16]{0:T(128)} %lengths_ref.1) | copy-start | bytes 196
  33.1 1.6 %copy-start.6 = (bf16[1,1024,1024]{2,1,0:T(8,128)(2,1)S(1)}, bf16[1,1024,1024]{2,1,0:T(8,128)(2,1)}, u32[]{:S(2)}) copy-start(bf16[1,1024,1024]{2,1,0:T(8,128)(2,1)} %param.15) | copy-start | bytes 6291460
  34.7 8.9 %copy-start.12 = (s32[16,32]{1,0:T(8,128)S(1)}, s32[16,32]{1,0:T(8,128)}, u32[]{:S(2)}) copy-start(s32[16,32]{1,0:T(8,128)} %holders_ref.1) | copy-start | bytes 6148
  38.9 2.1 %copy-start = (bf16[8,144,2048]{2,1,0:T(8,128)(2,1)}, bf16[8,144,2048]{2,1,0:T(8,128)(2,1)S(1)}, u32[]{:S(2)}) copy-start(bf16[8,144,2048]{2,1,0:T(8,128)(2,1)S(1)} %get-tuple-element.16.value_ref) | copy-start | bytes 14155780
  41.0 2.0 %copy-start.2 = (bf16[8,2048,128]{2,1,0:T(8,128)(2,1)}, bf16[8,2048,128]{2,1,0:T(8,128)(2,1)S(1)}, u32[]{:S(2)}) copy-start(bf16[8,2048,128]{2,1,0:T(8,128)(2,1)S(1)} %get-tuple-element.15.key_ref) | copy-start | bytes 12582916
  43.6 2.3 %copy-start.1 = (bf16[8,144,2048]{2,1,0:T(8,128)(2,1)S(1)}, bf16[8,144,2048]{2,1,0:T(8,128)(2,1)}, u32[]{:S(2)}) copy-start(bf16[8,144,2048]{2,1,0:T(8,128)(2,1)} %copy-done) | copy-start | bytes 14155780
  45.9 2.2 %copy-start.3 = (bf16[8,2048,128]{2,1,0:T(8,128)(2,1)S(1)}, bf16[8,2048,128]{2,1,0:T(8,128)(2,1)}, u32[]{:S(2)}) copy-start(bf16[8,2048,128]{2,1,0:T(8,128)(2,1)} %copy-done.2) | copy-start | bytes 12582916
  49.3 49.8 %copy-start.4 = (bf16[4096,256]{1,0:T(8,128)(2,1)S(1)}, bf16[4096,256]{1,0:T(8,128)(2,1)}, u32[]{:S(2)}) copy-start(bf16[4096,256]{1,0:T(8,128)(2,1)} %param.19) | copy-start | bytes 6291460

commit v4 on v3

--- a/solution.py
+++ b/solution.py
@@ -14,11 +14,7 @@
 CHUNK = HEAD + STAT
 DEAD = -1e30
 EXP2_SCALE = HEAD ** (-0.5) * math.log2(math.e)
-VMEM_LIMIT = 32 * 1024 * 1024
-
-
-def params():
-    return pltpu.CompilerParams(vmem_limit_bytes=VMEM_LIMIT)
+MIB = 1024 * 1024
 
 
 def one_hot_rows(index_row, count):
@@ -31,42 +27,72 @@
     return jnp.concatenate(parts, axis=1)
 
 
-def look(hot, table_ref):
-    return jnp.dot(hot, table_ref[...], preferred_element_type=jnp.float32)
-
-
-def own_kernel(index_ref, query_ref, kv_ref, embed_ref, query_out, kv_out, residual_out):
-    rows = query_out.shape[0]
-    hot = one_hot_rows(index_ref[...], query_ref.shape[0])
-    query_out[...] = look(hot, query_ref)[:rows].astype(jnp.bfloat16)
-    kv_out[...] = look(hot, kv_ref)[:rows].astype(jnp.bfloat16)
-    residual_out[...] = look(hot, embed_ref)[:rows]
-
-
-def both_kernel(pair_ref, index_ref, query_ref, kv_ref, own_query_ref, own_kv_ref, query_out, kv_out):
-    rows = own_query_ref.shape[0]
-    hot = one_hot_rows(index_ref[...], query_ref.shape[0])
-    mine = pl.ds(pl.multiple_of(pair_ref[0] * rows, rows), rows)
-    theirs = pl.ds(pl.multiple_of((1 - pair_ref[0]) * rows, rows), rows)
-    found = look(hot, query_ref)[:rows].astype(jnp.bfloat16)
-    for copy in range(query_out.shape[0]):
-        query_out[copy, mine] = own_query_ref[...]
-        query_out[copy, theirs] = found
-    kv_out[mine] = own_kv_ref[...]
-    kv_out[theirs] = look(hot, kv_ref)[:rows].astype(jnp.bfloat16)
+def residual_kernel(codes_ref, embed_hbm, out_ref, embed_ref, sem):
+    copy = pltpu.make_async_copy(embed_hbm, embed_ref, sem.at[0])
+    copy.start()
+    beams = codes_ref.shape[1]
+    hots = [one_hot_rows(codes_ref[level : level + 1], embed_ref.shape[1]) for level in range(codes_ref.shape[0])]
+    copy.wait()
+    for level, hot in enumerate(hots):
+        out_ref[level * beams : (level + 1) * beams] = jnp.dot(
+            hot, embed_ref[level], preferred_element_type=jnp.float32
+        )
+
+
+def look_kernel(pair_ref, mine_ref, other_ref, query_hbm, kv_hbm, query_out, kv_out, query_ref, kv_ref, sem):
+    copies = [
+        pltpu.make_async_copy(query_hbm, query_ref, sem.at[0]),
+        pltpu.make_async_copy(kv_hbm, kv_ref, sem.at[1]),
+    ]
+    for copy in copies:
+        copy.start()
+    levels, beams = mine_ref.shape
+    hots = [
+        jnp.concatenate([one_hot_rows(ref[level : level + 1], query_ref.shape[1]) for ref in (mine_ref, other_ref)])
+        for level in range(levels)
+    ]
+    for copy in copies:
+        copy.wait()
+    half = levels * beams
+    for level, hot in enumerate(hots):
+        queries = jnp.dot(hot, query_ref[level], preferred_element_type=jnp.float32).astype(jnp.bfloat16)
+        kvs = jnp.dot(hot, kv_ref[level], preferred_element_type=jnp.float32).astype(jnp.bfloat16)
+        for part, x in enumerate((pair_ref[0], 1 - pair_ref[0])):
+            rows = slice(part * beams, (part + 1) * beams)
+            place = pl.ds(pl.multiple_of(x * half + level * beams, beams), beams)
+            for copy in range(query_out.shape[0]):
+                query_out[copy, place] = queries[rows]
+            kv_out[place] = kvs[rows]
 
 
 def stage_kernel(*refs):
-    *blocks, key_out, value_out = refs
-    slots = blocks[0].shape[0]
-    for block in range(len(blocks) // 2):
-        key_ref, value_ref = blocks[2 * block : 2 * block + 2]
-        span = slice(block * slots, (block + 1) * slots)
-        for head in range(key_out.shape[0]):
+    *blocks, key_out, value_out, value_ref, key_sem, value_sem = refs
+    heads = key_out.shape[0]
+    count = len(blocks) // 2
+    slots = value_ref.shape[1]
+    key_copies, value_copies = [], []
+    for block in range(count):
+        span = pl.ds(block * slots, slots)
+        value_copies.append(
+            pltpu.make_async_copy(blocks[2 * block + 1], value_ref.at[block], value_sem.at[block])
+        )
+        for head in range(heads):
+            lanes = pl.ds(head * HEAD, HEAD)
+            key_copies.append(
+                pltpu.make_async_copy(
+                    blocks[2 * block].at[:, lanes], key_out.at[head, span], key_sem.at[block * heads + head]
+                )
+            )
+    for copy in value_copies + key_copies:
+        copy.start()
+    value_out[:, HEAD:CHUNK] = jnp.ones((heads, STAT, count * slots), jnp.bfloat16)
+    for block in range(count):
+        value_copies[block].wait()
+        for head in range(heads):
             lanes = slice(head * HEAD, (head + 1) * HEAD)
-            key_out[head, span] = key_ref[:, lanes]
-            value_out[head, 0:HEAD, span] = jnp.transpose(value_ref[:, lanes])
-            value_out[head, HEAD:CHUNK, span] = jnp.ones((STAT, slots), jnp.bfloat16)
+            value_out[head, 0:HEAD, block * slots : (block + 1) * slots] = jnp.transpose(value_ref[block, :, lanes])
+    for copy in key_copies:
+        copy.wait()
 
 
 def split3(value):
@@ -217,21 +243,17 @@
     out_ref[...] = total.astype(out_ref.dtype)
 
 
-def call(kernel, out_shape, scalars, name, **rest):
-    specs = lambda count, space: [pl.BlockSpec(memory_space=space)] * count
-
-    def run(*args):
-        return pl.pallas_call(
-            kernel,
-            out_shape=out_shape,
-            in_specs=specs(scalars, pltpu.SMEM) + specs(len(args) - scalars, pltpu.VMEM),
-            out_specs=jax.tree.map(lambda _: pl.BlockSpec(memory_space=pltpu.VMEM), out_shape),
-            compiler_params=params(),
-            name=name,
-            **rest,
-        )(*args)
-
-    return run
+def call(kernel, out_shape, name, spaces, vmem, **rest):
+    kinds = {"s": pltpu.SMEM, "v": pltpu.VMEM, "h": pltpu.HBM, "a": pl.ANY}
+    return pl.pallas_call(
+        kernel,
+        out_shape=out_shape,
+        in_specs=[pl.BlockSpec(memory_space=kinds[space]) for space in spaces],
+        out_specs=jax.tree.map(lambda _: pl.BlockSpec(memory_space=pltpu.VMEM), out_shape),
+        compiler_params=pltpu.CompilerParams(vmem_limit_bytes=vmem * MIB),
+        name=name,
+        **rest,
+    )
 
 
 def shards(
@@ -248,37 +270,46 @@
     first = pair == 0
     bf16, f32 = jnp.bfloat16, jnp.float32
     array = jax.ShapeDtypeStruct
+    dma = pltpu.SemaphoreType.DMA
     swap = [(0, 1), (1, 0)]
 
-    mine = jnp.concatenate([codes, parents[None]])
-    other = lax.ppermute(mine, "pair", swap)
-    other_codes, other_parents = other[:levels], other[levels]
-    near_keys, near_values = history_keys[0], history_values[0]
+    other_codes = lax.ppermute(codes, "pair", swap)
+    residual = call(
+        residual_kernel,
+        array((half, width), f32),
+        "residual",
+        "vh",
+        4,
+        scratch_shapes=[pltpu.VMEM(embed_table.shape, bf16), dma((1,))],
+    )(codes, embed_table)
+
+    query_rows, kv_rows = call(
+        look_kernel,
+        (array((z_count, rows, width), bf16), array((rows, HEAD), bf16)),
+        "look",
+        "svvhh",
+        4,
+        scratch_shapes=[pltpu.VMEM(query_table.shape, bf16), pltpu.VMEM(kv_table.shape, bf16), dma((2,))],
+    )(pair.reshape(1), codes, other_codes, query_table, kv_table)
+    queries = lax.all_to_all(query_rows, "z", split_axis=0, concat_axis=0, tiled=True)
+
+    kv_rows, near_keys, near_values, parents = lax.optimization_barrier(
+        (kv_rows, history_keys[0], history_values[0], parents)
+    )
     far_keys = lax.ppermute(near_keys, "core", swap)
     far_values = lax.ppermute(near_values, "core", swap)
-
-    def index_of(picks):
-        flat = (picks + code_count * jnp.arange(levels, dtype=jnp.int32)[:, None]).reshape(half)
-        return jnp.concatenate([flat, flat]).reshape(1, rows)
-
-    query_flat = query_table.reshape(levels * code_count, width)
-    kv_flat = kv_table.reshape(levels * code_count, HEAD)
-    embed_flat = embed_table.reshape(levels * code_count, width)
-    own_query, own_kv, residual = call(
-        own_kernel, (array((half, width), bf16), array((half, HEAD), bf16), array((half, width), f32)), 0, "own"
-    )(index_of(codes), query_flat, kv_flat, embed_flat)
-    query_rows, kv_rows = call(
-        both_kernel, (array((z_count, rows, width), bf16), array((rows, HEAD), bf16)), 1, "both"
-    )(pair.reshape(1), index_of(other_codes), query_flat, kv_flat, own_query, own_kv)
-    queries = lax.all_to_all(query_rows, "z", split_axis=0, concat_axis=0, tiled=True)
     far_kv = lax.ppermute(kv_rows, "core", swap)
+    other_parents = lax.ppermute(parents, "pair", swap)
     gen_keys = jnp.where(first, kv_rows, far_kv)
     gen_values = lax.ppermute(gen_keys, "z", [(i + z_count // 2, i) for i in range(z_count // 2)])
     staged_keys, staged_values = call(
         stage_kernel,
         (array((KEY_HEADS, 2 * slots, HEAD), bf16), array((KEY_HEADS, CHUNK, 2 * slots), bf16)),
-        0,
         "stage",
+        "hhaa",
+        8,
+        scratch_shapes=[pltpu.VMEM((2, slots, KEY_HEADS * HEAD), bf16), dma((2 * KEY_HEADS,)), dma((2,))],
+        cost_estimate=pl.CostEstimate(flops=0, bytes_accessed=16 * MIB, transcendentals=0),
     )(near_keys, near_values, far_keys, far_values)
 
     lower = jnp.where(first, parents, other_parents)
@@ -293,8 +324,9 @@
     partials = call(
         attend_kernel,
         array((2, z_count, CHUNK, 2 * half), bf16),
-        3,
         "attend",
+        "sssvvvvvv",
+        16,
         scratch_shapes=[pltpu.VMEM((2, 2 * slots, 2 * rows), f32)],
         cost_estimate=pl.CostEstimate(
             flops=4 * 4 * rows * KEY_HEADS * slots * HEAD,
@@ -305,9 +337,9 @@
 
     shape = (2 * z_count, CHUNK, 2 * half)
     parts = lax.all_to_all(partials.reshape(shape), ("pair", "z"), split_axis=0, concat_axis=0, tiled=True)
-    attention = call(combine_kernel, array((half, width), bf16), 0, "combine")(parts)
+    attention = call(combine_kernel, array((half, width), bf16), "combine", "v", 4)(parts)
     gathered = lax.all_gather(attention, ("z", "core"), axis=0)
-    out = call(project_kernel, array((half, width), bf16), 0, "project")(
+    out = call(project_kernel, array((half, width), bf16), "project", "vvv", 4)(
         gathered, out_weight.reshape(2 * z_count, width, width), residual
     )
     return out.reshape(levels, beams, width)

time: 101 us -> 101 us (level)
  blocking collectives: 49.6 us -> 21 us
  starting transfers between devices: 22.9 us -> 39 us
  waiting for transfers between devices: 1.89 us -> 16.3 us
  other arithmetic: 2.38 us -> 0.76 us
    all_to_all x1 -> x0, blocking collectives: 30.4 us -> none  [shards(): lax.all_to_all(partials.reshape(shape), ('pair', 'z'), split_axis=0, conc...]
    all_to_all x0 -> x1, waiting for transfers between devices: none -> 14.5 us  [shards(): lax.all_to_all(partials.reshape(shape), ('pair', 'z'), split_axis=0, conc...]
    all_to_all x0 -> x1, starting transfers between devices: none -> 12.8 us  [shards(): lax.all_to_all(partials.reshape(shape), ('pair', 'z'), split_axis=0, conc...]
    ppermute x1 -> x2, starting transfers between devices: 3.11 us -> 6.22 us  [the longest x1 3.11 us: shards(): other_parents = lax.ppermute(parents, 'pair', swap)]
    all_gather x1, blocking collectives: 19.2 us -> 21 us  [shards(): gathered = lax.all_gather(attention, ('z', 'core'), axis=0)]
    ppermute x1, starting transfers between devices: 2.7 us -> 3.73 us  [shards(): far_keys = lax.ppermute(near_keys, 'core', swap)]
  transfers between devices with their start and end apart: 6 -> 8, of which waited for: 3 -> 4; matrix products, arithmetic and copies ran while one was open for 3% -> 1% of each run, Pallas kernels for 6% -> 3%
where the time goes in v4:
time: 101 us; the launch traced here: 99.4 us
  starting transfers between devices  39 us (39%)
  blocking collectives  21 us (21%)
  waiting for transfers between devices  16.3 us (16%)
  local copies, waits for them, and re-layouts  14.5 us (14%)
  Pallas kernels  7.62 us (8%)
    all_gather x1, blocking collectives, shards(): gathered = lax.all_gather(attention, ('z', 'core'), axis=0)  21 us
    all_to_all x1, waiting for transfers between devices, shards(): lax.all_to_all(partials.reshape(shape), ('pair', 'z'), split_axis=0, conc...  14.5 us
    unnamed x28, local copies, waits for them, and re-layouts  14.4 us
    all_to_all x1, starting transfers between devices, shards(): lax.all_to_all(partials.reshape(shape), ('pair', 'z'), split_axis=0, conc...  12.8 us
    all_to_all x1, starting transfers between devices, shards(): lax.all_to_all(query_rows, 'z', split_axis=0, concat_axis=0, tiled=True)  10 us
    ppermute x1, starting transfers between devices, shards(): far_keys = lax.ppermute(near_keys, 'core', swap)  3.73 us
    ppermute x1, starting transfers between devices, shards(): other_parents = lax.ppermute(parents, 'pair', swap)  3.11 us
    ppermute x1, starting transfers between devices, shards(): other_codes = lax.ppermute(codes, 'pair', swap)  3.11 us
  transfers between devices with their start and end apart: 8, of which 4 were waited for; matrix products, arithmetic and copies ran while one was open for 1% of the time, Pallas kernels for 3%

profile of v4, /device:TPU:57, one launch (start us, length us, event | category | flops | bytes accessed | tf_op | source)
XLA Modules:
  0.0 99.4 jit_solution(11163983843411533372)
XLA Ops:
  0.0 3.1 %collective-permute-start = (s32[2,32]{1,0:T(2,128)}, s32[2,32]{1,0:T(2,128)S(1)}, u32[]{:S(2)}, u32[]{:S(2)}) collective-permute-start(s32[2,32]{1,0:T(2,128)} %codes_ref.1), channel_id=1, source_target_pairs={{0,16},{16,0},{1,17},{17,1},{2,18},{18,2},{3,19},{19,3},{4,20},{20... | collective-permute-start | bytes 776 | tf_op jit(solution)/shard_map/ppermute | solution.py:276
  3.1 1.4 %collective-permute-done.other_ref = s32[2,32]{1,0:T(2,128)S(1)} collective-permute-done((s32[2,32]{1,0:T(2,128)}, s32[2,32]{1,0:T(2,128)S(1)}, u32[]{:S(2)}, u32[]{:S(2)}) %collective-permute-start) | collective-permute-done | bytes 288 | tf_op jit(solution)/shard_map/ppermute | solution.py:276
  4.5 0.0 copy-start.8
  4.5 0.9 copy-done.8
  5.5 0.0 copy-start.9
  5.5 0.9 copy-done.9
  6.4 0.0 copy-start.11
  6.4 0.7 copy-done.11
  7.0 1.3 %look.1 = (bf16[8,128,256]{2,1,0:T(8,128)(2,1)}, bf16[128,128]{1,0:T(8,128)(2,1)S(1)}) custom-call(s32[1]{0:T(128)} %bitcast.3.pair_ref, s32[2,32]{1,0:T(2,128)S(1)} %copy-done.11, s32[2,32]{1,0:T(2,128)S(1)} %collective-permute-done.other_ref, bf16[2,256,256]{2,1,0:T(8,128)(2,1)S(1)} %copy-done.8, bf16[2,256,128]{2,1,0:T(8,128)(2,1)S(1)} %copy-done.9), custom_call_target="tpu_custom_call" | custom-call | tf_op jit(solution)/shard_map/look/pallas_call | solution.py:286
  8.4 3.7 %collective-permute-start.1 = (bf16[1024,1024]{1,0:T(8,128)(2,1)}, bf16[1024,1024]{1,0:T(8,128)(2,1)S(1)}, u32[]{:S(2)}, u32[]{:S(2)}) collective-permute-start(bf16[1024,1024]{1,0:T(8,128)(2,1)} %bitcast.16), channel_id=1, source_target_pairs={{0,1},{1,0},{2,3},{3,2},{4,5},{5,4},{6,7},{7,6},{8,9},{9,8},{10,11... | collective-permute-start | bytes 6291464 | tf_op jit(solution)/shard_map/ppermute | solution.py:299
  12.1 1.9 %collective-permute-start.2 = (bf16[1024,1024]{1,0:T(8,128)(2,1)}, bf16[1024,1024]{1,0:T(8,128)(2,1)}, u32[]{:S(2)}, u32[]{:S(2)}) collective-permute-start(bf16[1024,1024]{1,0:T(8,128)(2,1)} %bitcast.18), channel_id=1, source_target_pairs={{0,1},{1,0},{2,3},{3,2},{4,5},{5,4},{6,7},{7,6},{8,9},{9,8},{10,11... | collective-permute-start | bytes 6291464 | tf_op jit(solution)/shard_map/ppermute | solution.py:300
  14.0 10.0 %all-to-all-start = ((bf16[8,128,256]{2,1,0:T(8,128)(2,1)}), bf16[8,128,256]{2,1,0:T(8,128)(2,1)S(1)}, u32[]{:S(2)}, u32[]{:S(2)}) async-start(bf16[8,128,256]{2,1,0:T(8,128)(2,1)} %get-tuple-element.13), calls=%async_computation | async-start | bytes 1048576 | tf_op jit(solution)/shard_map/all_to_all | solution.py:294
  24.1 0.1 pad_add_fusion.1.meta_ref
  24.2 3.1 %collective-permute-start.5 = (s32[32]{0:T(128)}, s32[32]{0:T(128)S(1)}, u32[]{:S(2)}, u32[]{:S(2)}) collective-permute-start(s32[32]{0:T(128)} %param.11), channel_id=1, source_target_pairs={{0,16},{16,0},{1,17},{17,1},{2,18},{18,2},{3,19},{19,3},{4,20},{20... | collective-permute-start | bytes 392 | tf_op jit(solution)/shard_map/ppermute | solution.py:302
  27.3 3.0 %collective-permute-start.3 = (bf16[128,128]{1,0:T(8,128)(2,1)S(1)}, bf16[128,128]{1,0:T(8,128)(2,1)S(1)}, u32[]{:S(2)}, u32[]{:S(2)}) collective-permute-start(bf16[128,128]{1,0:T(8,128)(2,1)S(1)} %get-tuple-element.19), channel_id=1, source_target_pairs={{0,1},{1,0},{2,3},{3,2},{4,5},{5,4},{6,7},{7,6},{8,9},{9,8},{10,11... | collective-permute-start | bytes 98312 | tf_op jit(solution)/shard_map/ppermute | solution.py:301
  30.2 0.0 collective-permute-done.5
  30.3 0.7 fusion.1
  30.9 0.2 collective-permute-done.3
  31.1 1.3 %collective-permute-start.4 = (bf16[128,128]{1,0:T(8,128)(2,1)S(1)}, bf16[128,128]{1,0:T(8,128)(2,1)S(1)}, u32[]{:S(2)}, u32[]{:S(2)}) collective-permute-start(bf16[128,128]{1,0:T(8,128)(2,1)S(1)} %broadcast_select_fusion.gen_key_ref), channel_id=1, source_target_pairs={{8,0},{10,2},{12,4},{14,6},{9,1},{11,3},{13,5},{15,7},{24,16},{26,... | collective-permute-start | bytes 98312 | tf_op jit(solution)/shard_map/ppermute | solution.py:304
  32.4 0.1 concatenate.3
  32.5 0.0 copy-start.13
  32.5 0.1 reshape.17.parent_ref
  32.6 0.0 collective-permute-done.1.refs_2_
  32.6 0.0 collective-permute-done.2.refs_3_
  32.6 0.0 copy-start.5
  32.6 1.6 %copy-done.5 = bf16[1,1024,1024]{2,1,0:T(8,128)(2,1)S(1)} copy-done((bf16[1,1024,1024]{2,1,0:T(8,128)(2,1)S(1)}, bf16[1,1024,1024]{2,1,0:T(8,128)(2,1)}, u32[]{:S(2)}) %copy-start.5) | copy-done | bytes 2097176
  34.2 0.0 copy-start.6
  34.2 1.6 %copy-done.6 = bf16[1,1024,1024]{2,1,0:T(8,128)(2,1)S(1)} copy-done((bf16[1,1024,1024]{2,1,0:T(8,128)(2,1)S(1)}, bf16[1,1024,1024]{2,1,0:T(8,128)(2,1)}, u32[]{:S(2)}) %copy-start.6) | copy-done | bytes 2097176
  35.8 0.0 copy-start.10
  35.8 2.6 %stage.1 = (bf16[8,2048,128]{2,1,0:T(8,128)(2,1)S(1)}, bf16[8,144,2048]{2,1,0:T(8,128)(2,1)S(1)}) custom-call(bf16[1024,1024]{1,0:T(8,128)(2,1)S(1)} %bitcast.17, bf16[1024,1024]{1,0:T(8,128)(2,1)S(1)} %bitcast.19, bf16[1024,1024]{1,0:T(8,128)(2,1)S(1)} %collective-permute-done.1.refs_2_, bf16[1024,1024]{1,0:T(8,128)(2,1)} %collective-permute-done.2.refs_3_), custom_call_target="tpu_custom_call" | custom-call | bytes 16777216 | tf_op jit(solution)/shard_map/stage/pallas_call | solution.py:305
  38.4 0.0 copy-start
  38.4 2.1 %copy-done = bf16[8,144,2048]{2,1,0:T(8,128)(2,1)} copy-done((bf16[8,144,2048]{2,1,0:T(8,128)(2,1)}, bf16[8,144,2048]{2,1,0:T(8,128)(2,1)S(1)}, u32[]{:S(2)}) %copy-start) | copy-done | bytes 4718616
  40.6 0.0 copy-start.2
  40.6 2.0 %copy-done.2 = bf16[8,2048,128]{2,1,0:T(8,128)(2,1)} copy-done((bf16[8,2048,128]{2,1,0:T(8,128)(2,1)}, bf16[8,2048,128]{2,1,0:T(8,128)(2,1)S(1)}, u32[]{:S(2)}) %copy-start.2) | copy-done | bytes 4194328
  42.5 0.2 collective-permute-done.4.gen_value_ref
  42.7 0.0 all-to-all-done.query_ref
  42.7 0.0 copy-done.13
  42.7 0.0 copy-done.10
  42.7 0.0 copy-start.1
  42.8 2.3 %copy-done.1 = bf16[8,144,2048]{2,1,0:T(8,128)(2,1)S(1)} copy-done((bf16[8,144,2048]{2,1,0:T(8,128)(2,1)S(1)}, bf16[8,144,2048]{2,1,0:T(8,128)(2,1)}, u32[]{:S(2)}) %copy-start.1) | copy-done | bytes 4718616
  45.1 0.0 copy-start.3
  45.1 2.2 %copy-done.3 = bf16[8,2048,128]{2,1,0:T(8,128)(2,1)S(1)} copy-done((bf16[8,2048,128]{2,1,0:T(8,128)(2,1)S(1)}, bf16[8,2048,128]{2,1,0:T(8,128)(2,1)}, u32[]{:S(2)}) %copy-start.3) | copy-done | bytes 4194328
  47.3 0.0 copy-start.7
  47.3 0.0 copy-start.12
  47.3 2.1 %attend.1 = bf16[2,8,144,128]{3,2,1,0:T(8,128)(2,1)} custom-call(s32[3]{0:T(128)S(1)} %pad_add_fusion.1.meta_ref, s32[16]{0:T(128)S(1)} %copy-done.13, s32[16,32]{1,0:T(8,128)S(1)} %copy-done.10, bf16[8,128,256]{2,1,0:T(8,128)(2,1)S(1)} %all-to-all-done.query_ref, bf16[8,2048,128]{2,1,0:T(8,128)(2,1)S(1)} %copy-done.3, bf16[8,144,2048]{2,1,0:T(8,128)(2,1)S(1)} %copy-done.1, ...), custom_call_target="tpu_custom_call" | custom-call | flops 2147483648 | bytes 4194304 | tf_op jit(solution)/shard_map/attend/pallas_call | solution.py:324
  49.4 0.0 copy-start.4
  49.4 12.8 %all-to-all-start.1 = ((bf16[16,144,128]{2,1,0:T(8,128)(2,1)}), bf16[16,144,128]{2,1,0:T(8,128)(2,1)S(1)}, u32[]{:S(2)}, u32[]{:S(2)}) async-start(bf16[16,144,128]{2,1,0:T(8,128)(2,1)} %bitcast.8), calls=%async_computation.1 | async-start | bytes 1179648 | tf_op jit(solution)/shard_map/all_to_all | solution.py:339
  62.2 0.0 copy-done.7
  62.2 0.0 copy-done.12
  62.2 0.3 residual.1.residual_ref
  62.5 14.5 %all-to-all-done.1.parts_ref = bf16[16,144,128]{2,1,0:T(8,128)(2,1)S(1)} async-done(((bf16[16,144,128]{2,1,0:T(8,128)(2,1)}), bf16[16,144,128]{2,1,0:T(8,128)(2,1)S(1)}, u32[]{:S(2)}, u32[]{:S(2)}) %all-to-all-start.1) | async-done | bytes 589856 | tf_op jit(solution)/shard_map/all_to_all | solution.py:339
  77.0 0.2 combine.1
  77.3 21.0 %all-gather = bf16[1024,256]{1,0:T(8,128)(2,1)S(1)} all-gather(bf16[64,256]{1,0:T(8,128)(2,1)S(1)} %combine.1), channel_id=2, replica_groups=mesh['grp'=16,'pair'=2,'z'=8,'core'=2] {'z','core'}, dimensions={0}, use_global_device_ids=true | all-gather | bytes 557056 | tf_op jit(solution)/shard_map/all_gather | solution.py:341
  98.3 0.0 copy-done.4
  98.3 1.1 %project.1 = bf16[64,256]{1,0:T(8,128)(2,1)} custom-call(bf16[16,64,256]{2,1,0:T(8,128)(2,1)S(1)} %bitcast.15, bf16[16,256,256]{2,1,0:T(8,128)(2,1)S(1)} %bitcast.14, f32[64,256]{1,0:T(8,128)S(1)} %residual.1.residual_ref), custom_call_target="tpu_custom_call" | custom-call | tf_op jit(solution)/shard_map/project/pallas_call | solution.py:342
  (3 shorter events, 0.0 us)
Async XLA Ops:
  0.0 4.5 %collective-permute-start = (s32[2,32]{1,0:T(2,128)}, s32[2,32]{1,0:T(2,128)S(1)}, u32[]{:S(2)}, u32[]{:S(2)}) collective-permute-start(s32[2,32]{1,0:T(2,128)} %codes_ref.1), channel_id=1, source_target_pairs={{0,16},{16,0},{1,17},{17,1},{2,18},{18,2},{3,19},{19,3},{4,20},{20... | collective-permute-start | bytes 776 | tf_op jit(solution)/shard_map/ppermute | solution.py:276
  4.5 1.0 copy-start.8
  5.5 0.9 copy-start.9
  6.4 0.7 copy-start.11
  8.4 24.2 %collective-permute-start.1 = (bf16[1024,1024]{1,0:T(8,128)(2,1)}, bf16[1024,1024]{1,0:T(8,128)(2,1)S(1)}, u32[]{:S(2)}, u32[]{:S(2)}) collective-permute-start(bf16[1024,1024]{1,0:T(8,128)(2,1)} %bitcast.16), channel_id=1, source_target_pairs={{0,1},{1,0},{2,3},{3,2},{4,5},{5,4},{6,7},{7,6},{8,9},{9,8},{10,11... | collective-permute-start | bytes 6291464 | tf_op jit(solution)/shard_map/ppermute | solution.py:299
  12.1 20.5 %collective-permute-start.2 = (bf16[1024,1024]{1,0:T(8,128)(2,1)}, bf16[1024,1024]{1,0:T(8,128)(2,1)}, u32[]{:S(2)}, u32[]{:S(2)}) collective-permute-start(bf16[1024,1024]{1,0:T(8,128)(2,1)} %bitcast.18), channel_id=1, source_target_pairs={{0,1},{1,0},{2,3},{3,2},{4,5},{5,4},{6,7},{7,6},{8,9},{9,8},{10,11... | collective-permute-start | bytes 6291464 | tf_op jit(solution)/shard_map/ppermute | solution.py:300
  14.0 28.7 %all-to-all-start = ((bf16[8,128,256]{2,1,0:T(8,128)(2,1)}), bf16[8,128,256]{2,1,0:T(8,128)(2,1)S(1)}, u32[]{:S(2)}, u32[]{:S(2)}) async-start(bf16[8,128,256]{2,1,0:T(8,128)(2,1)} %get-tuple-element.13), calls=%async_computation | async-start | bytes 1048576 | tf_op jit(solution)/shard_map/all_to_all | solution.py:294
  24.2 6.1 %collective-permute-start.5 = (s32[32]{0:T(128)}, s32[32]{0:T(128)S(1)}, u32[]{:S(2)}, u32[]{:S(2)}) collective-permute-start(s32[32]{0:T(128)} %param.11), channel_id=1, source_target_pairs={{0,16},{16,0},{1,17},{17,1},{2,18},{18,2},{3,19},{19,3},{4,20},{20... | collective-permute-start | bytes 392 | tf_op jit(solution)/shard_map/ppermute | solution.py:302
  27.3 3.8 %collective-permute-start.3 = (bf16[128,128]{1,0:T(8,128)(2,1)S(1)}, bf16[128,128]{1,0:T(8,128)(2,1)S(1)}, u32[]{:S(2)}, u32[]{:S(2)}) collective-permute-start(bf16[128,128]{1,0:T(8,128)(2,1)S(1)} %get-tuple-element.19), channel_id=1, source_target_pairs={{0,1},{1,0},{2,3},{3,2},{4,5},{5,4},{6,7},{7,6},{8,9},{9,8},{10,11... | collective-permute-start | bytes 98312 | tf_op jit(solution)/shard_map/ppermute | solution.py:301
  31.1 11.6 %collective-permute-start.4 = (bf16[128,128]{1,0:T(8,128)(2,1)S(1)}, bf16[128,128]{1,0:T(8,128)(2,1)S(1)}, u32[]{:S(2)}, u32[]{:S(2)}) collective-permute-start(bf16[128,128]{1,0:T(8,128)(2,1)S(1)} %broadcast_select_fusion.gen_key_ref), channel_id=1, source_target_pairs={{8,0},{10,2},{12,4},{14,6},{9,1},{11,3},{13,5},{15,7},{24,16},{26,... | collective-permute-start | bytes 98312 | tf_op jit(solution)/shard_map/ppermute | solution.py:304
  32.5 10.3 %copy-start.13 = (s32[16]{0:T(128)S(1)}, s32[16]{0:T(128)}, u32[]{:S(2)}) copy-start(s32[16]{0:T(128)} %lengths_ref.1) | copy-start | bytes 196
  32.6 1.6 %copy-start.5 = (bf16[1,1024,1024]{2,1,0:T(8,128)(2,1)S(1)}, bf16[1,1024,1024]{2,1,0:T(8,128)(2,1)}, u32[]{:S(2)}) copy-start(bf16[1,1024,1024]{2,1,0:T(8,128)(2,1)} %param.14) | copy-start | bytes 6291460
  34.2 1.6 %copy-start.6 = (bf16[1,1024,1024]{2,1,0:T(8,128)(2,1)S(1)}, bf16[1,1024,1024]{2,1,0:T(8,128)(2,1)}, u32[]{:S(2)}) copy-start(bf16[1,1024,1024]{2,1,0:T(8,128)(2,1)} %param.15) | copy-start | bytes 6291460
  35.8 7.0 %copy-start.10 = (s32[16,32]{1,0:T(8,128)S(1)}, s32[16,32]{1,0:T(8,128)}, u32[]{:S(2)}) copy-start(s32[16,32]{1,0:T(8,128)} %holders_ref.1) | copy-start | bytes 6148
  38.4 2.1 %copy-start = (bf16[8,144,2048]{2,1,0:T(8,128)(2,1)}, bf16[8,144,2048]{2,1,0:T(8,128)(2,1)S(1)}, u32[]{:S(2)}) copy-start(bf16[8,144,2048]{2,1,0:T(8,128)(2,1)S(1)} %get-tuple-element.18.value_ref) | copy-start | bytes 14155780
  40.6 2.0 %copy-start.2 = (bf16[8,2048,128]{2,1,0:T(8,128)(2,1)}, bf16[8,2048,128]{2,1,0:T(8,128)(2,1)S(1)}, u32[]{:S(2)}) copy-start(bf16[8,2048,128]{2,1,0:T(8,128)(2,1)S(1)} %get-tuple-element.17.key_ref) | copy-start | bytes 12582916
  42.7 2.3 %copy-start.1 = (bf16[8,144,2048]{2,1,0:T(8,128)(2,1)S(1)}, bf16[8,144,2048]{2,1,0:T(8,128)(2,1)}, u32[]{:S(2)}) copy-start(bf16[8,144,2048]{2,1,0:T(8,128)(2,1)} %copy-done) | copy-start | bytes 14155780
  45.1 2.2 %copy-start.3 = (bf16[8,2048,128]{2,1,0:T(8,128)(2,1)S(1)}, bf16[8,2048,128]{2,1,0:T(8,128)(2,1)}, u32[]{:S(2)}) copy-start(bf16[8,2048,128]{2,1,0:T(8,128)(2,1)} %copy-done.2) | copy-start | bytes 12582916
  47.3 15.0 %copy-start.7 = (bf16[2,256,256]{2,1,0:T(8,128)(2,1)S(1)}, bf16[2,256,256]{2,1,0:T(8,128)(2,1)}, u32[]{:S(2)}) copy-start(bf16[2,256,256]{2,1,0:T(8,128)(2,1)} %embed_hbm.1) | copy-start | bytes 786436
  47.3 15.0 %copy-start.12 = (s32[2,32]{1,0:T(2,128)S(1)}, s32[2,32]{1,0:T(2,128)}, u32[]{:S(2)}) copy-start(s32[2,32]{1,0:T(2,128)} %codes_ref.1) | copy-start | bytes 772
  49.4 48.9 %copy-start.4 = (bf16[4096,256]{1,0:T(8,128)(2,1)S(1)}, bf16[4096,256]{1,0:T(8,128)(2,1)}, u32[]{:S(2)}) copy-start(bf16[4096,256]{1,0:T(8,128)(2,1)} %param.19) | copy-start | bytes 6291460
  49.4 27.6 %all-to-all-start.1 = ((bf16[16,144,128]{2,1,0:T(8,128)(2,1)}), bf16[16,144,128]{2,1,0:T(8,128)(2,1)S(1)}, u32[]{:S(2)}, u32[]{:S(2)}) async-start(bf16[16,144,128]{2,1,0:T(8,128)(2,1)} %bitcast.8), calls=%async_computation.1 | async-start | bytes 1179648 | tf_op jit(solution)/shard_map/all_to_all | solution.py:339

commit v5 on v4

--- a/solution.py
+++ b/solution.py
@@ -39,30 +39,32 @@
         )
 
 
-def look_kernel(pair_ref, mine_ref, other_ref, query_hbm, kv_hbm, query_out, kv_out, query_ref, kv_ref, sem):
-    copies = [
-        pltpu.make_async_copy(query_hbm, query_ref, sem.at[0]),
-        pltpu.make_async_copy(kv_hbm, kv_ref, sem.at[1]),
-    ]
-    for copy in copies:
-        copy.start()
-    levels, beams = mine_ref.shape
+def look_kernel(codes_ref, query_hbm, out_ref, query_ref, sem):
+    copy = pltpu.make_async_copy(query_hbm, query_ref, sem.at[0])
+    copy.start()
+    levels, beams = codes_ref.shape
+    hots = [one_hot_rows(codes_ref[level : level + 1], query_ref.shape[1]) for level in range(levels)]
+    copy.wait()
+    for level, hot in enumerate(hots):
+        found = jnp.dot(hot, query_ref[level], preferred_element_type=jnp.float32).astype(jnp.bfloat16)
+        for target in range(out_ref.shape[0]):
+            out_ref[target, level * beams : (level + 1) * beams] = found
+
+
+def generated_kernel(pair_ref, mine_ref, other_ref, kv_hbm, out_ref, kv_ref, sem):
+    copy = pltpu.make_async_copy(kv_hbm, kv_ref, sem.at[0])
+    copy.start()
+    levels, beams = kv_ref.shape[0], mine_ref.shape[1]
     hots = [
-        jnp.concatenate([one_hot_rows(ref[level : level + 1], query_ref.shape[1]) for ref in (mine_ref, other_ref)])
+        jnp.concatenate([one_hot_rows(ref[level : level + 1], kv_ref.shape[1]) for ref in (mine_ref, other_ref)])
         for level in range(levels)
     ]
-    for copy in copies:
-        copy.wait()
-    half = levels * beams
+    copy.wait()
     for level, hot in enumerate(hots):
-        queries = jnp.dot(hot, query_ref[level], preferred_element_type=jnp.float32).astype(jnp.bfloat16)
-        kvs = jnp.dot(hot, kv_ref[level], preferred_element_type=jnp.float32).astype(jnp.bfloat16)
+        found = jnp.dot(hot, kv_ref[level], preferred_element_type=jnp.float32).astype(jnp.bfloat16)
         for part, x in enumerate((pair_ref[0], 1 - pair_ref[0])):
-            rows = slice(part * beams, (part + 1) * beams)
-            place = pl.ds(pl.multiple_of(x * half + level * beams, beams), beams)
-            for copy in range(query_out.shape[0]):
-                query_out[copy, place] = queries[rows]
-            kv_out[place] = kvs[rows]
+            place = pl.ds(pl.multiple_of((x * levels + level) * beams, beams), beams)
+            out_ref[place] = found[part * beams : (part + 1) * beams]
 
 
 def stage_kernel(*refs):
@@ -124,7 +126,7 @@
     out_ref, score_ref,
 ):
     heads, slots = key_ref.shape[0], key_ref.shape[1]
-    half = query_ref.shape[1] // 2
+    half = query_ref.shape[1]
     width = 4 * half
     request, place, gen_head = meta_ref[0], meta_ref[1], meta_ref[2]
 
@@ -140,10 +142,11 @@
     live = near_live + far_live
 
     def queries(head):
-        pair = query_ref[head]
-        return jnp.concatenate(
-            [pair[x * half : (x + 1) * half, h * HEAD : (h + 1) * HEAD] for x in range(2) for h in range(2)], axis=0
-        )
+        pieces = []
+        for x in range(2):
+            pair = query_ref[x * heads + head]
+            pieces += [pair[:, h * HEAD : (h + 1) * HEAD] for h in range(2)]
+        return jnp.concatenate(pieces, axis=0)
 
     def write(head, sums, total, top):
         for x in range(2):
@@ -273,7 +276,18 @@
     dma = pltpu.SemaphoreType.DMA
     swap = [(0, 1), (1, 0)]
 
-    other_codes = lax.ppermute(codes, "pair", swap)
+    hbm = lambda x: pltpu.with_memory_space_constraint(x, pltpu.HBM)
+    vmem = lambda x: pltpu.with_memory_space_constraint(x, pltpu.VMEM)
+
+    query_rows = call(
+        look_kernel,
+        array((2 * z_count, half, width), bf16),
+        "look",
+        "vh",
+        4,
+        scratch_shapes=[pltpu.VMEM(query_table.shape, bf16), dma((1,))],
+    )(codes, hbm(query_table))
+    queries = lax.all_to_all(query_rows, ("pair", "z"), split_axis=0, concat_axis=0, tiled=True)
     residual = call(
         residual_kernel,
         array((half, width), f32),
@@ -281,36 +295,36 @@
         "vh",
         4,
         scratch_shapes=[pltpu.VMEM(embed_table.shape, bf16), dma((1,))],
-    )(codes, embed_table)
-
-    query_rows, kv_rows = call(
-        look_kernel,
-        (array((z_count, rows, width), bf16), array((rows, HEAD), bf16)),
-        "look",
-        "svvhh",
-        4,
-        scratch_shapes=[pltpu.VMEM(query_table.shape, bf16), pltpu.VMEM(kv_table.shape, bf16), dma((2,))],
-    )(pair.reshape(1), codes, other_codes, query_table, kv_table)
-    queries = lax.all_to_all(query_rows, "z", split_axis=0, concat_axis=0, tiled=True)
-
-    kv_rows, near_keys, near_values, parents = lax.optimization_barrier(
-        (kv_rows, history_keys[0], history_values[0], parents)
-    )
+    )(codes, hbm(embed_table))
+
+    query_rows, mine, near_keys, near_values = lax.optimization_barrier(
+        (query_rows, jnp.concatenate([codes, parents[None]]), history_keys[0], history_values[0])
+    )
+    other = lax.ppermute(mine, "pair", swap)
+    other_parents = other[levels]
     far_keys = lax.ppermute(near_keys, "core", swap)
     far_values = lax.ppermute(near_values, "core", swap)
+    kv_rows = call(
+        generated_kernel,
+        array((rows, HEAD), bf16),
+        "generated",
+        "svvh",
+        4,
+        scratch_shapes=[pltpu.VMEM(kv_table.shape, bf16), dma((1,))],
+    )(pair.reshape(1), mine, other, hbm(kv_table))
     far_kv = lax.ppermute(kv_rows, "core", swap)
-    other_parents = lax.ppermute(parents, "pair", swap)
     gen_keys = jnp.where(first, kv_rows, far_kv)
     gen_values = lax.ppermute(gen_keys, "z", [(i + z_count // 2, i) for i in range(z_count // 2)])
     staged_keys, staged_values = call(
         stage_kernel,
-        (array((KEY_HEADS, 2 * slots, HEAD), bf16), array((KEY_HEADS, CHUNK, 2 * slots), bf16)),
+        (pltpu.VMEM((KEY_HEADS, 2 * slots, HEAD), bf16), pltpu.VMEM((KEY_HEADS, CHUNK, 2 * slots), bf16)),
         "stage",
         "hhaa",
         8,
         scratch_shapes=[pltpu.VMEM((2, slots, KEY_HEADS * HEAD), bf16), dma((2 * KEY_HEADS,)), dma((2,))],
         cost_estimate=pl.CostEstimate(flops=0, bytes_accessed=16 * MIB, transcendentals=0),
-    )(near_keys, near_values, far_keys, far_values)
+    )(hbm(near_keys), hbm(near_values), far_keys, far_values)
+    staged_keys, staged_values = vmem(staged_keys), vmem(staged_values)
 
     lower = jnp.where(first, parents, other_parents)
     upper = jnp.where(first, other_parents, parents)

time: 101 us -> 97.2 us (0.962)
  Pallas kernels: 7.62 us -> 16.6 us
  starting transfers between devices: 39 us -> 32.4 us
  local copies, waits for them, and re-layouts: 14.5 us -> 9.5 us
  blocking collectives: 21 us -> 19.7 us
    pallas_call x1, Pallas kernels: 2.11 us -> 7.46 us  [shards(): call(attend_kernel, array((2, z_count, CHUNK, 2 * half), bf16), 'attend',...]
    unnamed x28 -> x18, local copies, waits for them, and re-layouts: 14.4 us -> 9.34 us
    all_to_all x1, starting transfers between devices: 12.8 us -> 8.48 us  [shards(): lax.all_to_all(partials.reshape(shape), ('pair', 'z'), split_axis=0, conc...]
    ppermute x2 -> x1, starting transfers between devices: 6.22 us -> 3.27 us  [shards(): other = lax.ppermute(mine, 'pair', swap)]
    pallas_call x2 -> x3, Pallas kernels: 3.93 us -> 6.71 us  [the longest x1 3.65 us: shards(): call(stage_kernel, (pltpu.VMEM((KEY_HEADS, 2 * slots, HEAD), bf16), pltpu...]
    all_gather x1, blocking collectives: 21 us -> 19.7 us  [shards(): gathered = lax.all_gather(attention, ('z', 'core'), axis=0)]
    ppermute x1, starting transfers between devices: 3.73 us -> 2.57 us  [shards(): far_keys = lax.ppermute(near_keys, 'core', swap)]
    all_to_all x1, starting transfers between devices: 10 us -> 11.1 us  [shards(): lax.all_to_all(query_rows, ('pair', 'z'), split_axis=0, concat_axis=0, ti...]
  transfers between devices with their start and end apart: 8 -> 7, of which waited for: 4 -> 3; matrix products, arithmetic and copies ran while one was open for 1% -> 1% of each run, Pallas kernels for 3% -> 6%
where the time goes in v5:
time: 97.2 us; the launch traced here: 95.7 us
  starting transfers between devices  32.4 us (33%)
  blocking collectives  19.7 us (20%)
  Pallas kernels  16.6 us (17%)
  waiting for transfers between devices  15.9 us (16%)
  local copies, waits for them, and re-layouts  9.5 us (10%)
  other arithmetic  1.43 us (1%)
    all_gather x1, blocking collectives, shards(): gathered = lax.all_gather(attention, ('z', 'core'), axis=0)  19.7 us
    all_to_all x1, waiting for transfers between devices, shards(): lax.all_to_all(partials.reshape(shape), ('pair', 'z'), split_axis=0, conc...  14.7 us
    all_to_all x1, starting transfers between devices, shards(): lax.all_to_all(query_rows, ('pair', 'z'), split_axis=0, concat_axis=0, ti...  11.1 us
    unnamed x18, local copies, waits for them, and re-layouts  9.34 us
    all_to_all x1, starting transfers between devices, shards(): lax.all_to_all(partials.reshape(shape), ('pair', 'z'), split_axis=0, conc...  8.48 us
    pallas_call x1, Pallas kernels, shards(): call(attend_kernel, array((2, z_count, CHUNK, 2 * half), bf16), 'attend',...  7.46 us
    ppermute x1, starting transfers between devices, shards(): far_kv = lax.ppermute(kv_rows, 'core', swap)  3.76 us
    pallas_call x1, Pallas kernels, shards(): call(stage_kernel, (pltpu.VMEM((KEY_HEADS, 2 * slots, HEAD), bf16), pltpu...  3.65 us
  transfers between devices with their start and end apart: 7, of which 3 were waited for; matrix products, arithmetic and copies ran while one was open for 1% of the time, Pallas kernels for 6%

profile of v5, /device:TPU:57, one launch (start us, length us, event | category | flops | bytes accessed | tf_op | source)
XLA Modules:
  0.0 95.7 jit_solution(13960607310462212884)
XLA Ops:
  0.0 0.0 copy-start.5
  0.0 0.7 copy-done.5
  0.7 2.0 %look.1 = bf16[16,64,256]{2,1,0:T(8,128)(2,1)} custom-call(s32[2,32]{1,0:T(2,128)S(1)} %copy-done.5, bf16[2,256,256]{2,1,0:T(8,128)(2,1)} %query_hbm.1), custom_call_target="tpu_custom_call" | custom-call | tf_op jit(solution)/shard_map/look/pallas_call | solution.py:282
  2.7 0.7 pad_add_fusion.mine_ref
  3.3 2.6 %collective-permute-start = (bf16[1024,1024]{1,0:T(8,128)(2,1)}, bf16[1024,1024]{1,0:T(8,128)(2,1)S(1)}, u32[]{:S(2)}, u32[]{:S(2)}) collective-permute-start(bf16[1024,1024]{1,0:T(8,128)(2,1)} %bitcast.20), channel_id=1, source_target_pairs={{0,1},{1,0},{2,3},{3,2},{4,5},{5,4},{6,7},{7,6},{8,9},{9,8},{10,11... | collective-permute-start | bytes 6291464 | tf_op jit(solution)/shard_map/ppermute | solution.py:305
  5.9 1.9 %collective-permute-start.1 = (bf16[1024,1024]{1,0:T(8,128)(2,1)}, bf16[1024,1024]{1,0:T(8,128)(2,1)}, u32[]{:S(2)}, u32[]{:S(2)}) collective-permute-start(bf16[1024,1024]{1,0:T(8,128)(2,1)} %bitcast.22), channel_id=1, source_target_pairs={{0,1},{1,0},{2,3},{3,2},{4,5},{5,4},{6,7},{7,6},{8,9},{9,8},{10,11... | collective-permute-start | bytes 6291464 | tf_op jit(solution)/shard_map/ppermute | solution.py:306
  7.9 11.1 %all-to-all-start = ((bf16[16,64,256]{2,1,0:T(8,128)(2,1)}), bf16[16,64,256]{2,1,0:T(8,128)(2,1)S(1)}, u32[]{:S(2)}, u32[]{:S(2)}) async-start(bf16[16,64,256]{2,1,0:T(8,128)(2,1)} %look.1), calls=%async_computation | async-start | bytes 1048576 | tf_op jit(solution)/shard_map/all_to_all | solution.py:290
  18.9 3.3 %collective-permute-start.2 = (s32[3,32]{1,0:T(4,128)S(1)}, s32[3,32]{1,0:T(4,128)S(1)}, u32[]{:S(2)}, u32[]{:S(2)}) collective-permute-start(s32[3,32]{1,0:T(4,128)S(1)} %pad_add_fusion.mine_ref), channel_id=1, source_target_pairs={{0,16},{16,0},{1,17},{17,1},{2,18},{18,2},{3,19},{19,3},{4,20},{20... | collective-permute-start | bytes 1160 | tf_op jit(solution)/shard_map/ppermute | solution.py:303
  22.2 0.1 pad_add_fusion.2.meta_ref
  22.3 1.0 %collective-permute-done.2.other_ref = s32[3,32]{1,0:T(4,128)S(1)} collective-permute-done((s32[3,32]{1,0:T(4,128)S(1)}, s32[3,32]{1,0:T(4,128)S(1)}, u32[]{:S(2)}, u32[]{:S(2)}) %collective-permute-start.2) | collective-permute-done | bytes 416 | tf_op jit(solution)/shard_map/ppermute | solution.py:303
  23.3 1.1 %generated.1 = bf16[128,128]{1,0:T(8,128)(2,1)S(1)} custom-call(s32[1]{0:T(128)} %bitcast.6.pair_ref, s32[3,32]{1,0:T(4,128)S(1)} %pad_add_fusion.mine_ref, s32[3,32]{1,0:T(4,128)S(1)} %collective-permute-done.2.other_ref, bf16[2,256,128]{2,1,0:T(8,128)(2,1)} %kv_hbm.1), custom_call_target="tpu_custom_call" | custom-call | tf_op jit(solution)/shard_map/generated/pallas_call | solution.py:307
  24.4 3.8 %collective-permute-start.3 = (bf16[128,128]{1,0:T(8,128)(2,1)S(1)}, bf16[128,128]{1,0:T(8,128)(2,1)S(1)}, u32[]{:S(2)}, u32[]{:S(2)}) collective-permute-start(bf16[128,128]{1,0:T(8,128)(2,1)S(1)} %generated.1), channel_id=1, source_target_pairs={{0,1},{1,0},{2,3},{3,2},{4,5},{5,4},{6,7},{7,6},{8,9},{9,8},{10,11... | collective-permute-start | bytes 98312 | tf_op jit(solution)/shard_map/ppermute | solution.py:315
  28.2 0.7 fusion.1
  28.9 0.2 collective-permute-done.3
  29.0 1.3 %collective-permute-start.4 = (bf16[128,128]{1,0:T(8,128)(2,1)S(1)}, bf16[128,128]{1,0:T(8,128)(2,1)S(1)}, u32[]{:S(2)}, u32[]{:S(2)}) collective-permute-start(bf16[128,128]{1,0:T(8,128)(2,1)S(1)} %broadcast_select_fusion.gen_key_ref), channel_id=1, source_target_pairs={{8,0},{10,2},{12,4},{14,6},{9,1},{11,3},{13,5},{15,7},{24,16},{26,... | collective-permute-start | bytes 98312 | tf_op jit(solution)/shard_map/ppermute | solution.py:317
  30.4 0.1 concatenate.7
  30.4 0.1 reshape.17.parent_ref
  30.5 0.0 copy-start.7
  30.5 0.0 copy-start.8
  30.5 0.0 collective-permute-done.refs_2_
  30.5 0.0 collective-permute-done.1.refs_3_
  30.5 3.7 %stage.1 = (bf16[8,2048,128]{2,1,0:T(8,128)(2,1)S(1)}, bf16[8,144,2048]{2,1,0:T(8,128)(2,1)S(1)}) custom-call(bf16[1024,1024]{1,0:T(8,128)(2,1)} %bitcast.21, bf16[1024,1024]{1,0:T(8,128)(2,1)} %bitcast.23, bf16[1024,1024]{1,0:T(8,128)(2,1)S(1)} %collective-permute-done.refs_2_, bf16[1024,1024]{1,0:T(8,128)(2,1)} %collective-permute-done.1.refs_3_), custom_call_target="tpu_custom_call" | custom-call | bytes 16777216 | tf_op jit(solution)/shard_map/stage/pallas_call | solution.py:318
  34.2 0.0 copy-start
  34.2 2.1 %copy-done = bf16[8,144,2048]{2,1,0:T(8,128)(2,1)} copy-done((bf16[8,144,2048]{2,1,0:T(8,128)(2,1)}, bf16[8,144,2048]{2,1,0:T(8,128)(2,1)S(1)}, u32[]{:S(2)}) %copy-start) | copy-done | bytes 4718616
  36.3 0.0 copy-start.2
  36.3 2.0 %copy-done.2 = bf16[8,2048,128]{2,1,0:T(8,128)(2,1)} copy-done((bf16[8,2048,128]{2,1,0:T(8,128)(2,1)}, bf16[8,2048,128]{2,1,0:T(8,128)(2,1)S(1)}, u32[]{:S(2)}) %copy-start.2) | copy-done | bytes 4194328
  38.3 0.0 collective-permute-done.4.gen_value_ref
  38.3 0.0 all-to-all-done.query_ref
  38.3 0.0 copy-done.7
  38.3 0.0 copy-done.8
  38.3 0.0 copy-start.1
  38.4 2.3 %copy-done.1 = bf16[8,144,2048]{2,1,0:T(8,128)(2,1)S(1)} copy-done((bf16[8,144,2048]{2,1,0:T(8,128)(2,1)S(1)}, bf16[8,144,2048]{2,1,0:T(8,128)(2,1)}, u32[]{:S(2)}) %copy-start.1) | copy-done | bytes 4718616
  40.7 0.0 copy-start.3
  40.7 2.2 %copy-done.3 = bf16[8,2048,128]{2,1,0:T(8,128)(2,1)S(1)} copy-done((bf16[8,2048,128]{2,1,0:T(8,128)(2,1)S(1)}, bf16[8,2048,128]{2,1,0:T(8,128)(2,1)}, u32[]{:S(2)}) %copy-start.3) | copy-done | bytes 4194328
  42.9 0.0 copy-start.6
  42.9 7.5 %attend.1 = bf16[2,8,144,128]{3,2,1,0:T(8,128)(2,1)} custom-call(s32[3]{0:T(128)S(1)} %pad_add_fusion.2.meta_ref, s32[16]{0:T(128)S(1)} %copy-done.8, s32[16,32]{1,0:T(8,128)S(1)} %copy-done.7, bf16[16,64,256]{2,1,0:T(8,128)(2,1)S(1)} %all-to-all-done.query_ref, bf16[8,2048,128]{2,1,0:T(8,128)(2,1)S(1)} %copy-done.3, bf16[8,144,2048]{2,1,0:T(8,128)(2,1)S(1)} %copy-done.1, ...), custom_call_target="tpu_custom_call" | custom-call | flops 2147483648 | bytes 4194304 | tf_op jit(solution)/shard_map/attend/pallas_call | solution.py:338
  50.3 0.0 copy-start.4
  50.3 8.5 %all-to-all-start.1 = ((bf16[16,144,128]{2,1,0:T(8,128)(2,1)}), bf16[16,144,128]{2,1,0:T(8,128)(2,1)S(1)}, u32[]{:S(2)}, u32[]{:S(2)}) async-start(bf16[16,144,128]{2,1,0:T(8,128)(2,1)} %bitcast.10), calls=%async_computation.1 | async-start | bytes 1179648 | tf_op jit(solution)/shard_map/all_to_all | solution.py:353
  58.8 0.0 copy-done.6
  58.8 1.1 %residual.1.residual_ref = f32[64,256]{1,0:T(8,128)S(1)} custom-call(s32[2,32]{1,0:T(2,128)S(1)} %copy-done.6, bf16[2,256,256]{2,1,0:T(8,128)(2,1)} %embed_hbm.1), custom_call_target="tpu_custom_call" | custom-call | tf_op jit(solution)/shard_map/residual/pallas_call | solution.py:291
  60.0 14.7 %all-to-all-done.1.parts_ref = bf16[16,144,128]{2,1,0:T(8,128)(2,1)S(1)} async-done(((bf16[16,144,128]{2,1,0:T(8,128)(2,1)}), bf16[16,144,128]{2,1,0:T(8,128)(2,1)S(1)}, u32[]{:S(2)}, u32[]{:S(2)}) %all-to-all-start.1) | async-done | bytes 589856 | tf_op jit(solution)/shard_map/all_to_all | solution.py:353
  74.7 0.2 combine.1
  74.9 19.7 %all-gather = bf16[1024,256]{1,0:T(8,128)(2,1)S(1)} all-gather(bf16[64,256]{1,0:T(8,128)(2,1)S(1)} %combine.1), channel_id=2, replica_groups=mesh['grp'=16,'pair'=2,'z'=8,'core'=2] {'z','core'}, dimensions={0}, use_global_device_ids=true | all-gather | bytes 557056 | tf_op jit(solution)/shard_map/all_gather | solution.py:355
  94.6 0.0 copy-done.4
  94.6 1.1 %project.1 = bf16[64,256]{1,0:T(8,128)(2,1)} custom-call(bf16[16,64,256]{2,1,0:T(8,128)(2,1)S(1)} %bitcast.19, bf16[16,256,256]{2,1,0:T(8,128)(2,1)S(1)} %bitcast.18, f32[64,256]{1,0:T(8,128)S(1)} %residual.1.residual_ref), custom_call_target="tpu_custom_call" | custom-call | tf_op jit(solution)/shard_map/project/pallas_call | solution.py:356
  (3 shorter events, 0.0 us)
Async XLA Ops:
  0.0 0.7 copy-start.5
  3.3 27.2 %collective-permute-start = (bf16[1024,1024]{1,0:T(8,128)(2,1)}, bf16[1024,1024]{1,0:T(8,128)(2,1)S(1)}, u32[]{:S(2)}, u32[]{:S(2)}) collective-permute-start(bf16[1024,1024]{1,0:T(8,128)(2,1)} %bitcast.20), channel_id=1, source_target_pairs={{0,1},{1,0},{2,3},{3,2},{4,5},{5,4},{6,7},{7,6},{8,9},{9,8},{10,11... | collective-permute-start | bytes 6291464 | tf_op jit(solution)/shard_map/ppermute | solution.py:305
  5.9 24.6 %collective-permute-start.1 = (bf16[1024,1024]{1,0:T(8,128)(2,1)}, bf16[1024,1024]{1,0:T(8,128)(2,1)}, u32[]{:S(2)}, u32[]{:S(2)}) collective-permute-start(bf16[1024,1024]{1,0:T(8,128)(2,1)} %bitcast.22), channel_id=1, source_target_pairs={{0,1},{1,0},{2,3},{3,2},{4,5},{5,4},{6,7},{7,6},{8,9},{9,8},{10,11... | collective-permute-start | bytes 6291464 | tf_op jit(solution)/shard_map/ppermute | solution.py:306
  7.9 30.5 %all-to-all-start = ((bf16[16,64,256]{2,1,0:T(8,128)(2,1)}), bf16[16,64,256]{2,1,0:T(8,128)(2,1)S(1)}, u32[]{:S(2)}, u32[]{:S(2)}) async-start(bf16[16,64,256]{2,1,0:T(8,128)(2,1)} %look.1), calls=%async_computation | async-start | bytes 1048576 | tf_op jit(solution)/shard_map/all_to_all | solution.py:290
  18.9 4.4 %collective-permute-start.2 = (s32[3,32]{1,0:T(4,128)S(1)}, s32[3,32]{1,0:T(4,128)S(1)}, u32[]{:S(2)}, u32[]{:S(2)}) collective-permute-start(s32[3,32]{1,0:T(4,128)S(1)} %pad_add_fusion.mine_ref), channel_id=1, source_target_pairs={{0,16},{16,0},{1,17},{17,1},{2,18},{18,2},{3,19},{19,3},{4,20},{20... | collective-permute-start | bytes 1160 | tf_op jit(solution)/shard_map/ppermute | solution.py:303
  24.4 4.6 %collective-permute-start.3 = (bf16[128,128]{1,0:T(8,128)(2,1)S(1)}, bf16[128,128]{1,0:T(8,128)(2,1)S(1)}, u32[]{:S(2)}, u32[]{:S(2)}) collective-permute-start(bf16[128,128]{1,0:T(8,128)(2,1)S(1)} %generated.1), channel_id=1, source_target_pairs={{0,1},{1,0},{2,3},{3,2},{4,5},{5,4},{6,7},{7,6},{8,9},{9,8},{10,11... | collective-permute-start | bytes 98312 | tf_op jit(solution)/shard_map/ppermute | solution.py:315
  29.0 9.3 %collective-permute-start.4 = (bf16[128,128]{1,0:T(8,128)(2,1)S(1)}, bf16[128,128]{1,0:T(8,128)(2,1)S(1)}, u32[]{:S(2)}, u32[]{:S(2)}) collective-permute-start(bf16[128,128]{1,0:T(8,128)(2,1)S(1)} %broadcast_select_fusion.gen_key_ref), channel_id=1, source_target_pairs={{8,0},{10,2},{12,4},{14,6},{9,1},{11,3},{13,5},{15,7},{24,16},{26,... | collective-permute-start | bytes 98312 | tf_op jit(solution)/shard_map/ppermute | solution.py:317
  30.5 7.8 %copy-start.7 = (s32[16,32]{1,0:T(8,128)S(1)}, s32[16,32]{1,0:T(8,128)}, u32[]{:S(2)}) copy-start(s32[16,32]{1,0:T(8,128)} %holders_ref.1) | copy-start | bytes 6148
  30.5 7.8 %copy-start.8 = (s32[16]{0:T(128)S(1)}, s32[16]{0:T(128)}, u32[]{:S(2)}) copy-start(s32[16]{0:T(128)} %lengths_ref.1) | copy-start | bytes 196
  34.2 2.1 %copy-start = (bf16[8,144,2048]{2,1,0:T(8,128)(2,1)}, bf16[8,144,2048]{2,1,0:T(8,128)(2,1)S(1)}, u32[]{:S(2)}) copy-start(bf16[8,144,2048]{2,1,0:T(8,128)(2,1)S(1)} %get-tuple-element.13.value_ref) | copy-start | bytes 14155780
  36.3 2.0 %copy-start.2 = (bf16[8,2048,128]{2,1,0:T(8,128)(2,1)}, bf16[8,2048,128]{2,1,0:T(8,128)(2,1)S(1)}, u32[]{:S(2)}) copy-start(bf16[8,2048,128]{2,1,0:T(8,128)(2,1)S(1)} %get-tuple-element.12.key_ref) | copy-start | bytes 12582916
  38.3 2.3 %copy-start.1 = (bf16[8,144,2048]{2,1,0:T(8,128)(2,1)S(1)}, bf16[8,144,2048]{2,1,0:T(8,128)(2,1)}, u32[]{:S(2)}) copy-start(bf16[8,144,2048]{2,1,0:T(8,128)(2,1)} %copy-done) | copy-start | bytes 14155780
  40.7 2.2 %copy-start.3 = (bf16[8,2048,128]{2,1,0:T(8,128)(2,1)S(1)}, bf16[8,2048,128]{2,1,0:T(8,128)(2,1)}, u32[]{:S(2)}) copy-start(bf16[8,2048,128]{2,1,0:T(8,128)(2,1)} %copy-done.2) | copy-start | bytes 12582916
  42.9 16.0 %copy-start.6 = (s32[2,32]{1,0:T(2,128)S(1)}, s32[2,32]{1,0:T(2,128)}, u32[]{:S(2)}) copy-start(s32[2,32]{1,0:T(2,128)} %codes_ref.3) | copy-start | bytes 772
  50.3 44.3 %copy-start.4 = (bf16[4096,256]{1,0:T(8,128)(2,1)S(1)}, bf16[4096,256]{1,0:T(8,128)(2,1)}, u32[]{:S(2)}) copy-start(bf16[4096,256]{1,0:T(8,128)(2,1)} %param.19) | copy-start | bytes 6291460
  50.3 24.3 %all-to-all-start.1 = ((bf16[16,144,128]{2,1,0:T(8,128)(2,1)}), bf16[16,144,128]{2,1,0:T(8,128)(2,1)S(1)}, u32[]{:S(2)}, u32[]{:S(2)}) async-start(bf16[16,144,128]{2,1,0:T(8,128)(2,1)} %bitcast.10), calls=%async_computation.1 | async-start | bytes 1179648 | tf_op jit(solution)/shard_map/all_to_all | solution.py:353

commit v6 on v5

--- a/solution.py
+++ b/solution.py
@@ -39,12 +39,19 @@
         )
 
 
-def look_kernel(codes_ref, query_hbm, out_ref, query_ref, sem):
-    copy = pltpu.make_async_copy(query_hbm, query_ref, sem.at[0])
-    copy.start()
-    levels, beams = codes_ref.shape
-    hots = [one_hot_rows(codes_ref[level : level + 1], query_ref.shape[1]) for level in range(levels)]
-    copy.wait()
+def look_kernel(codes_hbm, parents_hbm, query_hbm, out_ref, mine_ref, query_ref, sem):
+    levels, beams = codes_hbm.shape
+    copies = [
+        pltpu.make_async_copy(codes_hbm, mine_ref.at[pl.ds(0, levels)], sem.at[0]),
+        pltpu.make_async_copy(parents_hbm, mine_ref.at[pl.ds(levels, 1)], sem.at[1]),
+        pltpu.make_async_copy(query_hbm, query_ref, sem.at[2]),
+    ]
+    for copy in copies:
+        copy.start()
+    copies[0].wait()
+    copies[1].wait()
+    hots = [one_hot_rows(mine_ref[level : level + 1], query_ref.shape[1]) for level in range(levels)]
+    copies[2].wait()
     for level, hot in enumerate(hots):
         found = jnp.dot(hot, query_ref[level], preferred_element_type=jnp.float32).astype(jnp.bfloat16)
         for target in range(out_ref.shape[0]):
@@ -67,36 +74,6 @@
             out_ref[place] = found[part * beams : (part + 1) * beams]
 
 
-def stage_kernel(*refs):
-    *blocks, key_out, value_out, value_ref, key_sem, value_sem = refs
-    heads = key_out.shape[0]
-    count = len(blocks) // 2
-    slots = value_ref.shape[1]
-    key_copies, value_copies = [], []
-    for block in range(count):
-        span = pl.ds(block * slots, slots)
-        value_copies.append(
-            pltpu.make_async_copy(blocks[2 * block + 1], value_ref.at[block], value_sem.at[block])
-        )
-        for head in range(heads):
-            lanes = pl.ds(head * HEAD, HEAD)
-            key_copies.append(
-                pltpu.make_async_copy(
-                    blocks[2 * block].at[:, lanes], key_out.at[head, span], key_sem.at[block * heads + head]
-                )
-            )
-    for copy in value_copies + key_copies:
-        copy.start()
-    value_out[:, HEAD:CHUNK] = jnp.ones((heads, STAT, count * slots), jnp.bfloat16)
-    for block in range(count):
-        value_copies[block].wait()
-        for head in range(heads):
-            lanes = slice(head * HEAD, (head + 1) * HEAD)
-            value_out[head, 0:HEAD, block * slots : (block + 1) * slots] = jnp.transpose(value_ref[block, :, lanes])
-    for copy in key_copies:
-        copy.wait()
-
-
 def split3(value):
     high = value.astype(jnp.bfloat16).astype(jnp.float32)
     rest = value - high
@@ -121,9 +98,13 @@
     return lax.dot_general(keys, rows, (((1,), (1,)), ((), ())), preferred_element_type=jnp.float32)
 
 
+def extended(values):
+    return jnp.concatenate([jnp.transpose(values), jnp.ones((STAT, values.shape[0]), jnp.bfloat16)], axis=0)
+
+
 def attend_kernel(
-    meta_ref, lengths_ref, holders_ref, query_ref, key_ref, value_ref, gen_key_ref, gen_value_ref, parent_ref,
-    out_ref, score_ref,
+    meta_ref, lengths_ref, holders_ref, query_ref, near_key, near_value, far_key, far_value, kv_ref, far_kv_ref,
+    gen_value_ref, mine_ref, other_ref, out_ref, score_ref, key_ref, value_ref, key_sem, value_sem,
 ):
     heads, slots = key_ref.shape[0], key_ref.shape[1]
     half = query_ref.shape[1]
@@ -154,7 +135,29 @@
             out_ref[x, head, 0:HEAD] = sums[:, lanes].astype(jnp.bfloat16)
             out_ref[x, head, HEAD:CHUNK] = stat_rows(top[:, lanes], total[:, lanes])
 
+    def copies(head, keys):
+        sources, target, sem = ((near_key, far_key), key_ref, key_sem) if keys else ((near_value, far_value), value_ref, value_sem)
+        lanes = pl.ds(pl.multiple_of(head * HEAD, HEAD), HEAD)
+        return [
+            pltpu.make_async_copy(
+                source.at[:, lanes], target.at[head, pl.ds(block * block_slots, block_slots)], sem.at[block * heads + head]
+            )
+            for block, source in enumerate(sources)
+        ]
+
+    def wait(head, keys):
+        for copy in copies(head, keys):
+            copy.wait()
+
     def attend(masked):
+        def begin(head, _):
+            for keys in (True, False):
+                for copy in copies(head, keys):
+                    copy.start()
+            return 0
+
+        lax.fori_loop(0, heads, begin, 0)
+
         def score(head, at):
             scores = scores_of(key_ref[head], queries(head))
             if masked:
@@ -166,17 +169,25 @@
 
         def finish(head, at, top):
             weights = jnp.exp2((score_ref[at] - top) * EXP2_SCALE).astype(jnp.bfloat16)
-            sums = jnp.dot(value_ref[head], weights, preferred_element_type=jnp.float32)
+            sums = jnp.dot(extended(value_ref[head]), weights, preferred_element_type=jnp.float32)
             write(head, sums[0:HEAD], sums[HEAD : HEAD + 1], top)
 
         def step(i, top):
+            wait(2 * i + 1, True)
+            wait(2 * i + 2, True)
+            wait(2 * i, False)
+            wait(2 * i + 1, False)
             later = score(2 * i + 1, 1)
             finish(2 * i, 0, top)
-            top = score(jnp.minimum(2 * i + 2, heads - 1), 0)
+            top = score(2 * i + 2, 0)
             finish(2 * i + 1, 1, later)
             return top
 
+        wait(0, True)
         top = lax.fori_loop(0, heads // 2 - 1, step, score(0, 0))
+        wait(heads - 1, True)
+        wait(heads - 2, False)
+        wait(heads - 1, False)
         later = score(heads - 1, 1)
         finish(heads - 2, 0, top)
         finish(heads - 1, 1, later)
@@ -203,14 +214,20 @@
 
     @pl.when(gen_head >= 0)
     def _():
-        values = jnp.concatenate(
-            [jnp.transpose(gen_value_ref[...]), jnp.ones((STAT, 2 * half), jnp.bfloat16)], axis=0
-        )
+        values = extended(gen_value_ref[...])
         row = lax.broadcasted_iota(jnp.int32, (2 * half, width), 0)
         lane = lax.broadcasted_iota(jnp.int32, (2 * half, width), 1)
         own = (lane // (2 * half)) * half + lane % half
-        allowed = (row == own) | (row == parent_ref[...])
-        scores = jnp.where(allowed, scores_of(gen_key_ref[...], queries(gen_head)), DEAD)
+        beams = mine_ref.shape[1]
+        swapped = meta_ref[3] != 0
+        mine, other = (ref[mine_ref.shape[0] - 1 :] for ref in (mine_ref, other_ref))
+        pieces = []
+        for parents in (jnp.where(swapped, other, mine), jnp.where(swapped, mine, other)):
+            parents = (parents // beams) * half + parents % beams
+            pieces += [jnp.full_like(parents, -1), parents] * 2
+        allowed = (row == own) | (row == jnp.concatenate(pieces, axis=1))
+        keys = jnp.where(swapped, far_kv_ref[...], kv_ref[...])
+        scores = jnp.where(allowed, scores_of(keys, queries(gen_head)), DEAD)
         before = jnp.concatenate([out_ref[x, gen_head] for x in range(2)], axis=1)
         old_top, old_total = read_stats(before[HEAD:CHUNK])
         top = jnp.maximum(old_top, jnp.max(scores, axis=0, keepdims=True))
@@ -270,23 +287,21 @@
     z_count = lax.axis_size("z")
     pair, z, core = lax.axis_index("pair"), lax.axis_index("z"), lax.axis_index("core")
     hist = 2 * z + core
-    first = pair == 0
     bf16, f32 = jnp.bfloat16, jnp.float32
     array = jax.ShapeDtypeStruct
     dma = pltpu.SemaphoreType.DMA
     swap = [(0, 1), (1, 0)]
 
     hbm = lambda x: pltpu.with_memory_space_constraint(x, pltpu.HBM)
-    vmem = lambda x: pltpu.with_memory_space_constraint(x, pltpu.VMEM)
-
-    query_rows = call(
+
+    query_rows, mine = call(
         look_kernel,
-        array((2 * z_count, half, width), bf16),
+        (array((2 * z_count, half, width), bf16), array((levels + 1, beams), jnp.int32)),
         "look",
-        "vh",
+        "hhh",
         4,
-        scratch_shapes=[pltpu.VMEM(query_table.shape, bf16), dma((1,))],
-    )(codes, hbm(query_table))
+        scratch_shapes=[pltpu.VMEM(query_table.shape, bf16), dma((3,))],
+    )(hbm(codes), hbm(parents[None]), hbm(query_table))
     queries = lax.all_to_all(query_rows, ("pair", "z"), split_axis=0, concat_axis=0, tiled=True)
     residual = call(
         residual_kernel,
@@ -297,11 +312,8 @@
         scratch_shapes=[pltpu.VMEM(embed_table.shape, bf16), dma((1,))],
     )(codes, hbm(embed_table))
 
-    query_rows, mine, near_keys, near_values = lax.optimization_barrier(
-        (query_rows, jnp.concatenate([codes, parents[None]]), history_keys[0], history_values[0])
-    )
+    mine, near_keys, near_values = lax.optimization_barrier((mine, history_keys[0], history_values[0]))
     other = lax.ppermute(mine, "pair", swap)
-    other_parents = other[levels]
     far_keys = lax.ppermute(near_keys, "core", swap)
     far_values = lax.ppermute(near_values, "core", swap)
     kv_rows = call(
@@ -312,42 +324,38 @@
         4,
         scratch_shapes=[pltpu.VMEM(kv_table.shape, bf16), dma((1,))],
     )(pair.reshape(1), mine, other, hbm(kv_table))
-    far_kv = lax.ppermute(kv_rows, "core", swap)
-    gen_keys = jnp.where(first, kv_rows, far_kv)
-    gen_values = lax.ppermute(gen_keys, "z", [(i + z_count // 2, i) for i in range(z_count // 2)])
-    staged_keys, staged_values = call(
-        stage_kernel,
-        (pltpu.VMEM((KEY_HEADS, 2 * slots, HEAD), bf16), pltpu.VMEM((KEY_HEADS, CHUNK, 2 * slots), bf16)),
-        "stage",
-        "hhaa",
-        8,
-        scratch_shapes=[pltpu.VMEM((2, slots, KEY_HEADS * HEAD), bf16), dma((2 * KEY_HEADS,)), dma((2,))],
-        cost_estimate=pl.CostEstimate(flops=0, bytes_accessed=16 * MIB, transcendentals=0),
-    )(hbm(near_keys), hbm(near_values), far_keys, far_values)
-    staged_keys, staged_values = vmem(staged_keys), vmem(staged_values)
-
-    lower = jnp.where(first, parents, other_parents)
-    upper = jnp.where(first, other_parents, parents)
-    both = jnp.stack([lower, upper])
-    parent_rows = (both // beams) * half + both % beams
-    parent_lanes = jnp.concatenate([jnp.full((2, beams), -1, jnp.int32), parent_rows], axis=1)
-    parent_lanes = jnp.broadcast_to(parent_lanes[:, None, :], (2, 2, half)).reshape(1, 2 * rows)
+    at = lambda p, k, c: (p * z_count + k) * 2 + c
+    taken = [(p, k, c) for p in range(2) for k in range(z_count // 2) for c in range(2)]
+    gen_values = lax.ppermute(
+        kv_rows, ("pair", "z", "core"), [(at(p, k + z_count // 2, c ^ p), at(p, k, c)) for p, k, c in taken]
+    )
+    far_kv = lax.ppermute(kv_rows, ("pair", "z", "core"), [(at(1, k, 1 - c), at(1, k, c)) for p, k, c in taken if p])
 
     gen_head = jnp.where(z < z_count // 2, 2 * z + jnp.bitwise_xor(core, pair), -1)
-    meta = jnp.stack([lax.axis_index("grp"), pair * 2 * z_count + hist, gen_head]).astype(jnp.int32)
+    meta = jnp.stack([lax.axis_index("grp"), pair * 2 * z_count + hist, gen_head, pair]).astype(jnp.int32)
     partials = call(
         attend_kernel,
         array((2, z_count, CHUNK, 2 * half), bf16),
         "attend",
-        "sssvvvvvv",
-        16,
-        scratch_shapes=[pltpu.VMEM((2, 2 * slots, 2 * rows), f32)],
+        "sssvhhaavvvvv",
+        24,
+        scratch_shapes=[
+            pltpu.VMEM((2, 2 * slots, 2 * rows), f32),
+            pltpu.VMEM((KEY_HEADS, 2 * slots, HEAD), bf16),
+            pltpu.VMEM((KEY_HEADS, 2 * slots, HEAD), bf16),
+            dma((2 * KEY_HEADS,)),
+            dma((2 * KEY_HEADS,)),
+        ],
         cost_estimate=pl.CostEstimate(
             flops=4 * 4 * rows * KEY_HEADS * slots * HEAD,
             bytes_accessed=4 * slots * KEY_HEADS * HEAD,
             transcendentals=4 * rows * KEY_HEADS * slots,
         ),
-    )(meta, lengths, holders, queries, staged_keys, staged_values, gen_keys, gen_values, parent_lanes)
+    )(
+        *(meta, lengths, holders, queries),
+        *(hbm(near_keys), hbm(near_values), far_keys, far_values),
+        *(kv_rows, far_kv, gen_values, mine, other),
+    )
 
     shape = (2 * z_count, CHUNK, 2 * half)
     parts = lax.all_to_all(partials.reshape(shape), ("pair", "z"), split_axis=0, concat_axis=0, tiled=True)

time: 97.2 us -> 90 us (0.926)
  waiting for transfers between devices: 15.9 us -> 26.2 us
  Pallas kernels: 16.6 us -> 7.89 us
  local copies, waits for them, and re-layouts: 9.5 us -> 1.36 us
  starting transfers between devices: 32.4 us -> 33.8 us
  other arithmetic: 1.43 us -> 0.08 us
    ppermute x2, waiting for transfers between devices: 0.18 us -> 10.1 us  [the longest x1 10.1 us: shards(): lax.ppermute(kv_rows, ('pair', 'z', 'core'), [(at(p, k + z_count // 2, c...]
    unnamed x18 -> x8, local copies, waits for them, and re-layouts: 9.34 us -> 1.36 us
    pallas_call x1, Pallas kernels: 7.46 us -> 2.38 us  [shards(): call(attend_kernel, array((2, z_count, CHUNK, 2 * half), bf16), 'attend',...]
    all_to_all x1, starting transfers between devices: 8.48 us -> 13 us  [shards(): lax.all_to_all(partials.reshape(shape), ('pair', 'z'), split_axis=0, conc...]
    pallas_call x2 -> x1, Pallas kernels: 5.64 us -> 2.01 us  [shards(): call(look_kernel, (array((2 * z_count, half, width), bf16), array((levels...]
    ppermute x2, starting transfers between devices: 5.04 us -> 1.96 us  [the longest x1 1.29 us: shards(): lax.ppermute(kv_rows, ('pair', 'z', 'core'), [(at(p, k + z_count // 2, c...]
  transfers between devices with their start and end apart: 7 -> 7, of which waited for: 3 -> 3; matrix products, arithmetic and copies ran while one was open for 1% -> 0% of each run, Pallas kernels for 6% -> 2%
where the time goes in v6:
time: 90 us; the launch traced here: 88.8 us
  starting transfers between devices  33.8 us (38%)
  waiting for transfers between devices  26.2 us (29%)
  blocking collectives  19.2 us (21%)
  Pallas kernels  7.89 us (9%)
  local copies, waits for them, and re-layouts  1.36 us (2%)
    all_gather x1, blocking collectives, shards(): gathered = lax.all_gather(attention, ('z', 'core'), axis=0)  19.2 us
    all_to_all x1, waiting for transfers between devices, shards(): lax.all_to_all(partials.reshape(shape), ('pair', 'z'), split_axis=0, conc...  15 us
    all_to_all x1, starting transfers between devices, shards(): lax.all_to_all(partials.reshape(shape), ('pair', 'z'), split_axis=0, conc...  13 us
    all_to_all x1, starting transfers between devices, shards(): lax.all_to_all(query_rows, ('pair', 'z'), split_axis=0, concat_axis=0, ti...  11.1 us
    ppermute x1, waiting for transfers between devices, shards(): lax.ppermute(kv_rows, ('pair', 'z', 'core'), [(at(p, k + z_count // 2, c...  10.1 us
    ppermute x1, starting transfers between devices, shards(): other = lax.ppermute(mine, 'pair', swap)  3.27 us
    ppermute x1, starting transfers between devices, shards(): far_keys = lax.ppermute(near_keys, 'core', swap)  2.59 us
    pallas_call x1, Pallas kernels, shards(): call(attend_kernel, array((2, z_count, CHUNK, 2 * half), bf16), 'attend',...  2.38 us
  transfers between devices with their start and end apart: 7, of which 3 were waited for; matrix products, arithmetic and copies ran while one was open for 0% of the time, Pallas kernels for 2%

profile of v6, /device:TPU:57, one launch (start us, length us, event | category | flops | bytes accessed | tf_op | source)
XLA Modules:
  0.0 88.8 jit_solution(6737451564328909266)
XLA Ops:
  0.0 2.0 %look.1 = (bf16[16,64,256]{2,1,0:T(8,128)(2,1)}, s32[3,32]{1,0:T(4,128)S(1)}) custom-call(s32[2,32]{1,0:T(2,128)} %codes_ref.1, s32[1,32]{1,0:T(1,128)} %bitcast.17, bf16[2,256,256]{2,1,0:T(8,128)(2,1)} %query_hbm.1), custom_call_target="tpu_custom_call" | custom-call | tf_op jit(solution)/shard_map/look/pallas_call | solution.py:297
  2.0 2.6 %collective-permute-start = (bf16[1024,1024]{1,0:T(8,128)(2,1)}, bf16[1024,1024]{1,0:T(8,128)(2,1)S(1)}, u32[]{:S(2)}, u32[]{:S(2)}) collective-permute-start(bf16[1024,1024]{1,0:T(8,128)(2,1)} %bitcast.13), channel_id=1, source_target_pairs={{0,1},{1,0},{2,3},{3,2},{4,5},{5,4},{6,7},{7,6},{8,9},{9,8},{10,11... | collective-permute-start | bytes 6291464 | tf_op jit(solution)/shard_map/ppermute | solution.py:317
  4.6 1.9 %collective-permute-start.1 = (bf16[1024,1024]{1,0:T(8,128)(2,1)}, bf16[1024,1024]{1,0:T(8,128)(2,1)}, u32[]{:S(2)}, u32[]{:S(2)}) collective-permute-start(bf16[1024,1024]{1,0:T(8,128)(2,1)} %bitcast.15), channel_id=1, source_target_pairs={{0,1},{1,0},{2,3},{3,2},{4,5},{5,4},{6,7},{7,6},{8,9},{9,8},{10,11... | collective-permute-start | bytes 6291464 | tf_op jit(solution)/shard_map/ppermute | solution.py:318
  6.5 11.1 %all-to-all-start = ((bf16[16,64,256]{2,1,0:T(8,128)(2,1)}), bf16[16,64,256]{2,1,0:T(8,128)(2,1)S(1)}, u32[]{:S(2)}, u32[]{:S(2)}) async-start(bf16[16,64,256]{2,1,0:T(8,128)(2,1)} %get-tuple-element.10), calls=%async_computation | async-start | bytes 1048576 | tf_op jit(solution)/shard_map/all_to_all | solution.py:305
  17.6 3.3 %collective-permute-start.2 = (s32[3,32]{1,0:T(4,128)S(1)}, s32[3,32]{1,0:T(4,128)S(1)}, u32[]{:S(2)}, u32[]{:S(2)}) collective-permute-start(s32[3,32]{1,0:T(4,128)S(1)} %get-tuple-element.14.mine_ref), channel_id=1, source_target_pairs={{0,16},{16,0},{1,17},{17,1},{2,18},{18,2},{3,19},{19,3},{4,20},{20... | collective-permute-start | bytes 1160 | tf_op jit(solution)/shard_map/ppermute | solution.py:316
  20.9 1.1 %collective-permute-done.2.other_ref = s32[3,32]{1,0:T(4,128)S(1)} collective-permute-done((s32[3,32]{1,0:T(4,128)S(1)}, s32[3,32]{1,0:T(4,128)S(1)}, u32[]{:S(2)}, u32[]{:S(2)}) %collective-permute-start.2) | collective-permute-done | bytes 416 | tf_op jit(solution)/shard_map/ppermute | solution.py:316
  22.0 1.1 %generated.1.kv_ref = bf16[128,128]{1,0:T(8,128)(2,1)S(1)} custom-call(s32[1]{0:T(128)} %bitcast.3.pair_ref, s32[3,32]{1,0:T(4,128)S(1)} %get-tuple-element.14.mine_ref, s32[3,32]{1,0:T(4,128)S(1)} %collective-permute-done.2.other_ref, bf16[2,256,128]{2,1,0:T(8,128)(2,1)} %kv_hbm.1), custom_call_target="tpu_custom_call" | custom-call | tf_op jit(solution)/shard_map/generated/pallas_call | solution.py:319
  23.1 0.7 collective-permute-start.3
  23.8 1.3 %collective-permute-start.4 = (bf16[128,128]{1,0:T(8,128)(2,1)S(1)}, bf16[128,128]{1,0:T(8,128)(2,1)S(1)}, u32[]{:S(2)}, u32[]{:S(2)}) collective-permute-start(bf16[128,128]{1,0:T(8,128)(2,1)S(1)} %generated.1.kv_ref), channel_id=1, source_target_pairs={{8,0},{9,1},{10,2},{11,3},{12,4},{13,5},{14,6},{15,7},{25,16},{24,... | collective-permute-start | bytes 98312 | tf_op jit(solution)/shard_map/ppermute | solution.py:329
  25.1 0.0 copy-start.2
  25.1 0.1 pad_add_fusion.meta_ref
  25.2 0.0 collective-permute-done.3.far_kv_ref
  25.2 10.1 %collective-permute-done.4.gen_value_ref = bf16[128,128]{1,0:T(8,128)(2,1)S(1)} collective-permute-done((bf16[128,128]{1,0:T(8,128)(2,1)S(1)}, bf16[128,128]{1,0:T(8,128)(2,1)S(1)}, u32[]{:S(2)}, u32[]{:S(2)}) %collective-permute-start.4) | collective-permute-done | bytes 32800 | tf_op jit(solution)/shard_map/ppermute | solution.py:329
  35.3 0.0 all-to-all-done.query_ref
  35.3 0.0 collective-permute-done.far_key
  35.3 0.0 collective-permute-done.1.far_value
  35.3 0.0 copy-start.1
  35.3 0.7 copy-done.1
  36.0 0.0 copy-start.3
  36.0 0.7 copy-done.3
  36.7 2.4 %attend.1 = bf16[2,8,144,128]{3,2,1,0:T(8,128)(2,1)} custom-call(s32[4]{0:T(128)S(1)} %pad_add_fusion.meta_ref, s32[16]{0:T(128)S(1)} %copy-done.3, s32[16,32]{1,0:T(8,128)S(1)} %copy-done.1, bf16[16,64,256]{2,1,0:T(8,128)(2,1)S(1)} %all-to-all-done.query_ref, bf16[1024,1024]{1,0:T(8,128)(2,1)} %bitcast.14, bf16[1024,1024]{1,0:T(8,128)(2,1)} %bitcast.16, ...), custom_call_target="tpu_custom_call" | custom-call | flops 2147483648 | bytes 4194304 | tf_op jit(solution)/shard_map/attend/pallas_call | solution.py:336
  39.0 0.0 copy-start
  39.1 13.0 %all-to-all-start.1 = ((bf16[16,144,128]{2,1,0:T(8,128)(2,1)}), bf16[16,144,128]{2,1,0:T(8,128)(2,1)S(1)}, u32[]{:S(2)}, u32[]{:S(2)}) async-start(bf16[16,144,128]{2,1,0:T(8,128)(2,1)} %bitcast.7), calls=%async_computation.1 | async-start | bytes 1179648 | tf_op jit(solution)/shard_map/all_to_all | solution.py:361
  52.1 0.0 copy-done.2
  52.1 1.1 %residual.1.residual_ref = f32[64,256]{1,0:T(8,128)S(1)} custom-call(s32[2,32]{1,0:T(2,128)S(1)} %copy-done.2, bf16[2,256,256]{2,1,0:T(8,128)(2,1)} %embed_hbm.1), custom_call_target="tpu_custom_call" | custom-call | tf_op jit(solution)/shard_map/residual/pallas_call | solution.py:306
  53.2 15.0 %all-to-all-done.1.parts_ref = bf16[16,144,128]{2,1,0:T(8,128)(2,1)S(1)} async-done(((bf16[16,144,128]{2,1,0:T(8,128)(2,1)}), bf16[16,144,128]{2,1,0:T(8,128)(2,1)S(1)}, u32[]{:S(2)}, u32[]{:S(2)}) %all-to-all-start.1) | async-done | bytes 589856 | tf_op jit(solution)/shard_map/all_to_all | solution.py:361
  68.2 0.2 combine.1
  68.5 19.2 %all-gather = bf16[1024,256]{1,0:T(8,128)(2,1)S(1)} all-gather(bf16[64,256]{1,0:T(8,128)(2,1)S(1)} %combine.1), channel_id=2, replica_groups=mesh['grp'=16,'pair'=2,'z'=8,'core'=2] {'z','core'}, dimensions={0}, use_global_device_ids=true | all-gather | bytes 557056 | tf_op jit(solution)/shard_map/all_gather | solution.py:363
  87.7 0.0 copy-done
  87.7 1.1 %project.1 = bf16[64,256]{1,0:T(8,128)(2,1)} custom-call(bf16[16,64,256]{2,1,0:T(8,128)(2,1)S(1)} %bitcast.12, bf16[16,256,256]{2,1,0:T(8,128)(2,1)S(1)} %bitcast.11, f32[64,256]{1,0:T(8,128)S(1)} %residual.1.residual_ref), custom_call_target="tpu_custom_call" | custom-call | tf_op jit(solution)/shard_map/project/pallas_call | solution.py:364
Async XLA Ops:
  2.0 33.3 %collective-permute-start = (bf16[1024,1024]{1,0:T(8,128)(2,1)}, bf16[1024,1024]{1,0:T(8,128)(2,1)S(1)}, u32[]{:S(2)}, u32[]{:S(2)}) collective-permute-start(bf16[1024,1024]{1,0:T(8,128)(2,1)} %bitcast.13), channel_id=1, source_target_pairs={{0,1},{1,0},{2,3},{3,2},{4,5},{5,4},{6,7},{7,6},{8,9},{9,8},{10,11... | collective-permute-start | bytes 6291464 | tf_op jit(solution)/shard_map/ppermute | solution.py:317
  4.6 30.7 %collective-permute-start.1 = (bf16[1024,1024]{1,0:T(8,128)(2,1)}, bf16[1024,1024]{1,0:T(8,128)(2,1)}, u32[]{:S(2)}, u32[]{:S(2)}) collective-permute-start(bf16[1024,1024]{1,0:T(8,128)(2,1)} %bitcast.15), channel_id=1, source_target_pairs={{0,1},{1,0},{2,3},{3,2},{4,5},{5,4},{6,7},{7,6},{8,9},{9,8},{10,11... | collective-permute-start | bytes 6291464 | tf_op jit(solution)/shard_map/ppermute | solution.py:318
  6.5 28.7 %all-to-all-start = ((bf16[16,64,256]{2,1,0:T(8,128)(2,1)}), bf16[16,64,256]{2,1,0:T(8,128)(2,1)S(1)}, u32[]{:S(2)}, u32[]{:S(2)}) async-start(bf16[16,64,256]{2,1,0:T(8,128)(2,1)} %get-tuple-element.10), calls=%async_computation | async-start | bytes 1048576 | tf_op jit(solution)/shard_map/all_to_all | solution.py:305
  17.6 4.4 %collective-permute-start.2 = (s32[3,32]{1,0:T(4,128)S(1)}, s32[3,32]{1,0:T(4,128)S(1)}, u32[]{:S(2)}, u32[]{:S(2)}) collective-permute-start(s32[3,32]{1,0:T(4,128)S(1)} %get-tuple-element.14.mine_ref), channel_id=1, source_target_pairs={{0,16},{16,0},{1,17},{17,1},{2,18},{18,2},{3,19},{19,3},{4,20},{20... | collective-permute-start | bytes 1160 | tf_op jit(solution)/shard_map/ppermute | solution.py:316
  23.1 2.1 %collective-permute-start.3 = (bf16[128,128]{1,0:T(8,128)(2,1)S(1)}, bf16[128,128]{1,0:T(8,128)(2,1)S(1)}, u32[]{:S(2)}, u32[]{:S(2)}) collective-permute-start(bf16[128,128]{1,0:T(8,128)(2,1)S(1)} %generated.1.kv_ref), channel_id=1, source_target_pairs={{17,16},{16,17},{19,18},{18,19},{21,20},{20,21},{23,22},{22,23},{4... | collective-permute-start | bytes 98312 | tf_op jit(solution)/shard_map/ppermute | solution.py:332
  23.8 11.5 %collective-permute-start.4 = (bf16[128,128]{1,0:T(8,128)(2,1)S(1)}, bf16[128,128]{1,0:T(8,128)(2,1)S(1)}, u32[]{:S(2)}, u32[]{:S(2)}) collective-permute-start(bf16[128,128]{1,0:T(8,128)(2,1)S(1)} %generated.1.kv_ref), channel_id=1, source_target_pairs={{8,0},{9,1},{10,2},{11,3},{12,4},{13,5},{14,6},{15,7},{25,16},{24,... | collective-permute-start | bytes 98312 | tf_op jit(solution)/shard_map/ppermute | solution.py:329
  25.1 27.0 %copy-start.2 = (s32[2,32]{1,0:T(2,128)S(1)}, s32[2,32]{1,0:T(2,128)}, u32[]{:S(2)}) copy-start(s32[2,32]{1,0:T(2,128)} %codes_ref.1) | copy-start | bytes 772
  35.3 0.7 copy-start.1
  36.0 0.7 copy-start.3
  39.0 48.7 %copy-start = (bf16[4096,256]{1,0:T(8,128)(2,1)S(1)}, bf16[4096,256]{1,0:T(8,128)(2,1)}, u32[]{:S(2)}) copy-start(bf16[4096,256]{1,0:T(8,128)(2,1)} %param.19) | copy-start | bytes 6291460
  39.1 29.2 %all-to-all-start.1 = ((bf16[16,144,128]{2,1,0:T(8,128)(2,1)}), bf16[16,144,128]{2,1,0:T(8,128)(2,1)S(1)}, u32[]{:S(2)}, u32[]{:S(2)}) async-start(bf16[16,144,128]{2,1,0:T(8,128)(2,1)} %bitcast.7), calls=%async_computation.1 | async-start | bytes 1179648 | tf_op jit(solution)/shard_map/all_to_all | solution.py:361

commit v7 on v6

--- a/solution.py
+++ b/solution.py
@@ -58,20 +58,36 @@
             out_ref[target, level * beams : (level + 1) * beams] = found
 
 
-def generated_kernel(pair_ref, mine_ref, other_ref, kv_hbm, out_ref, kv_ref, sem):
-    copy = pltpu.make_async_copy(kv_hbm, kv_ref, sem.at[0])
-    copy.start()
+def generated_kernel(
+    meta_ref, mine_ref, other_ref, kv_hbm, lengths_hbm, holders_hbm, out_ref, live_ref, kv_ref, lengths_ref, holders_ref, sem
+):
+    copies = [
+        pltpu.make_async_copy(lengths_hbm, lengths_ref, sem.at[0]),
+        pltpu.make_async_copy(holders_hbm, holders_ref, sem.at[1]),
+        pltpu.make_async_copy(kv_hbm, kv_ref, sem.at[2]),
+    ]
+    for copy in copies:
+        copy.start()
     levels, beams = kv_ref.shape[0], mine_ref.shape[1]
     hots = [
         jnp.concatenate([one_hot_rows(ref[level : level + 1], kv_ref.shape[1]) for ref in (mine_ref, other_ref)])
         for level in range(levels)
     ]
-    copy.wait()
+    for copy in copies:
+        copy.wait()
     for level, hot in enumerate(hots):
         found = jnp.dot(hot, kv_ref[level], preferred_element_type=jnp.float32).astype(jnp.bfloat16)
-        for part, x in enumerate((pair_ref[0], 1 - pair_ref[0])):
+        for part, x in enumerate((meta_ref[3], 1 - meta_ref[3])):
             place = pl.ds(pl.multiple_of((x * levels + level) * beams, beams), beams)
             out_ref[place] = found[part * beams : (part + 1) * beams]
+    request, place, block_slots = meta_ref[0], meta_ref[1], meta_ref[4]
+    near, far = jnp.int32(0), jnp.int32(0)
+    for block in range(holders_ref.shape[1]):
+        holder = holders_ref[request, block]
+        near = jnp.where(holder == place, block, near)
+        far = jnp.where(holder == jnp.bitwise_xor(place, 1), block, far)
+    for at, position in enumerate((near, far)):
+        live_ref[at] = jnp.clip(lengths_ref[request] - position * block_slots, 0, block_slots)
 
 
 def split3(value):
@@ -102,38 +118,30 @@
     return jnp.concatenate([jnp.transpose(values), jnp.ones((STAT, values.shape[0]), jnp.bfloat16)], axis=0)
 
 
+def queries_of(query_ref, head):
+    pieces = []
+    for x in range(2):
+        pair = query_ref[x * KEY_HEADS + head]
+        pieces += [pair[:, h * HEAD : (h + 1) * HEAD] for h in range(2)]
+    return jnp.concatenate(pieces, axis=0)
+
+
+def write(out_ref, head, sums, total, top):
+    width = sums.shape[1] // 2
+    for x in range(2):
+        lanes = slice(x * width, (x + 1) * width)
+        out_ref[x, head, 0:HEAD] = sums[:, lanes].astype(jnp.bfloat16)
+        out_ref[x, head, HEAD:CHUNK] = stat_rows(top[:, lanes], total[:, lanes])
+
+
 def attend_kernel(
-    meta_ref, lengths_ref, holders_ref, query_ref, near_key, near_value, far_key, far_value, kv_ref, far_kv_ref,
-    gen_value_ref, mine_ref, other_ref, out_ref, score_ref, key_ref, value_ref, key_sem, value_sem,
+    live_ref, query_ref, near_key, near_value, far_key, far_value, out_ref, score_ref, key_ref, value_ref, key_sem, value_sem
 ):
     heads, slots = key_ref.shape[0], key_ref.shape[1]
     half = query_ref.shape[1]
-    width = 4 * half
-    request, place, gen_head = meta_ref[0], meta_ref[1], meta_ref[2]
-
     block_slots = slots // 2
-    near, far = jnp.int32(0), jnp.int32(0)
-    for block in range(holders_ref.shape[1]):
-        holder = holders_ref[request, block]
-        near = jnp.where(holder == place, block, near)
-        far = jnp.where(holder == jnp.bitwise_xor(place, 1), block, far)
-    near_live, far_live = (
-        jnp.clip(lengths_ref[request] - each * block_slots, 0, block_slots) for each in (near, far)
-    )
+    near_live, far_live = live_ref[0], live_ref[1]
     live = near_live + far_live
-
-    def queries(head):
-        pieces = []
-        for x in range(2):
-            pair = query_ref[x * heads + head]
-            pieces += [pair[:, h * HEAD : (h + 1) * HEAD] for h in range(2)]
-        return jnp.concatenate(pieces, axis=0)
-
-    def write(head, sums, total, top):
-        for x in range(2):
-            lanes = slice(x * 2 * half, (x + 1) * 2 * half)
-            out_ref[x, head, 0:HEAD] = sums[:, lanes].astype(jnp.bfloat16)
-            out_ref[x, head, HEAD:CHUNK] = stat_rows(top[:, lanes], total[:, lanes])
 
     def copies(head, keys):
         sources, target, sem = ((near_key, far_key), key_ref, key_sem) if keys else ((near_value, far_value), value_ref, value_sem)
@@ -159,7 +167,7 @@
         lax.fori_loop(0, heads, begin, 0)
 
         def score(head, at):
-            scores = scores_of(key_ref[head], queries(head))
+            scores = scores_of(key_ref[head], queries_of(query_ref, head))
             if masked:
                 slot = lax.broadcasted_iota(jnp.int32, (slots, 1), 0)
                 allowed = (slot < near_live) | ((slot >= block_slots) & (slot < block_slots + far_live))
@@ -170,7 +178,7 @@
         def finish(head, at, top):
             weights = jnp.exp2((score_ref[at] - top) * EXP2_SCALE).astype(jnp.bfloat16)
             sums = jnp.dot(extended(value_ref[head]), weights, preferred_element_type=jnp.float32)
-            write(head, sums[0:HEAD], sums[HEAD : HEAD + 1], top)
+            write(out_ref, head, sums[0:HEAD], sums[HEAD : HEAD + 1], top)
 
         def step(i, top):
             wait(2 * i + 1, True)
@@ -212,7 +220,15 @@
             for head in range(heads):
                 out_ref[x, head] = dead
 
-    @pl.when(gen_head >= 0)
+
+def add_generated_kernel(
+    meta_ref, query_ref, kv_ref, far_kv_ref, gen_value_ref, mine_ref, other_ref, before_ref, out_ref
+):
+    half = query_ref.shape[1]
+    width = 4 * half
+    head = meta_ref[2]
+
+    @pl.when(head >= 0)
     def _():
         values = extended(gen_value_ref[...])
         row = lax.broadcasted_iota(jnp.int32, (2 * half, width), 0)
@@ -227,8 +243,8 @@
             pieces += [jnp.full_like(parents, -1), parents] * 2
         allowed = (row == own) | (row == jnp.concatenate(pieces, axis=1))
         keys = jnp.where(swapped, far_kv_ref[...], kv_ref[...])
-        scores = jnp.where(allowed, scores_of(keys, queries(gen_head)), DEAD)
-        before = jnp.concatenate([out_ref[x, gen_head] for x in range(2)], axis=1)
+        scores = jnp.where(allowed, scores_of(keys, queries_of(query_ref, head)), DEAD)
+        before = jnp.concatenate([before_ref[x, head] for x in range(2)], axis=1)
         old_top, old_total = read_stats(before[HEAD:CHUNK])
         top = jnp.maximum(old_top, jnp.max(scores, axis=0, keepdims=True))
         weights = jnp.where(allowed, jnp.exp2((scores - top) * EXP2_SCALE), 0.0)
@@ -238,7 +254,7 @@
         added = added + jnp.dot(values, low, preferred_element_type=jnp.float32)
         factor = jnp.exp2((old_top - top) * EXP2_SCALE)
         sums = before[0:HEAD].astype(jnp.float32) * factor + added[0:HEAD]
-        write(gen_head, sums, old_total * factor + added[HEAD : HEAD + 1], top)
+        write(out_ref, head, sums, old_total * factor + added[HEAD : HEAD + 1], top)
 
 
 def combine_kernel(parts_ref, out_ref):
@@ -252,24 +268,28 @@
         total = total + stats[part][1] * factor
         sums = sums + parts_ref[part, 0:HEAD].astype(jnp.float32) * factor
     tall = jnp.transpose(sums / total)
-    rows = out_ref.shape[0]
-    out_ref[...] = jnp.concatenate([tall[0:rows], tall[rows : 2 * rows]], axis=1).astype(jnp.bfloat16)
-
-
-def project_kernel(rows_ref, weight_ref, residual_ref, out_ref):
-    total = residual_ref[...]
+    rows = out_ref.shape[1]
+    found = jnp.concatenate([tall[0:rows], tall[rows : 2 * rows]], axis=1).astype(jnp.bfloat16)
+    for target in range(out_ref.shape[0]):
+        out_ref[target] = found
+
+
+def project_kernel(flip, meta_ref, rows_ref, weight_ref, before_ref, out_ref):
+    total = before_ref[...]
+    parity = jnp.bitwise_xor(jnp.bitwise_and(meta_ref[1], 1), flip)
     for part in range(rows_ref.shape[0]):
-        total = total + jnp.dot(rows_ref[part], weight_ref[part], preferred_element_type=jnp.float32)
+        total = total + jnp.dot(rows_ref[part], weight_ref[part, parity], preferred_element_type=jnp.float32)
     out_ref[...] = total.astype(out_ref.dtype)
 
 
-def call(kernel, out_shape, name, spaces, vmem, **rest):
+def call(kernel, out_shape, name, spaces, vmem, out_spaces="v", **rest):
     kinds = {"s": pltpu.SMEM, "v": pltpu.VMEM, "h": pltpu.HBM, "a": pl.ANY}
+    specs = lambda letters: [pl.BlockSpec(memory_space=kinds[letter]) for letter in letters]
     return pl.pallas_call(
         kernel,
         out_shape=out_shape,
-        in_specs=[pl.BlockSpec(memory_space=kinds[space]) for space in spaces],
-        out_specs=jax.tree.map(lambda _: pl.BlockSpec(memory_space=pltpu.VMEM), out_shape),
+        in_specs=specs(spaces),
+        out_specs=specs(out_spaces) if len(out_spaces) > 1 else specs(out_spaces)[0],
         compiler_params=pltpu.CompilerParams(vmem_limit_bytes=vmem * MIB),
         name=name,
         **rest,
@@ -300,6 +320,7 @@
         "look",
         "hhh",
         4,
+        "vv",
         scratch_shapes=[pltpu.VMEM(query_table.shape, bf16), dma((3,))],
     )(hbm(codes), hbm(parents[None]), hbm(query_table))
     queries = lax.all_to_all(query_rows, ("pair", "z"), split_axis=0, concat_axis=0, tiled=True)
@@ -316,14 +337,22 @@
     other = lax.ppermute(mine, "pair", swap)
     far_keys = lax.ppermute(near_keys, "core", swap)
     far_values = lax.ppermute(near_values, "core", swap)
-    kv_rows = call(
+    gen_head = jnp.where(z < z_count // 2, 2 * z + jnp.bitwise_xor(core, pair), -1)
+    meta = jnp.stack([lax.axis_index("grp"), pair * 2 * z_count + hist, gen_head, pair, jnp.int32(slots)]).astype(jnp.int32)
+    kv_rows, live = call(
         generated_kernel,
-        array((rows, HEAD), bf16),
+        (array((rows, HEAD), bf16), array((2,), jnp.int32)),
         "generated",
-        "svvh",
+        "svvhhh",
         4,
-        scratch_shapes=[pltpu.VMEM(kv_table.shape, bf16), dma((1,))],
-    )(pair.reshape(1), mine, other, hbm(kv_table))
+        "vs",
+        scratch_shapes=[
+            pltpu.VMEM(kv_table.shape, bf16),
+            pltpu.SMEM(lengths.shape, jnp.int32),
+            pltpu.SMEM(holders.shape, jnp.int32),
+            dma((3,)),
+        ],
+    )(meta, mine, other, hbm(kv_table), hbm(lengths), hbm(holders))
     at = lambda p, k, c: (p * z_count + k) * 2 + c
     taken = [(p, k, c) for p in range(2) for k in range(z_count // 2) for c in range(2)]
     gen_values = lax.ppermute(
@@ -331,13 +360,12 @@
     )
     far_kv = lax.ppermute(kv_rows, ("pair", "z", "core"), [(at(1, k, 1 - c), at(1, k, c)) for p, k, c in taken if p])
 
-    gen_head = jnp.where(z < z_count // 2, 2 * z + jnp.bitwise_xor(core, pair), -1)
-    meta = jnp.stack([lax.axis_index("grp"), pair * 2 * z_count + hist, gen_head, pair]).astype(jnp.int32)
+    partial_shape = (2, z_count, CHUNK, 2 * half)
     partials = call(
         attend_kernel,
-        array((2, z_count, CHUNK, 2 * half), bf16),
+        array(partial_shape, bf16),
         "attend",
-        "sssvhhaavvvvv",
+        "svhhaa",
         24,
         scratch_shapes=[
             pltpu.VMEM((2, 2 * slots, 2 * rows), f32),
@@ -351,18 +379,22 @@
             bytes_accessed=4 * slots * KEY_HEADS * HEAD,
             transcendentals=4 * rows * KEY_HEADS * slots,
         ),
-    )(
-        *(meta, lengths, holders, queries),
-        *(hbm(near_keys), hbm(near_values), far_keys, far_values),
-        *(kv_rows, far_kv, gen_values, mine, other),
-    )
+    )(live, queries, hbm(near_keys), hbm(near_values), far_keys, far_values)
+    partials = call(
+        add_generated_kernel, array(partial_shape, bf16), "add_generated", "svvvvvvv", 4, input_output_aliases={7: 0}
+    )(meta, queries, kv_rows, far_kv, gen_values, mine, other, partials)
 
     shape = (2 * z_count, CHUNK, 2 * half)
     parts = lax.all_to_all(partials.reshape(shape), ("pair", "z"), split_axis=0, concat_axis=0, tiled=True)
-    attention = call(combine_kernel, array((half, width), bf16), "combine", "v", 4)(parts)
-    gathered = lax.all_gather(attention, ("z", "core"), axis=0)
-    out = call(project_kernel, array((half, width), bf16), "project", "vvv", 4)(
-        gathered, out_weight.reshape(2 * z_count, width, width), residual
+    attention = call(combine_kernel, array((z_count, half, width), bf16), "combine", "v", 4)(parts)
+    near_rows = lax.all_to_all(attention, "z", split_axis=0, concat_axis=0, tiled=True)
+    far_rows = lax.ppermute(near_rows, "core", swap)
+    weight = out_weight.reshape(z_count, 2, width, width)
+    begun = call(functools.partial(project_kernel, 0), array((half, width), f32), "project_near", "svvv", 4)(
+        meta, near_rows, weight, residual
+    )
+    out = call(functools.partial(project_kernel, 1), array((half, width), bf16), "project_far", "svvv", 4)(
+        meta, far_rows, weight, begun
     )
     return out.reshape(levels, beams, width)
 

time: 90 us -> 85.7 us (0.952)
  waiting for transfers between devices: 26.2 us -> 5.77 us
  blocking collectives: 19.2 us -> 37.7 us
  starting transfers between devices: 33.8 us -> 25.4 us
  Pallas kernels: 7.89 us -> 16.1 us
  local copies, waits for them, and re-layouts: 1.36 us -> 0.1 us
    all_to_all x0 -> x2, blocking collectives: none -> 37.7 us  [the longest x1 23.7 us: shards(): lax.all_to_all(partials.reshape(shape), ('pair', 'z'), split_axis=0, conc...]
    all_gather x1 -> x0, blocking collectives: 19.2 us -> none  [shards(): gathered = lax.all_gather(attention, ('z', 'core'), axis=0)]
    all_to_all x1 -> x0, waiting for transfers between devices: 15 us -> none  [shards(): lax.all_to_all(partials.reshape(shape), ('pair', 'z'), split_axis=0, conc...]
    all_to_all x1 -> x0, starting transfers between devices: 13 us -> none  [shards(): lax.all_to_all(partials.reshape(shape), ('pair', 'z'), split_axis=0, conc...]
    ppermute x1, waiting for transfers between devices: 10.1 us -> 0.01 us  [shards(): lax.ppermute(kv_rows, ('pair', 'z', 'core'), [(at(p, k + z_count // 2, c...]
    pallas_call x4 -> x6, Pallas kernels: 4.76 us -> 12.9 us  [the longest x1 7.31 us: shards(): call(attend_kernel, array(partial_shape, bf16), 'attend', 'svhhaa', 24, s...]
    all_to_all x1, waiting for transfers between devices: 0.01 us -> 4.73 us  [shards(): lax.all_to_all(query_rows, ('pair', 'z'), split_axis=0, concat_axis=0, ti...]
    ppermute x0 -> x1, starting transfers between devices: none -> 4.56 us  [shards(): far_rows = lax.ppermute(near_rows, 'core', swap)]
  transfers between devices with their start and end apart: 7 -> 7, of which waited for: 3 -> 2; matrix products, arithmetic and copies ran while one was open for 0% -> 0% of each run, Pallas kernels for 2% -> 13%
where the time goes in v7:
time: 85.7 us; the launch traced here: 85.2 us
  blocking collectives  37.7 us (44%)
  starting transfers between devices  25.4 us (30%)
  Pallas kernels  16.1 us (19%)
  waiting for transfers between devices  5.77 us (7%)
    all_to_all x1, blocking collectives, shards(): lax.all_to_all(partials.reshape(shape), ('pair', 'z'), split_axis=0, conc...  23.7 us
    all_to_all x1, blocking collectives, shards(): lax.all_to_all(attention, 'z', split_axis=0, concat_axis=0, tiled=True)  14 us
    all_to_all x1, starting transfers between devices, shards(): lax.all_to_all(query_rows, ('pair', 'z'), split_axis=0, concat_axis=0, ti...  11.1 us
    pallas_call x1, Pallas kernels, shards(): call(attend_kernel, array(partial_shape, bf16), 'attend', 'svhhaa', 24, s...  7.31 us
    all_to_all x1, waiting for transfers between devices, shards(): lax.all_to_all(query_rows, ('pair', 'z'), split_axis=0, concat_axis=0, ti...  4.73 us
    ppermute x1, starting transfers between devices, shards(): far_rows = lax.ppermute(near_rows, 'core', swap)  4.56 us
    ppermute x1, starting transfers between devices, shards(): other = lax.ppermute(mine, 'pair', swap)  3.27 us
    ppermute x1, starting transfers between devices, shards(): far_keys = lax.ppermute(near_keys, 'core', swap)  2.59 us
  transfers between devices with their start and end apart: 7, of which 2 were waited for; matrix products, arithmetic and copies ran while one was open for 0% of the time, Pallas kernels for 13%

profile of v7, /device:TPU:57, one launch (start us, length us, event | category | flops | bytes accessed | tf_op | source)
XLA Modules:
  0.0 85.2 jit_solution(9364878359189014300)
XLA Ops:
  0.0 2.0 %look.1 = (bf16[16,64,256]{2,1,0:T(8,128)(2,1)}, s32[3,32]{1,0:T(4,128)S(1)}) custom-call(s32[2,32]{1,0:T(2,128)} %codes_ref.1, s32[1,32]{1,0:T(1,128)} %bitcast.17, bf16[2,256,256]{2,1,0:T(8,128)(2,1)} %query_hbm.1), custom_call_target="tpu_custom_call" | custom-call | tf_op jit(solution)/shard_map/look/pallas_call | solution.py:317
  2.0 2.6 %collective-permute-start.3 = (bf16[1024,1024]{1,0:T(8,128)(2,1)}, bf16[1024,1024]{1,0:T(8,128)(2,1)S(1)}, u32[]{:S(2)}, u32[]{:S(2)}) collective-permute-start(bf16[1024,1024]{1,0:T(8,128)(2,1)} %bitcast.13), channel_id=1, source_target_pairs={{0,1},{1,0},{2,3},{3,2},{4,5},{5,4},{6,7},{7,6},{8,9},{9,8},{10,11... | collective-permute-start | bytes 6291464 | tf_op jit(solution)/shard_map/ppermute | solution.py:338
  4.6 1.9 %collective-permute-start.4 = (bf16[1024,1024]{1,0:T(8,128)(2,1)}, bf16[1024,1024]{1,0:T(8,128)(2,1)}, u32[]{:S(2)}, u32[]{:S(2)}) collective-permute-start(bf16[1024,1024]{1,0:T(8,128)(2,1)} %bitcast.15), channel_id=1, source_target_pairs={{0,1},{1,0},{2,3},{3,2},{4,5},{5,4},{6,7},{7,6},{8,9},{9,8},{10,11... | collective-permute-start | bytes 6291464 | tf_op jit(solution)/shard_map/ppermute | solution.py:339
  6.5 11.1 %all-to-all-start = ((bf16[16,64,256]{2,1,0:T(8,128)(2,1)}), bf16[16,64,256]{2,1,0:T(8,128)(2,1)S(1)}, u32[]{:S(2)}, u32[]{:S(2)}) async-start(bf16[16,64,256]{2,1,0:T(8,128)(2,1)} %get-tuple-element.12), calls=%async_computation | async-start | bytes 1048576 | tf_op jit(solution)/shard_map/all_to_all | solution.py:326
  17.6 3.3 %collective-permute-start = (s32[3,32]{1,0:T(4,128)S(1)}, s32[3,32]{1,0:T(4,128)S(1)}, u32[]{:S(2)}, u32[]{:S(2)}) collective-permute-start(s32[3,32]{1,0:T(4,128)S(1)} %get-tuple-element.14.mine_ref), channel_id=1, source_target_pairs={{0,16},{16,0},{1,17},{17,1},{2,18},{18,2},{3,19},{19,3},{4,20},{20... | collective-permute-start | bytes 1160 | tf_op jit(solution)/shard_map/ppermute | solution.py:337
  20.9 0.1 stack.19.meta_ref
  21.0 1.0 %collective-permute-done.other_ref = s32[3,32]{1,0:T(4,128)S(1)} collective-permute-done((s32[3,32]{1,0:T(4,128)S(1)}, s32[3,32]{1,0:T(4,128)S(1)}, u32[]{:S(2)}, u32[]{:S(2)}) %collective-permute-start) | collective-permute-done | bytes 416 | tf_op jit(solution)/shard_map/ppermute | solution.py:337
  22.0 2.1 %generated.1 = (bf16[128,128]{1,0:T(8,128)(2,1)S(1)}, s32[2]{0:T(128)S(1)}) custom-call(s32[5]{0:T(128)S(1)} %stack.19.meta_ref, s32[3,32]{1,0:T(4,128)S(1)} %get-tuple-element.14.mine_ref, s32[3,32]{1,0:T(4,128)S(1)} %collective-permute-done.other_ref, bf16[2,256,128]{2,1,0:T(8,128)(2,1)} %kv_hbm.1, s32[16]{0:T(128)} %lengths_hbm.1, s32[16,32]{1,0:T(8,128)} %holders_hbm.1), custom_call_target="tpu_custom_call" | custom-call | tf_op jit(solution)/shard_map/generated/pallas_call | solution.py:342
  24.2 0.7 collective-permute-start.1
  24.8 1.3 %collective-permute-start.2 = (bf16[128,128]{1,0:T(8,128)(2,1)S(1)}, bf16[128,128]{1,0:T(8,128)(2,1)S(1)}, u32[]{:S(2)}, u32[]{:S(2)}) collective-permute-start(bf16[128,128]{1,0:T(8,128)(2,1)S(1)} %get-tuple-element.15.kv_ref), channel_id=1, source_target_pairs={{8,0},{9,1},{10,2},{11,3},{12,4},{13,5},{14,6},{15,7},{25,16},{24,... | collective-permute-start | bytes 98312 | tf_op jit(solution)/shard_map/ppermute | solution.py:358
  26.1 4.7 %all-to-all-done.query_ref = bf16[16,64,256]{2,1,0:T(8,128)(2,1)S(1)} async-done(((bf16[16,64,256]{2,1,0:T(8,128)(2,1)}), bf16[16,64,256]{2,1,0:T(8,128)(2,1)S(1)}, u32[]{:S(2)}, u32[]{:S(2)}) %all-to-all-start) | async-done | bytes 524320 | tf_op jit(solution)/shard_map/all_to_all | solution.py:326
  30.9 0.0 collective-permute-done.3.far_key
  30.9 0.0 collective-permute-done.4.far_value
  30.9 7.3 %attend.1.before_ref = bf16[2,8,144,128]{3,2,1,0:T(8,128)(2,1)S(1)} custom-call(s32[2]{0:T(128)S(1)} %get-tuple-element.16.live_ref, bf16[16,64,256]{2,1,0:T(8,128)(2,1)S(1)} %all-to-all-done.query_ref, bf16[1024,1024]{1,0:T(8,128)(2,1)} %bitcast.14, bf16[1024,1024]{1,0:T(8,128)(2,1)} %bitcast.16, bf16[1024,1024]{1,0:T(8,128)(2,1)S(1)} %collective-permute-done.3.far_key, ...), custom_call_target="tpu_custom_call" | custom-call | flops 2147483648 | bytes 4194304 | tf_op jit(solution)/shard_map/attend/pallas_call | solution.py:364
  38.2 0.0 copy-start.1
  38.2 0.0 copy-start
  38.2 0.0 collective-permute-done.1.far_kv_ref
  38.2 0.0 collective-permute-done.2.gen_value_ref
  38.2 1.0 %add_generated.1 = bf16[2,8,144,128]{3,2,1,0:T(8,128)(2,1)S(1)} custom-call(s32[5]{0:T(128)S(1)} %stack.19.meta_ref, bf16[16,64,256]{2,1,0:T(8,128)(2,1)S(1)} %all-to-all-done.query_ref, bf16[128,128]{1,0:T(8,128)(2,1)S(1)} %get-tuple-element.15.kv_ref, bf16[128,128]{1,0:T(8,128)(2,1)S(1)} %collective-permute-done.1.far_kv_ref, ...), custom_call_target="tpu_custom_call", output_to_operand_aliasing={{}: (7, {})} | custom-call | tf_op jit(solution)/shard_map/add_generated/pallas_call | solution.py:383
  39.2 23.7 %all_to_all.15.parts_ref = bf16[16,144,128]{2,1,0:T(8,128)(2,1)S(1)} all-to-all(bf16[16,144,128]{2,1,0:T(8,128)(2,1)S(1)} %bitcast.12), channel_id=1, replica_groups=mesh['grp'=16,'pair'=2,'z'=8,'core'=2] {'pair','z'}, dimensions={0} | all-to-all | bytes 1179648 | tf_op jit(solution)/shard_map/all_to_all | solution.py:388
  62.9 0.2 combine.1
  63.2 14.0 %all_to_all.16.rows_ref = bf16[8,64,256]{2,1,0:T(8,128)(2,1)S(1)} all-to-all(bf16[8,64,256]{2,1,0:T(8,128)(2,1)S(1)} %combine.1), channel_id=1, replica_groups=mesh['grp'=16,'pair'=2,'z'=8,'core'=2] {'z'}, dimensions={0} | all-to-all | bytes 524288 | tf_op jit(solution)/shard_map/all_to_all | solution.py:390
  77.2 4.6 %collective-permute-start.5 = (bf16[8,64,256]{2,1,0:T(8,128)(2,1)S(1)}, bf16[8,64,256]{2,1,0:T(8,128)(2,1)S(1)}, u32[]{:S(2)}, u32[]{:S(2)}) collective-permute-start(bf16[8,64,256]{2,1,0:T(8,128)(2,1)S(1)} %all_to_all.16.rows_ref), channel_id=1, source_target_pairs={{0,1},{1,0},{2,3},{3,2},{4,5},{5,4},{6,7},{7,6},{8,9},{9,8},{10,11... | collective-permute-start | bytes 786440 | tf_op jit(solution)/shard_map/ppermute | solution.py:391
  81.8 0.0 copy-done.1
  81.8 1.1 %residual.1.before_ref = f32[64,256]{1,0:T(8,128)S(1)} custom-call(s32[2,32]{1,0:T(2,128)S(1)} %copy-done.1, bf16[2,256,256]{2,1,0:T(8,128)(2,1)} %embed_hbm.1), custom_call_target="tpu_custom_call" | custom-call | tf_op jit(solution)/shard_map/residual/pallas_call | solution.py:327
  82.9 0.0 copy-done
  82.9 0.9 project_near.1.before_ref
  83.8 0.0 collective-permute-done.5.rows_ref
  83.8 1.5 %project_far.1 = bf16[64,256]{1,0:T(8,128)(2,1)} custom-call(s32[5]{0:T(128)S(1)} %stack.19.meta_ref, bf16[8,64,256]{2,1,0:T(8,128)(2,1)S(1)} %collective-permute-done.5.rows_ref, bf16[8,2,256,256]{3,2,1,0:T(8,128)(2,1)S(1)} %bitcast.11, f32[64,256]{1,0:T(8,128)S(1)} %project_near.1.before_ref), custom_call_target="tpu_custom_call" | custom-call | tf_op jit(solution)/shard_map/project_far/pallas_call | solution.py:396
Async XLA Ops:
  2.0 28.9 %collective-permute-start.3 = (bf16[1024,1024]{1,0:T(8,128)(2,1)}, bf16[1024,1024]{1,0:T(8,128)(2,1)S(1)}, u32[]{:S(2)}, u32[]{:S(2)}) collective-permute-start(bf16[1024,1024]{1,0:T(8,128)(2,1)} %bitcast.13), channel_id=1, source_target_pairs={{0,1},{1,0},{2,3},{3,2},{4,5},{5,4},{6,7},{7,6},{8,9},{9,8},{10,11... | collective-permute-start | bytes 6291464 | tf_op jit(solution)/shard_map/ppermute | solution.py:338
  4.6 26.3 %collective-permute-start.4 = (bf16[1024,1024]{1,0:T(8,128)(2,1)}, bf16[1024,1024]{1,0:T(8,128)(2,1)}, u32[]{:S(2)}, u32[]{:S(2)}) collective-permute-start(bf16[1024,1024]{1,0:T(8,128)(2,1)} %bitcast.15), channel_id=1, source_target_pairs={{0,1},{1,0},{2,3},{3,2},{4,5},{5,4},{6,7},{7,6},{8,9},{9,8},{10,11... | collective-permute-start | bytes 6291464 | tf_op jit(solution)/shard_map/ppermute | solution.py:339
  6.5 24.3 %all-to-all-start = ((bf16[16,64,256]{2,1,0:T(8,128)(2,1)}), bf16[16,64,256]{2,1,0:T(8,128)(2,1)S(1)}, u32[]{:S(2)}, u32[]{:S(2)}) async-start(bf16[16,64,256]{2,1,0:T(8,128)(2,1)} %get-tuple-element.12), calls=%async_computation | async-start | bytes 1048576 | tf_op jit(solution)/shard_map/all_to_all | solution.py:326
  17.6 4.4 %collective-permute-start = (s32[3,32]{1,0:T(4,128)S(1)}, s32[3,32]{1,0:T(4,128)S(1)}, u32[]{:S(2)}, u32[]{:S(2)}) collective-permute-start(s32[3,32]{1,0:T(4,128)S(1)} %get-tuple-element.14.mine_ref), channel_id=1, source_target_pairs={{0,16},{16,0},{1,17},{17,1},{2,18},{18,2},{3,19},{19,3},{4,20},{20... | collective-permute-start | bytes 1160 | tf_op jit(solution)/shard_map/ppermute | solution.py:337
  24.2 14.1 %collective-permute-start.1 = (bf16[128,128]{1,0:T(8,128)(2,1)S(1)}, bf16[128,128]{1,0:T(8,128)(2,1)S(1)}, u32[]{:S(2)}, u32[]{:S(2)}) collective-permute-start(bf16[128,128]{1,0:T(8,128)(2,1)S(1)} %get-tuple-element.15.kv_ref), channel_id=1, source_target_pairs={{17,16},{16,17},{19,18},{18,19},{21,20},{20,21},{23,22},{22,23},{4... | collective-permute-start | bytes 98312 | tf_op jit(solution)/shard_map/ppermute | solution.py:361
  24.8 13.4 %collective-permute-start.2 = (bf16[128,128]{1,0:T(8,128)(2,1)S(1)}, bf16[128,128]{1,0:T(8,128)(2,1)S(1)}, u32[]{:S(2)}, u32[]{:S(2)}) collective-permute-start(bf16[128,128]{1,0:T(8,128)(2,1)S(1)} %get-tuple-element.15.kv_ref), channel_id=1, source_target_pairs={{8,0},{9,1},{10,2},{11,3},{12,4},{13,5},{14,6},{15,7},{25,16},{24,... | collective-permute-start | bytes 98312 | tf_op jit(solution)/shard_map/ppermute | solution.py:358
  38.2 43.6 %copy-start.1 = (s32[2,32]{1,0:T(2,128)S(1)}, s32[2,32]{1,0:T(2,128)}, u32[]{:S(2)}) copy-start(s32[2,32]{1,0:T(2,128)} %codes_ref.1) | copy-start | bytes 772
  38.2 44.7 %copy-start = (bf16[4096,256]{1,0:T(8,128)(2,1)S(1)}, bf16[4096,256]{1,0:T(8,128)(2,1)}, u32[]{:S(2)}) copy-start(bf16[4096,256]{1,0:T(8,128)(2,1)} %param.19) | copy-start | bytes 6291460
  77.2 6.6 %collective-permute-start.5 = (bf16[8,64,256]{2,1,0:T(8,128)(2,1)S(1)}, bf16[8,64,256]{2,1,0:T(8,128)(2,1)S(1)}, u32[]{:S(2)}, u32[]{:S(2)}) collective-permute-start(bf16[8,64,256]{2,1,0:T(8,128)(2,1)S(1)} %all_to_all.16.rows_ref), channel_id=1, source_target_pairs={{0,1},{1,0},{2,3},{3,2},{4,5},{5,4},{6,7},{7,6},{8,9},{9,8},{10,11... | collective-permute-start | bytes 786440 | tf_op jit(solution)/shard_map/ppermute | solution.py:391

commit v8 on v7

v8 whole, which is shorter than its diff:
```python
import functools
import math

import jax
import jax.numpy as jnp
from jax import lax
from jax.experimental import pallas as pl
from jax.experimental.pallas import tpu as pltpu
from jax.sharding import Mesh, PartitionSpec as P

KEY_HEADS = 8
HEAD = 128
STAT = 16
CHUNK = HEAD + STAT
DEAD = -1e30
EXP2_SCALE = HEAD ** (-0.5) * math.log2(math.e)
MIB = 1024 * 1024


def one_hot_rows(index_row, count):
    rows = index_row.shape[1]
    tall = jnp.transpose(jnp.broadcast_to(index_row, (128, rows)))
    parts = []
    for start in range(0, count, 128):
        lane = lax.broadcasted_iota(jnp.int32, (rows, 128), 1) + start
        parts.append((tall == lane).astype(jnp.float32).astype(jnp.bfloat16))
    return jnp.concatenate(parts, axis=1)


def look_kernel(codes_hbm, parents_hbm, query_hbm, out_ref, own_ref, mine_ref, query_ref, sem):
    levels, beams = codes_hbm.shape
    copies = [
        pltpu.make_async_copy(codes_hbm, mine_ref.at[pl.ds(0, levels)], sem.at[0]),
        pltpu.make_async_copy(parents_hbm, mine_ref.at[pl.ds(levels, 1)], sem.at[1]),
        pltpu.make_async_copy(query_hbm, query_ref, sem.at[2]),
    ]
    for copy in copies:
        copy.start()
    copies[0].wait()
    copies[1].wait()
    hots = [one_hot_rows(mine_ref[level : level + 1], query_ref.shape[1]) for level in range(levels)]
    copies[2].wait()
    for level, hot in enumerate(hots):
        found = jnp.dot(hot, query_ref[level], preferred_element_type=jnp.float32).astype(jnp.bfloat16)
        own_ref[level * beams : (level + 1) * beams] = found
        for target in range(out_ref.shape[0]):
            out_ref[target, level * beams : (level + 1) * beams] = found


def generated_kernel(
    meta_ref, mine_ref, other_ref, kv_hbm, embed_hbm, lengths_hbm, holders_hbm, out_ref, residual_ref, live_ref,
    kv_ref, embed_ref, lengths_ref, holders_ref, sem
):
    copies = [
        pltpu.make_async_copy(lengths_hbm, lengths_ref, sem.at[0]),
        pltpu.make_async_copy(holders_hbm, holders_ref, sem.at[1]),
        pltpu.make_async_copy(kv_hbm, kv_ref, sem.at[2]),
        pltpu.make_async_copy(embed_hbm, embed_ref, sem.at[3]),
    ]
    for copy in copies:
        copy.start()
    levels, beams = kv_ref.shape[0], mine_ref.shape[1]
    hots = [
        jnp.concatenate([one_hot_rows(ref[level : level + 1], kv_ref.shape[1]) for ref in (mine_ref, other_ref)])
        for level in range(levels)
    ]
    for copy in copies:
        copy.wait()
    for level, hot in enumerate(hots):
        found = jnp.dot(hot, kv_ref[level], preferred_element_type=jnp.float32).astype(jnp.bfloat16)
        residual_ref[level * beams : (level + 1) * beams] = jnp.dot(
            hot[:beams], embed_ref[level], preferred_element_type=jnp.float32
        )
        for part, x in enumerate((meta_ref[2], 1 - meta_ref[2])):
            place = pl.ds(pl.multiple_of((x * levels + level) * beams, beams), beams)
            out_ref[place] = found[part * beams : (part + 1) * beams]
    request, place, block_slots = meta_ref[0], meta_ref[1], meta_ref[3]
    near, far = jnp.int32(0), jnp.int32(0)
    for block in range(holders_ref.shape[1]):
        holder = holders_ref[request, block]
        near = jnp.where(holder == place, block, near)
        far = jnp.where(holder == jnp.bitwise_xor(place, 1), block, far)
    for at, position in enumerate((near, far)):
        live_ref[at] = jnp.clip(lengths_ref[request] - position * block_slots, 0, block_slots)


def split3(value):
    high = value.astype(jnp.bfloat16).astype(jnp.float32)
    rest = value - high
    middle = rest.astype(jnp.bfloat16).astype(jnp.float32)
    return high, middle, rest - middle


def stat_rows(top, total):
    row = lax.broadcasted_iota(jnp.int32, (STAT, top.shape[1]), 0)
    out = jnp.zeros((STAT, top.shape[1]), jnp.float32)
    for at, piece in enumerate(split3(top) + split3(total)):
        out = jnp.where(row == at, piece, out)
    return out.astype(jnp.bfloat16)


def read_stats(rows):
    wide = rows.astype(jnp.float32)
    return wide[0:1] + wide[1:2] + wide[2:3], wide[3:4] + wide[4:5] + wide[5:6]


def scores_of(keys, rows):
    return lax.dot_general(keys, rows, (((1,), (1,)), ((), ())), preferred_element_type=jnp.float32)


def extended(values):
    return jnp.concatenate([jnp.transpose(values), jnp.ones((STAT, values.shape[0]), jnp.bfloat16)], axis=0)


def query_rows_of(pair):
    return jnp.concatenate([pair[:, h * HEAD : (h + 1) * HEAD] for h in range(2)], axis=0)


def attend_kernel(
    flip, meta_ref, live_ref, query_ref, near_key, near_value, far_key, far_value,
    out_ref, score_ref, key_ref, value_ref, key_sem, value_sem
):
    heads, slots, pair_lanes = key_ref.shape
    block_slots = slots // 2
    near_live, far_live = live_ref[0], live_ref[1]
    live = near_live + far_live
    first = jnp.bitwise_xor(meta_ref[2], flip) * 2 * heads

    def queries(head):
        pieces = []
        for part in range(2):
            rows = query_rows_of(query_ref[first + 2 * head + part])
            blank = jnp.zeros_like(rows)
            pieces.append(jnp.concatenate([blank, rows] if part else [rows, blank], axis=1))
        return jnp.concatenate(pieces, axis=0)

    def write(head, sums, top):
        width = sums.shape[1] // 2
        for part in range(2):
            lanes = slice(part * width, (part + 1) * width)
            out_ref[2 * head + part, 0:HEAD] = sums[part * HEAD : (part + 1) * HEAD, lanes].astype(jnp.bfloat16)
            out_ref[2 * head + part, HEAD:CHUNK] = stat_rows(top[:, lanes], sums[2 * HEAD : 2 * HEAD + 1, lanes])

    def copies(head, keys):
        sources, target, sem = ((near_key, far_key), key_ref, key_sem) if keys else ((near_value, far_value), value_ref, value_sem)
        lanes = pl.ds(pl.multiple_of(head * pair_lanes, pair_lanes), pair_lanes)
        return [
            pltpu.make_async_copy(
                source.at[:, lanes], target.at[head, pl.ds(block * block_slots, block_slots)], sem.at[block * heads + head]
            )
            for block, source in enumerate(sources)
        ]

    def wait(head, keys):
        for copy in copies(head, keys):
            copy.wait()

    def attend(masked):
        def begin(head, _):
            for keys in (True, False):
                for copy in copies(head, keys):
                    copy.start()
            return 0

        lax.fori_loop(0, heads, begin, 0)

        def score(head, at):
            scores = scores_of(key_ref[head], queries(head))
            if masked:
                slot = lax.broadcasted_iota(jnp.int32, (slots, 1), 0)
                allowed = (slot < near_live) | ((slot >= block_slots) & (slot < block_slots + far_live))
                scores = jnp.where(allowed, scores, DEAD)
            score_ref[at] = scores
            return jnp.max(scores, axis=0, keepdims=True)

        def finish(head, at, top):
            weights = jnp.exp2((score_ref[at] - top) * EXP2_SCALE).astype(jnp.bfloat16)
            sums = jnp.dot(extended(value_ref[head]), weights, preferred_element_type=jnp.float32)
            write(head, sums, top)

        def step(i, top):
            wait(2 * i + 1, True)
            wait(2 * i + 2, True)
            wait(2 * i, False)
            wait(2 * i + 1, False)
            later = score(2 * i + 1, 1)
            finish(2 * i, 0, top)
            top = score(2 * i + 2, 0)
            finish(2 * i + 1, 1, later)
            return top

        wait(0, True)
        top = lax.fori_loop(0, heads // 2 - 1, step, score(0, 0))
        wait(heads - 1, True)
        wait(heads - 2, False)
        wait(heads - 1, False)
        later = score(heads - 1, 1)
        finish(heads - 2, 0, top)
        finish(heads - 1, 1, later)

    @pl.when(live == slots)
    def _():
        attend(False)

    @pl.when((live > 0) & (live < slots))
    def _():
        attend(True)

    @pl.when(live == 0)
    def _():
        row = lax.broadcasted_iota(jnp.int32, out_ref.shape[1:], 0)
        dead = jnp.zeros(out_ref.shape[1:], jnp.float32)
        for at, piece in enumerate(split3(jnp.full(out_ref.shape[1:], DEAD, jnp.float32))):
            dead = jnp.where(row == HEAD + at, piece, dead)
        for head in range(out_ref.shape[0]):
            out_ref[head] = dead.astype(jnp.bfloat16)


def merge_kernel(mine_ref, other_ref, out_ref):
    for chunk in range(mine_ref.shape[0]):
        tops, totals = zip(*(read_stats(ref[chunk, HEAD:CHUNK]) for ref in (mine_ref, other_ref)))
        top = jnp.maximum(*tops)
        factors = [jnp.exp2((each - top) * EXP2_SCALE) for each in tops]
        total = totals[0] * factors[0] + totals[1] * factors[1]
        sums = (
            mine_ref[chunk, 0:HEAD].astype(jnp.float32) * factors[0]
            + other_ref[chunk, 0:HEAD].astype(jnp.float32) * factors[1]
        )
        out_ref[chunk, 0:HEAD] = sums.astype(jnp.bfloat16)
        out_ref[chunk, HEAD:CHUNK] = stat_rows(top, total)


def combine_kernel(meta_ref, parts_ref, query_ref, even_ref, odd_ref, mine_ref, out_ref):
    count, _, lanes = parts_ref.shape
    half = query_ref.shape[0]
    beams = mine_ref.shape[1]
    second = jnp.bitwise_and(meta_ref[1], 1) == 1
    keys = jnp.where(second, odd_ref[...], even_ref[...])
    values = jnp.where(second, even_ref[...], odd_ref[...])
    row = lax.broadcasted_iota(jnp.int32, (2 * half, lanes), 0)
    lane = lax.broadcasted_iota(jnp.int32, (2 * half, lanes), 1)
    parents = mine_ref[mine_ref.shape[0] - 1 :]
    parents = (parents // beams) * half + parents % beams
    parents = jnp.concatenate([jnp.full_like(parents, -1), parents] * 2, axis=1)
    allowed = (row == meta_ref[2] * half + lane % half) | (row == parents)
    scores = jnp.where(allowed, scores_of(keys, query_rows_of(query_ref[...])), DEAD)

    stats = [read_stats(parts_ref[part, HEAD:CHUNK]) for part in range(count)]
    top = functools.reduce(jnp.maximum, [each for each, _ in stats], jnp.max(scores, axis=0, keepdims=True))
    weights = jnp.where(allowed, jnp.exp2((scores - top) * EXP2_SCALE), 0.0)
    high = weights.astype(jnp.bfloat16)
    low = (weights - high.astype(jnp.float32)).astype(jnp.bfloat16)
    tall_values = jnp.transpose(values)
    sums = jnp.dot(tall_values, high, preferred_element_type=jnp.float32)
    sums = sums + jnp.dot(tall_values, low, preferred_element_type=jnp.float32)
    total = jnp.sum(weights, axis=0, keepdims=True)
    for part in range(count):
        factor = jnp.exp2((stats[part][0] - top) * EXP2_SCALE)
        total = total + stats[part][1] * factor
        sums = sums + parts_ref[part, 0:HEAD].astype(jnp.float32) * factor
    tall = jnp.transpose(sums / total)
    found = jnp.concatenate([tall[0:half], tall[half : 2 * half]], axis=1).astype(jnp.bfloat16)
    for target in range(out_ref.shape[0]):
        out_ref[target] = found


def project_kernel(flip, meta_ref, rows_ref, weight_ref, before_ref, out_ref):
    total = before_ref[...]
    parity = jnp.bitwise_xor(jnp.bitwise_and(meta_ref[1], 1), flip)
    for part in range(rows_ref.shape[0]):
        total = total + jnp.dot(rows_ref[part], weight_ref[part, parity], preferred_element_type=jnp.float32)
    out_ref[...] = total.astype(out_ref.dtype)


def call(kernel, out_shape, name, spaces, vmem, out_spaces="v", **rest):
    kinds = {"s": pltpu.SMEM, "v": pltpu.VMEM, "h": pltpu.HBM, "a": pl.ANY}
    specs = lambda letters: [pl.BlockSpec(memory_space=kinds[letter]) for letter in letters]
    return pl.pallas_call(
        kernel,
        out_shape=out_shape,
        in_specs=specs(spaces),
        out_specs=specs(out_spaces) if len(out_spaces) > 1 else specs(out_spaces)[0],
        compiler_params=pltpu.CompilerParams(vmem_limit_bytes=vmem * MIB),
        name=name,
        **rest,
    )


def shards(
    codes, parents, lengths, holders, history_keys, history_values, query_table, kv_table, embed_table, out_weight
):
    beams = parents.shape[0]
    levels, code_count, width = query_table.shape
    half = levels * beams
    rows = 2 * half
    slots = history_keys.shape[1]
    z_count = lax.axis_size("z")
    pair, z, core = lax.axis_index("pair"), lax.axis_index("z"), lax.axis_index("core")
    hist = 2 * z + core
    bf16, f32 = jnp.bfloat16, jnp.float32
    array = jax.ShapeDtypeStruct
    dma = pltpu.SemaphoreType.DMA
    swap = [(0, 1), (1, 0)]

    hbm = lambda x: pltpu.with_memory_space_constraint(x, pltpu.HBM)

    query_rows, own_query, mine = call(
        look_kernel,
        (array((2 * z_count, half, width), bf16), array((half, width), bf16), array((levels + 1, beams), jnp.int32)),
        "look",
        "hhh",
        4,
        "vvv",
        scratch_shapes=[pltpu.VMEM(query_table.shape, bf16), dma((3,))],
    )(hbm(codes), hbm(parents[None]), hbm(query_table))
    queries = lax.all_to_all(query_rows, ("pair", "z"), split_axis=0, concat_axis=0, tiled=True)

    mine, near_keys, near_values = lax.optimization_barrier((mine, history_keys[0], history_values[0]))
    other = lax.ppermute(mine, "pair", swap)
    far_keys = lax.ppermute(near_keys, "core", swap)
    far_values = lax.ppermute(near_values, "core", swap)
    meta = jnp.stack([lax.axis_index("grp"), pair * 2 * z_count + hist, pair, jnp.int32(slots)]).astype(jnp.int32)
    kv_rows, residual, live = call(
        generated_kernel,
        (array((rows, HEAD), bf16), array((half, width), f32), array((2,), jnp.int32)),
        "generated",
        "svvhhhh",
        4,
        "vvs",
        scratch_shapes=[
            pltpu.VMEM(kv_table.shape, bf16),
            pltpu.VMEM(embed_table.shape, bf16),
            pltpu.SMEM(lengths.shape, jnp.int32),
            pltpu.SMEM(holders.shape, jnp.int32),
            dma((4,)),
        ],
    )(meta, mine, other, hbm(kv_table), hbm(embed_table), hbm(lengths), hbm(holders))
    even = [(k + KEY_HEADS * v, 2 * k + v) for k in range(KEY_HEADS) for v in range(2)]
    odd = [(k + KEY_HEADS * v, 2 * k + 1 - v) for k in range(KEY_HEADS) for v in range(2)]
    even_rows = lax.ppermute(kv_rows, ("z", "core"), even)
    odd_rows = lax.ppermute(kv_rows, ("z", "core"), odd)

    shape = (z_count, CHUNK, 2 * half)

    def attend(flip, name, queries):
        return call(
            functools.partial(attend_kernel, flip),
            array(shape, bf16),
            name,
            "ssvhhaa",
            24,
            scratch_shapes=[
                pltpu.VMEM((2, 2 * slots, 2 * rows), f32),
                pltpu.VMEM((KEY_HEADS // 2, 2 * slots, 2 * HEAD), bf16),
                pltpu.VMEM((KEY_HEADS // 2, 2 * slots, 2 * HEAD), bf16),
                dma((KEY_HEADS,)),
                dma((KEY_HEADS,)),
            ],
            cost_estimate=pl.CostEstimate(
                flops=2 * 4 * rows * KEY_HEADS * slots * HEAD,
                bytes_accessed=4 * slots * KEY_HEADS * HEAD,
                transcendentals=2 * rows * KEY_HEADS * slots,
            ),
        )(meta, live, queries, hbm(near_keys), hbm(near_values), far_keys, far_values)

    send = attend(1, "attend_other", queries)
    arrived = lax.ppermute(send, "pair", swap)
    queries, even_rows, odd_rows = lax.optimization_barrier((queries, even_rows, odd_rows))
    keep = attend(0, "attend_own", queries)
    merged = call(merge_kernel, array(shape, bf16), "merge", "vv", 4)(keep, arrived)
    parts = lax.all_to_all(merged, "z", split_axis=0, concat_axis=0, tiled=True)
    attention = call(combine_kernel, array((z_count, half, width), bf16), "combine", "svvvvv", 4)(
        meta, parts, own_query, even_rows, odd_rows, mine
    )
    near_rows = lax.all_to_all(attention, "z", split_axis=0, concat_axis=0, tiled=True)
    far_rows = lax.ppermute(near_rows, "core", swap)
    weight = out_weight.reshape(z_count, 2, width, width)
    begun = call(functools.partial(project_kernel, 0), array((half, width), f32), "project_near", "svvv", 4)(
        meta, near_rows, weight, residual
    )
    out = call(functools.partial(project_kernel, 1), array((half, width), bf16), "project_far", "svvv", 4)(
        meta, far_rows, weight, begun
    )
    return out.reshape(levels, beams, width)


def solution(mesh):
    split = Mesh(mesh.devices.reshape(16, 2, 8, 2), ("grp", "pair", "z", "core"))
    req, hist = ("grp", "pair"), ("z", "core")
    in_specs = (
        P(None, req),
        P(req),
        P(),
        P(),
        P(req, hist, None),
        P(req, hist, None),
        P(None, None, hist),
        P(None, None, hist),
        P(None, None, hist),
        P(None, hist),
    )
    return jax.shard_map(shards, mesh=split, in_specs=in_specs, out_specs=P(None, req, hist), check_vma=False)
```

time: 85.7 us -> 98.2 us (1.15)
  starting transfers between devices: 25.4 us -> 36.5 us
  blocking collectives: 37.7 us -> 26.8 us
  waiting for transfers between devices: 5.77 us -> 13.2 us
  Pallas kernels: 16.1 us -> 20.2 us
    ppermute x2 -> x3, starting transfers between devices: 1.96 us -> 11.8 us  [the longest x1 5.44 us: shards(): odd_rows = lax.ppermute(kv_rows, ('z', 'core'), odd)]
    all_to_all x1, blocking collectives: 23.7 us -> 14.1 us  [shards(): parts = lax.all_to_all(merged, 'z', split_axis=0, concat_axis=0, tiled=True)]
    ppermute x2 -> x3, waiting for transfers between devices: 0.01 us -> 5.3 us  [the longest x1 5.3 us: shards(): even_rows = lax.ppermute(kv_rows, ('z', 'core'), even)]
    pallas_call x6, Pallas kernels: 13.8 us -> 17.9 us  [the longest x2 12.5 us: attend(): call(functools.partial(attend_kernel, flip), array(shape, bf16), name, 's...]
    all_to_all x1, waiting for transfers between devices: 4.73 us -> 6.56 us  [shards(): lax.all_to_all(query_rows, ('pair', 'z'), split_axis=0, concat_axis=0, ti...]
    all_to_all x1, blocking collectives: 14 us -> 12.7 us  [shards(): lax.all_to_all(attention, 'z', split_axis=0, concat_axis=0, tiled=True)]
    ppermute x1, starting transfers between devices: 4.56 us -> 5.8 us  [shards(): far_rows = lax.ppermute(near_rows, 'core', swap)]
  transfers between devices with their start and end apart: 7 -> 8, of which waited for: 2 -> 4; matrix products, arithmetic and copies ran while one was open for 0% -> 0% of each run, Pallas kernels for 13% -> 10%
where the time goes in v8:
time: 98.2 us; the launch traced here: 96.9 us
  starting transfers between devices  36.5 us (37%)
  blocking collectives  26.8 us (27%)
  Pallas kernels  20.2 us (21%)
  waiting for transfers between devices  13.2 us (13%)
    all_to_all x1, blocking collectives, shards(): parts = lax.all_to_all(merged, 'z', split_axis=0, concat_axis=0, tiled=True)  14.1 us
    all_to_all x1, blocking collectives, shards(): lax.all_to_all(attention, 'z', split_axis=0, concat_axis=0, tiled=True)  12.7 us
    pallas_call x2, Pallas kernels, attend(): call(functools.partial(attend_kernel, flip), array(shape, bf16), name, 's...  12.5 us
    all_to_all x1, starting transfers between devices, shards(): lax.all_to_all(query_rows, ('pair', 'z'), split_axis=0, concat_axis=0, ti...  11.1 us
    all_to_all x1, waiting for transfers between devices, shards(): lax.all_to_all(query_rows, ('pair', 'z'), split_axis=0, concat_axis=0, ti...  6.56 us
    ppermute x1, starting transfers between devices, shards(): far_rows = lax.ppermute(near_rows, 'core', swap)  5.8 us
    ppermute x1, starting transfers between devices, shards(): odd_rows = lax.ppermute(kv_rows, ('z', 'core'), odd)  5.44 us
    ppermute x1, waiting for transfers between devices, shards(): even_rows = lax.ppermute(kv_rows, ('z', 'core'), even)  5.3 us
  transfers between devices with their start and end apart: 8, of which 4 were waited for; matrix products, arithmetic and copies ran while one was open for 0% of the time, Pallas kernels for 10%

profile of v8, /device:TPU:57, one launch (start us, length us, event | category | flops | bytes accessed | tf_op | source)
XLA Modules:
  0.0 96.9 jit_solution(6572224427406759893)
XLA Ops:
  0.0 2.0 %look.1 = (bf16[16,64,256]{2,1,0:T(8,128)(2,1)}, bf16[64,256]{1,0:T(8,128)(2,1)S(1)}, s32[3,32]{1,0:T(4,128)S(1)}) custom-call(s32[2,32]{1,0:T(2,128)} %codes_hbm.1, s32[1,32]{1,0:T(1,128)} %bitcast.16, bf16[2,256,256]{2,1,0:T(8,128)(2,1)} %query_hbm.1), custom_call_target="tpu_custom_call" | custom-call | tf_op jit(solution)/shard_map/look/pallas_call | solution.py:307
  2.0 2.6 %collective-permute-start.3 = (bf16[1024,1024]{1,0:T(8,128)(2,1)}, bf16[1024,1024]{1,0:T(8,128)(2,1)S(1)}, u32[]{:S(2)}, u32[]{:S(2)}) collective-permute-start(bf16[1024,1024]{1,0:T(8,128)(2,1)} %bitcast.10), channel_id=1, source_target_pairs={{0,1},{1,0},{2,3},{3,2},{4,5},{5,4},{6,7},{7,6},{8,9},{9,8},{10,11... | collective-permute-start | bytes 6291464 | tf_op jit(solution)/shard_map/ppermute | solution.py:320
  4.6 1.9 %collective-permute-start.4 = (bf16[1024,1024]{1,0:T(8,128)(2,1)}, bf16[1024,1024]{1,0:T(8,128)(2,1)}, u32[]{:S(2)}, u32[]{:S(2)}) collective-permute-start(bf16[1024,1024]{1,0:T(8,128)(2,1)} %bitcast.13), channel_id=1, source_target_pairs={{0,1},{1,0},{2,3},{3,2},{4,5},{5,4},{6,7},{7,6},{8,9},{9,8},{10,11... | collective-permute-start | bytes 6291464 | tf_op jit(solution)/shard_map/ppermute | solution.py:321
  6.5 11.1 %all-to-all-start = ((bf16[16,64,256]{2,1,0:T(8,128)(2,1)}), bf16[16,64,256]{2,1,0:T(8,128)(2,1)S(1)}, u32[]{:S(2)}, u32[]{:S(2)}) async-start(bf16[16,64,256]{2,1,0:T(8,128)(2,1)} %get-tuple-element.20), calls=%async_computation | async-start | bytes 1048576 | tf_op jit(solution)/shard_map/all_to_all | solution.py:316
  17.6 3.3 %collective-permute-start = (s32[3,32]{1,0:T(4,128)S(1)}, s32[3,32]{1,0:T(4,128)S(1)}, u32[]{:S(2)}, u32[]{:S(2)}) collective-permute-start(s32[3,32]{1,0:T(4,128)S(1)} %get-tuple-element.18.mine_ref), channel_id=1, source_target_pairs={{0,16},{16,0},{1,17},{17,1},{2,18},{18,2},{3,19},{19,3},{4,20},{20... | collective-permute-start | bytes 1160 | tf_op jit(solution)/shard_map/ppermute | solution.py:319
  20.9 0.1 pad_add_fusion.meta_ref
  21.0 1.0 %collective-permute-done.other_ref = s32[3,32]{1,0:T(4,128)S(1)} collective-permute-done((s32[3,32]{1,0:T(4,128)S(1)}, s32[3,32]{1,0:T(4,128)S(1)}, u32[]{:S(2)}, u32[]{:S(2)}) %collective-permute-start) | collective-permute-done | bytes 416 | tf_op jit(solution)/shard_map/ppermute | solution.py:319
  22.0 2.3 %generated.1 = (bf16[128,128]{1,0:T(8,128)(2,1)S(1)}, f32[64,256]{1,0:T(8,128)S(1)}, s32[2]{0:T(128)S(1)}) custom-call(s32[4]{0:T(128)S(1)} %pad_add_fusion.meta_ref, s32[3,32]{1,0:T(4,128)S(1)} %get-tuple-element.18.mine_ref, s32[3,32]{1,0:T(4,128)S(1)} %collective-permute-done.other_ref, bf16[2,256,128]{2,1,0:T(8,128)(2,1)} %kv_hbm.1, ...), custom_call_target="tpu_custom_call" | custom-call | tf_op jit(solution)/shard_map/generated/pallas_call | solution.py:323
  24.3 6.6 %all-to-all-done.query_ref = bf16[16,64,256]{2,1,0:T(8,128)(2,1)S(1)} async-done(((bf16[16,64,256]{2,1,0:T(8,128)(2,1)}), bf16[16,64,256]{2,1,0:T(8,128)(2,1)S(1)}, u32[]{:S(2)}, u32[]{:S(2)}) %all-to-all-start) | async-done | bytes 524320 | tf_op jit(solution)/shard_map/all_to_all | solution.py:316
  30.9 0.0 collective-permute-done.3.far_key
  30.9 0.0 collective-permute-done.4.far_value
  30.9 6.2 %attend_other.1 = bf16[8,144,128]{2,1,0:T(8,128)(2,1)S(1)} custom-call(s32[4]{0:T(128)S(1)} %pad_add_fusion.meta_ref, s32[2]{0:T(128)S(1)} %get-tuple-element.19.live_ref, bf16[16,64,256]{2,1,0:T(8,128)(2,1)S(1)} %all-to-all-done.query_ref, bf16[1024,1024]{1,0:T(8,128)(2,1)} %bitcast.11, bf16[1024,1024]{1,0:T(8,128)(2,1)} %bitcast.14, ...), custom_call_target="tpu_custom_call" | custom-call | flops 1073741824 | bytes 4194304 | tf_op jit(solution)/shard_map/attend_other/pallas_call | solution.py:346
  37.0 2.3 %collective-permute-start.5 = (bf16[8,144,128]{2,1,0:T(8,128)(2,1)S(1)}, bf16[8,144,128]{2,1,0:T(8,128)(2,1)S(1)}, u32[]{:S(2)}, u32[]{:S(2)}) collective-permute-start(bf16[8,144,128]{2,1,0:T(8,128)(2,1)S(1)} %attend_other.1), channel_id=1, source_target_pairs={{0,16},{16,0},{1,17},{17,1},{2,18},{18,2},{3,19},{19,3},{4,20},{20... | collective-permute-start | bytes 884744 | tf_op jit(solution)/shard_map/ppermute | solution.py:367
  39.3 5.4 %collective-permute-start.2 = (bf16[128,128]{1,0:T(8,128)(2,1)S(1)}, bf16[128,128]{1,0:T(8,128)(2,1)S(1)}, u32[]{:S(2)}, u32[]{:S(2)}) collective-permute-start(bf16[128,128]{1,0:T(8,128)(2,1)S(1)} %get-tuple-element.21), channel_id=1, source_target_pairs={{0,1},{8,0},{1,3},{9,2},{2,5},{10,4},{3,7},{11,6},{4,9},{12,8},{5,... | collective-permute-start | bytes 98312 | tf_op jit(solution)/shard_map/ppermute | solution.py:341
  44.8 4.1 %collective-permute-start.1 = (bf16[128,128]{1,0:T(8,128)(2,1)S(1)}, bf16[128,128]{1,0:T(8,128)(2,1)S(1)}, u32[]{:S(2)}, u32[]{:S(2)}) collective-permute-start(bf16[128,128]{1,0:T(8,128)(2,1)S(1)} %get-tuple-element.21), channel_id=1, source_target_pairs={{0,0},{8,1},{1,2},{9,3},{2,4},{10,5},{3,6},{11,7},{4,8},{12,9},{5,... | collective-permute-start | bytes 98312 | tf_op jit(solution)/shard_map/ppermute | solution.py:340
  48.8 0.0 collective-permute-done.2.odd_ref
  48.9 5.3 %collective-permute-done.1.even_ref = bf16[128,128]{1,0:T(8,128)(2,1)S(1)} collective-permute-done((bf16[128,128]{1,0:T(8,128)(2,1)S(1)}, bf16[128,128]{1,0:T(8,128)(2,1)S(1)}, u32[]{:S(2)}, u32[]{:S(2)}) %collective-permute-start.1) | collective-permute-done | bytes 32800 | tf_op jit(solution)/shard_map/ppermute | solution.py:340
  54.2 6.3 %attend_own.1.mine_ref = bf16[8,144,128]{2,1,0:T(8,128)(2,1)S(1)} custom-call(s32[4]{0:T(128)S(1)} %pad_add_fusion.meta_ref, s32[2]{0:T(128)S(1)} %get-tuple-element.19.live_ref, bf16[16,64,256]{2,1,0:T(8,128)(2,1)S(1)} %all-to-all-done.query_ref, bf16[1024,1024]{1,0:T(8,128)(2,1)} %bitcast.12, bf16[1024,1024]{1,0:T(8,128)(2,1)} %bitcast.15, ...), custom_call_target="tpu_custom_call" | custom-call | flops 1073741824 | bytes 4194304 | tf_op jit(solution)/shard_map/attend_own/pallas_call | solution.py:346
  60.5 0.0 copy-start
  60.5 0.0 collective-permute-done.5.other_ref
  60.5 0.2 merge.1
  60.7 14.1 %all_to_all.15.parts_ref = bf16[8,144,128]{2,1,0:T(8,128)(2,1)S(1)} all-to-all(bf16[8,144,128]{2,1,0:T(8,128)(2,1)S(1)} %merge.1), channel_id=1, replica_groups=mesh['grp'=16,'pair'=2,'z'=8,'core'=2] {'z'}, dimensions={0} | all-to-all | bytes 589824 | tf_op jit(solution)/shard_map/all_to_all | solution.py:371
  74.8 1.0 %combine.1 = bf16[8,64,256]{2,1,0:T(8,128)(2,1)S(1)} custom-call(s32[4]{0:T(128)S(1)} %pad_add_fusion.meta_ref, bf16[8,144,128]{2,1,0:T(8,128)(2,1)S(1)} %all_to_all.15.parts_ref, bf16[64,256]{1,0:T(8,128)(2,1)S(1)} %get-tuple-element.25.query_ref, bf16[128,128]{1,0:T(8,128)(2,1)S(1)} %collective-permute-done.1.even_ref, ...), custom_call_target="tpu_custom_call" | custom-call | tf_op jit(solution)/shard_map/combine/pallas_call | solution.py:372
  75.8 12.7 %all_to_all.16.rows_ref = bf16[8,64,256]{2,1,0:T(8,128)(2,1)S(1)} all-to-all(bf16[8,64,256]{2,1,0:T(8,128)(2,1)S(1)} %combine.1), channel_id=1, replica_groups=mesh['grp'=16,'pair'=2,'z'=8,'core'=2] {'z'}, dimensions={0} | all-to-all | bytes 524288 | tf_op jit(solution)/shard_map/all_to_all | solution.py:375
  88.5 5.8 %collective-permute-start.6 = (bf16[8,64,256]{2,1,0:T(8,128)(2,1)S(1)}, bf16[8,64,256]{2,1,0:T(8,128)(2,1)S(1)}, u32[]{:S(2)}, u32[]{:S(2)}) collective-permute-start(bf16[8,64,256]{2,1,0:T(8,128)(2,1)S(1)} %all_to_all.16.rows_ref), channel_id=1, source_target_pairs={{0,1},{1,0},{2,3},{3,2},{4,5},{5,4},{6,7},{7,6},{8,9},{9,8},{10,11... | collective-permute-start | bytes 786440 | tf_op jit(solution)/shard_map/ppermute | solution.py:376
  94.3 0.0 copy-done
  94.3 0.9 project_near.1.before_ref
  95.2 0.3 collective-permute-done.6.rows_ref
  95.5 1.5 %project_far.1 = bf16[64,256]{1,0:T(8,128)(2,1)} custom-call(s32[4]{0:T(128)S(1)} %pad_add_fusion.meta_ref, bf16[8,64,256]{2,1,0:T(8,128)(2,1)S(1)} %collective-permute-done.6.rows_ref, bf16[8,2,256,256]{3,2,1,0:T(8,128)(2,1)S(1)} %bitcast.9, f32[64,256]{1,0:T(8,128)S(1)} %project_near.1.before_ref), custom_call_target="tpu_custom_call" | custom-call | tf_op jit(solution)/shard_map/project_far/pallas_call | solution.py:381
Async XLA Ops:
  2.0 28.9 %collective-permute-start.3 = (bf16[1024,1024]{1,0:T(8,128)(2,1)}, bf16[1024,1024]{1,0:T(8,128)(2,1)S(1)}, u32[]{:S(2)}, u32[]{:S(2)}) collective-permute-start(bf16[1024,1024]{1,0:T(8,128)(2,1)} %bitcast.10), channel_id=1, source_target_pairs={{0,1},{1,0},{2,3},{3,2},{4,5},{5,4},{6,7},{7,6},{8,9},{9,8},{10,11... | collective-permute-start | bytes 6291464 | tf_op jit(solution)/shard_map/ppermute | solution.py:320
  4.6 26.3 %collective-permute-start.4 = (bf16[1024,1024]{1,0:T(8,128)(2,1)}, bf16[1024,1024]{1,0:T(8,128)(2,1)}, u32[]{:S(2)}, u32[]{:S(2)}) collective-permute-start(bf16[1024,1024]{1,0:T(8,128)(2,1)} %bitcast.13), channel_id=1, source_target_pairs={{0,1},{1,0},{2,3},{3,2},{4,5},{5,4},{6,7},{7,6},{8,9},{9,8},{10,11... | collective-permute-start | bytes 6291464 | tf_op jit(solution)/shard_map/ppermute | solution.py:321
  6.5 24.3 %all-to-all-start = ((bf16[16,64,256]{2,1,0:T(8,128)(2,1)}), bf16[16,64,256]{2,1,0:T(8,128)(2,1)S(1)}, u32[]{:S(2)}, u32[]{:S(2)}) async-start(bf16[16,64,256]{2,1,0:T(8,128)(2,1)} %get-tuple-element.20), calls=%async_computation | async-start | bytes 1048576 | tf_op jit(solution)/shard_map/all_to_all | solution.py:316
  17.6 4.4 %collective-permute-start = (s32[3,32]{1,0:T(4,128)S(1)}, s32[3,32]{1,0:T(4,128)S(1)}, u32[]{:S(2)}, u32[]{:S(2)}) collective-permute-start(s32[3,32]{1,0:T(4,128)S(1)} %get-tuple-element.18.mine_ref), channel_id=1, source_target_pairs={{0,16},{16,0},{1,17},{17,1},{2,18},{18,2},{3,19},{19,3},{4,20},{20... | collective-permute-start | bytes 1160 | tf_op jit(solution)/shard_map/ppermute | solution.py:319
  37.0 23.5 %collective-permute-start.5 = (bf16[8,144,128]{2,1,0:T(8,128)(2,1)S(1)}, bf16[8,144,128]{2,1,0:T(8,128)(2,1)S(1)}, u32[]{:S(2)}, u32[]{:S(2)}) collective-permute-start(bf16[8,144,128]{2,1,0:T(8,128)(2,1)S(1)} %attend_other.1), channel_id=1, source_target_pairs={{0,16},{16,0},{1,17},{17,1},{2,18},{18,2},{3,19},{19,3},{4,20},{20... | collective-permute-start | bytes 884744 | tf_op jit(solution)/shard_map/ppermute | solution.py:367
  39.3 9.5 %collective-permute-start.2 = (bf16[128,128]{1,0:T(8,128)(2,1)S(1)}, bf16[128,128]{1,0:T(8,128)(2,1)S(1)}, u32[]{:S(2)}, u32[]{:S(2)}) collective-permute-start(bf16[128,128]{1,0:T(8,128)(2,1)S(1)} %get-tuple-element.21), channel_id=1, source_target_pairs={{0,1},{8,0},{1,3},{9,2},{2,5},{10,4},{3,7},{11,6},{4,9},{12,8},{5,... | collective-permute-start | bytes 98312 | tf_op jit(solution)/shard_map/ppermute | solution.py:341
  44.8 9.4 %collective-permute-start.1 = (bf16[128,128]{1,0:T(8,128)(2,1)S(1)}, bf16[128,128]{1,0:T(8,128)(2,1)S(1)}, u32[]{:S(2)}, u32[]{:S(2)}) collective-permute-start(bf16[128,128]{1,0:T(8,128)(2,1)S(1)} %get-tuple-element.21), channel_id=1, source_target_pairs={{0,0},{8,1},{1,2},{9,3},{2,4},{10,5},{3,6},{11,7},{4,8},{12,9},{5,... | collective-permute-start | bytes 98312 | tf_op jit(solution)/shard_map/ppermute | solution.py:340
  60.5 33.8 %copy-start = (bf16[4096,256]{1,0:T(8,128)(2,1)S(1)}, bf16[4096,256]{1,0:T(8,128)(2,1)}, u32[]{:S(2)}) copy-start(bf16[4096,256]{1,0:T(8,128)(2,1)} %param.19) | copy-start | bytes 6291460
  88.5 7.0 %collective-permute-start.6 = (bf16[8,64,256]{2,1,0:T(8,128)(2,1)S(1)}, bf16[8,64,256]{2,1,0:T(8,128)(2,1)S(1)}, u32[]{:S(2)}, u32[]{:S(2)}) collective-permute-start(bf16[8,64,256]{2,1,0:T(8,128)(2,1)S(1)} %all_to_all.16.rows_ref), channel_id=1, source_target_pairs={{0,1},{1,0},{2,3},{3,2},{4,5},{5,4},{6,7},{7,6},{8,9},{9,8},{10,11... | collective-permute-start | bytes 786440 | tf_op jit(solution)/shard_map/ppermute | solution.py:376

commit v9 on v7

--- a/solution.py
+++ b/solution.py
@@ -25,18 +25,6 @@
         lane = lax.broadcasted_iota(jnp.int32, (rows, 128), 1) + start
         parts.append((tall == lane).astype(jnp.float32).astype(jnp.bfloat16))
     return jnp.concatenate(parts, axis=1)
-
-
-def residual_kernel(codes_ref, embed_hbm, out_ref, embed_ref, sem):
-    copy = pltpu.make_async_copy(embed_hbm, embed_ref, sem.at[0])
-    copy.start()
-    beams = codes_ref.shape[1]
-    hots = [one_hot_rows(codes_ref[level : level + 1], embed_ref.shape[1]) for level in range(codes_ref.shape[0])]
-    copy.wait()
-    for level, hot in enumerate(hots):
-        out_ref[level * beams : (level + 1) * beams] = jnp.dot(
-            hot, embed_ref[level], preferred_element_type=jnp.float32
-        )
 
 
 def look_kernel(codes_hbm, parents_hbm, query_hbm, out_ref, mine_ref, query_ref, sem):
@@ -59,12 +47,14 @@
 
 
 def generated_kernel(
-    meta_ref, mine_ref, other_ref, kv_hbm, lengths_hbm, holders_hbm, out_ref, live_ref, kv_ref, lengths_ref, holders_ref, sem
+    meta_ref, mine_ref, other_ref, kv_hbm, embed_hbm, lengths_hbm, holders_hbm, out_ref, residual_ref, live_ref,
+    kv_ref, embed_ref, lengths_ref, holders_ref, sem
 ):
     copies = [
         pltpu.make_async_copy(lengths_hbm, lengths_ref, sem.at[0]),
         pltpu.make_async_copy(holders_hbm, holders_ref, sem.at[1]),
         pltpu.make_async_copy(kv_hbm, kv_ref, sem.at[2]),
+        pltpu.make_async_copy(embed_hbm, embed_ref, sem.at[3]),
     ]
     for copy in copies:
         copy.start()
@@ -77,6 +67,9 @@
         copy.wait()
     for level, hot in enumerate(hots):
         found = jnp.dot(hot, kv_ref[level], preferred_element_type=jnp.float32).astype(jnp.bfloat16)
+        residual_ref[level * beams : (level + 1) * beams] = jnp.dot(
+            hot[:beams], embed_ref[level], preferred_element_type=jnp.float32
+        )
         for part, x in enumerate((meta_ref[3], 1 - meta_ref[3])):
             place = pl.ds(pl.multiple_of((x * levels + level) * beams, beams), beams)
             out_ref[place] = found[part * beams : (part + 1) * beams]
@@ -118,12 +111,13 @@
     return jnp.concatenate([jnp.transpose(values), jnp.ones((STAT, values.shape[0]), jnp.bfloat16)], axis=0)
 
 
-def queries_of(query_ref, head):
-    pieces = []
-    for x in range(2):
-        pair = query_ref[x * KEY_HEADS + head]
-        pieces += [pair[:, h * HEAD : (h + 1) * HEAD] for h in range(2)]
-    return jnp.concatenate(pieces, axis=0)
+def regroup_kernel(query_ref, out_ref):
+    heads, half = out_ref.shape[0], query_ref.shape[1]
+    for head in range(heads):
+        for x in range(2):
+            for h in range(2):
+                rows = slice((2 * x + h) * half, (2 * x + h + 1) * half)
+                out_ref[head, rows] = query_ref[x * heads + head, :, h * HEAD : (h + 1) * HEAD]
 
 
 def write(out_ref, head, sums, total, top):
@@ -138,7 +132,7 @@
     live_ref, query_ref, near_key, near_value, far_key, far_value, out_ref, score_ref, key_ref, value_ref, key_sem, value_sem
 ):
     heads, slots = key_ref.shape[0], key_ref.shape[1]
-    half = query_ref.shape[1]
+    half = query_ref.shape[1] // 4
     block_slots = slots // 2
     near_live, far_live = live_ref[0], live_ref[1]
     live = near_live + far_live
@@ -167,7 +161,7 @@
         lax.fori_loop(0, heads, begin, 0)
 
         def score(head, at):
-            scores = scores_of(key_ref[head], queries_of(query_ref, head))
+            scores = scores_of(key_ref[head], query_ref[head])
             if masked:
                 slot = lax.broadcasted_iota(jnp.int32, (slots, 1), 0)
                 allowed = (slot < near_live) | ((slot >= block_slots) & (slot < block_slots + far_live))
@@ -224,8 +218,8 @@
 def add_generated_kernel(
     meta_ref, query_ref, kv_ref, far_kv_ref, gen_value_ref, mine_ref, other_ref, before_ref, out_ref
 ):
-    half = query_ref.shape[1]
-    width = 4 * half
+    width = query_ref.shape[1]
+    half = width // 4
     head = meta_ref[2]
 
     @pl.when(head >= 0)
@@ -243,7 +237,7 @@
             pieces += [jnp.full_like(parents, -1), parents] * 2
         allowed = (row == own) | (row == jnp.concatenate(pieces, axis=1))
         keys = jnp.where(swapped, far_kv_ref[...], kv_ref[...])
-        scores = jnp.where(allowed, scores_of(keys, queries_of(query_ref, head)), DEAD)
+        scores = jnp.where(allowed, scores_of(keys, query_ref[head]), DEAD)
         before = jnp.concatenate([before_ref[x, head] for x in range(2)], axis=1)
         old_top, old_total = read_stats(before[HEAD:CHUNK])
         top = jnp.maximum(old_top, jnp.max(scores, axis=0, keepdims=True))
@@ -324,35 +318,27 @@
         scratch_shapes=[pltpu.VMEM(query_table.shape, bf16), dma((3,))],
     )(hbm(codes), hbm(parents[None]), hbm(query_table))
     queries = lax.all_to_all(query_rows, ("pair", "z"), split_axis=0, concat_axis=0, tiled=True)
-    residual = call(
-        residual_kernel,
-        array((half, width), f32),
-        "residual",
-        "vh",
-        4,
-        scratch_shapes=[pltpu.VMEM(embed_table.shape, bf16), dma((1,))],
-    )(codes, hbm(embed_table))
-
     mine, near_keys, near_values = lax.optimization_barrier((mine, history_keys[0], history_values[0]))
     other = lax.ppermute(mine, "pair", swap)
     far_keys = lax.ppermute(near_keys, "core", swap)
     far_values = lax.ppermute(near_values, "core", swap)
     gen_head = jnp.where(z < z_count // 2, 2 * z + jnp.bitwise_xor(core, pair), -1)
     meta = jnp.stack([lax.axis_index("grp"), pair * 2 * z_count + hist, gen_head, pair, jnp.int32(slots)]).astype(jnp.int32)
-    kv_rows, live = call(
+    kv_rows, residual, live = call(
         generated_kernel,
-        (array((rows, HEAD), bf16), array((2,), jnp.int32)),
+        (array((rows, HEAD), bf16), array((half, width), f32), array((2,), jnp.int32)),
         "generated",
-        "svvhhh",
+        "svvhhhh",
         4,
-        "vs",
+        "vvs",
         scratch_shapes=[
             pltpu.VMEM(kv_table.shape, bf16),
+            pltpu.VMEM(embed_table.shape, bf16),
             pltpu.SMEM(lengths.shape, jnp.int32),
             pltpu.SMEM(holders.shape, jnp.int32),
-            dma((3,)),
+            dma((4,)),
         ],
-    )(meta, mine, other, hbm(kv_table), hbm(lengths), hbm(holders))
+    )(meta, mine, other, hbm(kv_table), hbm(embed_table), hbm(lengths), hbm(holders))
     at = lambda p, k, c: (p * z_count + k) * 2 + c
     taken = [(p, k, c) for p in range(2) for k in range(z_count // 2) for c in range(2)]
     gen_values = lax.ppermute(
@@ -360,6 +346,15 @@
     )
     far_kv = lax.ppermute(kv_rows, ("pair", "z", "core"), [(at(1, k, 1 - c), at(1, k, c)) for p, k, c in taken if p])
 
+    queries, live = lax.optimization_barrier((queries, live))
+    queries = call(
+        regroup_kernel,
+        array((KEY_HEADS, 2 * rows, HEAD), bf16),
+        "regroup",
+        "v",
+        4,
+        cost_estimate=pl.CostEstimate(flops=0, bytes_accessed=44 * 10**6, transcendentals=0),
+    )(queries)
     partial_shape = (2, z_count, CHUNK, 2 * half)
     partials = call(
         attend_kernel,

time: 85.7 us -> 85.9 us (level)
  Pallas kernels: 16.1 us -> 8.79 us
  waiting for transfers between devices: 5.77 us -> 9.22 us
  blocking collectives: 37.7 us -> 41 us
    pallas_call x1, Pallas kernels: 7.31 us -> 0.92 us  [shards(): call(attend_kernel, array(partial_shape, bf16), 'attend', 'svhhaa', 24, s...]
    ppermute x1, waiting for transfers between devices: 0.01 us -> 3.32 us  [shards(): lax.ppermute(kv_rows, ('pair', 'z', 'core'), [(at(p, k + z_count // 2, c...]
    all_to_all x1, blocking collectives: 23.7 us -> 26.9 us  [shards(): lax.all_to_all(partials.reshape(shape), ('pair', 'z'), split_axis=0, conc...]
    pallas_call x2, Pallas kernels: 3.24 us -> 2.35 us  [the longest x1 2.26 us: shards(): call(generated_kernel, (array((rows, HEAD), bf16), array((half, width), f...]
  transfers between devices with their start and end apart: 7 -> 7, of which waited for: 2 -> 4; matrix products, arithmetic and copies ran while one was open for 0% -> 0% of each run, Pallas kernels for 13% -> 5%
where the time goes in v9:
time: 85.9 us; the launch traced here: 84.6 us
  blocking collectives  41 us (48%)
  starting transfers between devices  25.4 us (30%)
  waiting for transfers between devices  9.22 us (11%)
  Pallas kernels  8.79 us (10%)
    all_to_all x1, blocking collectives, shards(): lax.all_to_all(partials.reshape(shape), ('pair', 'z'), split_axis=0, conc...  26.9 us
    all_to_all x1, blocking collectives, shards(): lax.all_to_all(attention, 'z', split_axis=0, concat_axis=0, tiled=True)  14.1 us
    all_to_all x1, starting transfers between devices, shards(): lax.all_to_all(query_rows, ('pair', 'z'), split_axis=0, concat_axis=0, ti...  11.1 us
    all_to_all x1, waiting for transfers between devices, shards(): lax.all_to_all(query_rows, ('pair', 'z'), split_axis=0, concat_axis=0, ti...  4.59 us
    ppermute x1, starting transfers between devices, shards(): far_rows = lax.ppermute(near_rows, 'core', swap)  4.54 us
    ppermute x1, waiting for transfers between devices, shards(): lax.ppermute(kv_rows, ('pair', 'z', 'core'), [(at(p, k + z_count // 2, c...  3.32 us
    ppermute x1, starting transfers between devices, shards(): other = lax.ppermute(mine, 'pair', swap)  3.27 us
    ppermute x1, starting transfers between devices, shards(): far_keys = lax.ppermute(near_keys, 'core', swap)  2.59 us
  transfers between devices with their start and end apart: 7, of which 4 were waited for; matrix products, arithmetic and copies ran while one was open for 0% of the time, Pallas kernels for 5%

profile of v9, /device:TPU:57, one launch (start us, length us, event | category | flops | bytes accessed | tf_op | source)
XLA Modules:
  0.0 84.6 jit_solution(8927035270499378035)
XLA Ops:
  0.0 2.0 %look.1 = (bf16[16,64,256]{2,1,0:T(8,128)(2,1)}, s32[3,32]{1,0:T(4,128)S(1)}) custom-call(s32[2,32]{1,0:T(2,128)} %codes_hbm.1, s32[1,32]{1,0:T(1,128)} %bitcast.17, bf16[2,256,256]{2,1,0:T(8,128)(2,1)} %query_hbm.1), custom_call_target="tpu_custom_call" | custom-call | tf_op jit(solution)/shard_map/look/pallas_call | solution.py:311
  2.0 2.6 %collective-permute-start.3 = (bf16[1024,1024]{1,0:T(8,128)(2,1)}, bf16[1024,1024]{1,0:T(8,128)(2,1)S(1)}, u32[]{:S(2)}, u32[]{:S(2)}) collective-permute-start(bf16[1024,1024]{1,0:T(8,128)(2,1)} %bitcast.13), channel_id=1, source_target_pairs={{0,1},{1,0},{2,3},{3,2},{4,5},{5,4},{6,7},{7,6},{8,9},{9,8},{10,11... | collective-permute-start | bytes 6291464 | tf_op jit(solution)/shard_map/ppermute | solution.py:323
  4.6 1.9 %collective-permute-start.4 = (bf16[1024,1024]{1,0:T(8,128)(2,1)}, bf16[1024,1024]{1,0:T(8,128)(2,1)}, u32[]{:S(2)}, u32[]{:S(2)}) collective-permute-start(bf16[1024,1024]{1,0:T(8,128)(2,1)} %bitcast.15), channel_id=1, source_target_pairs={{0,1},{1,0},{2,3},{3,2},{4,5},{5,4},{6,7},{7,6},{8,9},{9,8},{10,11... | collective-permute-start | bytes 6291464 | tf_op jit(solution)/shard_map/ppermute | solution.py:324
  6.6 11.1 %all-to-all-start = ((bf16[16,64,256]{2,1,0:T(8,128)(2,1)}), bf16[16,64,256]{2,1,0:T(8,128)(2,1)S(1)}, u32[]{:S(2)}, u32[]{:S(2)}) async-start(bf16[16,64,256]{2,1,0:T(8,128)(2,1)} %get-tuple-element.15), calls=%async_computation | async-start | bytes 1048576 | tf_op jit(solution)/shard_map/all_to_all | solution.py:320
  17.6 3.3 %collective-permute-start = (s32[3,32]{1,0:T(4,128)S(1)}, s32[3,32]{1,0:T(4,128)S(1)}, u32[]{:S(2)}, u32[]{:S(2)}) collective-permute-start(s32[3,32]{1,0:T(4,128)S(1)} %get-tuple-element.17.mine_ref), channel_id=1, source_target_pairs={{0,16},{16,0},{1,17},{17,1},{2,18},{18,2},{3,19},{19,3},{4,20},{20... | collective-permute-start | bytes 1160 | tf_op jit(solution)/shard_map/ppermute | solution.py:322
  20.9 0.1 stack.19.meta_ref
  21.0 1.0 %collective-permute-done.other_ref = s32[3,32]{1,0:T(4,128)S(1)} collective-permute-done((s32[3,32]{1,0:T(4,128)S(1)}, s32[3,32]{1,0:T(4,128)S(1)}, u32[]{:S(2)}, u32[]{:S(2)}) %collective-permute-start) | collective-permute-done | bytes 416 | tf_op jit(solution)/shard_map/ppermute | solution.py:322
  22.0 2.3 %generated.1 = (bf16[128,128]{1,0:T(8,128)(2,1)S(1)}, f32[64,256]{1,0:T(8,128)S(1)}, s32[2]{0:T(128)S(1)}) custom-call(s32[5]{0:T(128)S(1)} %stack.19.meta_ref, s32[3,32]{1,0:T(4,128)S(1)} %get-tuple-element.17.mine_ref, s32[3,32]{1,0:T(4,128)S(1)} %collective-permute-done.other_ref, bf16[2,256,128]{2,1,0:T(8,128)(2,1)} %kv_hbm.1, ...), custom_call_target="tpu_custom_call" | custom-call | tf_op jit(solution)/shard_map/generated/pallas_call | solution.py:327
  24.3 0.7 collective-permute-start.1
  25.0 1.3 %collective-permute-start.2 = (bf16[128,128]{1,0:T(8,128)(2,1)S(1)}, bf16[128,128]{1,0:T(8,128)(2,1)S(1)}, u32[]{:S(2)}, u32[]{:S(2)}) collective-permute-start(bf16[128,128]{1,0:T(8,128)(2,1)S(1)} %get-tuple-element.20.kv_ref), channel_id=1, source_target_pairs={{8,0},{9,1},{10,2},{11,3},{12,4},{13,5},{14,6},{15,7},{25,16},{24,... | collective-permute-start | bytes 98312 | tf_op jit(solution)/shard_map/ppermute | solution.py:344
  26.3 4.6 %all-to-all-done.query_ref = bf16[16,64,256]{2,1,0:T(8,128)(2,1)S(1)} async-done(((bf16[16,64,256]{2,1,0:T(8,128)(2,1)}), bf16[16,64,256]{2,1,0:T(8,128)(2,1)S(1)}, u32[]{:S(2)}, u32[]{:S(2)}) %all-to-all-start) | async-done | bytes 524320 | tf_op jit(solution)/shard_map/all_to_all | solution.py:320
  30.9 0.1 regroup.1.query_ref
  31.0 0.0 collective-permute-done.3.far_key
  31.0 0.0 collective-permute-done.4.far_value
  31.0 0.9 %attend.1.before_ref = bf16[2,8,144,128]{3,2,1,0:T(8,128)(2,1)S(1)} custom-call(s32[2]{0:T(128)S(1)} %get-tuple-element.21.live_ref, bf16[8,256,128]{2,1,0:T(8,128)(2,1)S(1)} %regroup.1.query_ref, bf16[1024,1024]{1,0:T(8,128)(2,1)} %bitcast.14, bf16[1024,1024]{1,0:T(8,128)(2,1)} %bitcast.16, bf16[1024,1024]{1,0:T(8,128)(2,1)S(1)} %collective-permute-done.3.far_key, ...), custom_call_target="tpu_custom_call" | custom-call | flops 2147483648 | bytes 4194304 | tf_op jit(solution)/shard_map/attend/pallas_call | solution.py:359
  31.9 0.0 copy-start
  31.9 0.0 collective-permute-done.1.far_kv_ref
  31.9 3.3 %collective-permute-done.2.gen_value_ref = bf16[128,128]{1,0:T(8,128)(2,1)S(1)} collective-permute-done((bf16[128,128]{1,0:T(8,128)(2,1)S(1)}, bf16[128,128]{1,0:T(8,128)(2,1)S(1)}, u32[]{:S(2)}, u32[]{:S(2)}) %collective-permute-start.2) | collective-permute-done | bytes 32800 | tf_op jit(solution)/shard_map/ppermute | solution.py:344
  35.3 1.0 %add_generated.1 = bf16[2,8,144,128]{3,2,1,0:T(8,128)(2,1)S(1)} custom-call(s32[5]{0:T(128)S(1)} %stack.19.meta_ref, bf16[8,256,128]{2,1,0:T(8,128)(2,1)S(1)} %regroup.1.query_ref, bf16[128,128]{1,0:T(8,128)(2,1)S(1)} %get-tuple-element.20.kv_ref, bf16[128,128]{1,0:T(8,128)(2,1)S(1)} %collective-permute-done.1.far_kv_ref, ...), custom_call_target="tpu_custom_call", output_to_operand_aliasing={{}: (7, {})} | custom-call | tf_op jit(solution)/shard_map/add_generated/pallas_call | solution.py:378
  36.2 26.9 %all_to_all.15.parts_ref = bf16[16,144,128]{2,1,0:T(8,128)(2,1)S(1)} all-to-all(bf16[16,144,128]{2,1,0:T(8,128)(2,1)S(1)} %bitcast.12), channel_id=1, replica_groups=mesh['grp'=16,'pair'=2,'z'=8,'core'=2] {'pair','z'}, dimensions={0} | all-to-all | bytes 1179648 | tf_op jit(solution)/shard_map/all_to_all | solution.py:383
  63.2 0.2 combine.1
  63.4 14.1 %all_to_all.16.rows_ref = bf16[8,64,256]{2,1,0:T(8,128)(2,1)S(1)} all-to-all(bf16[8,64,256]{2,1,0:T(8,128)(2,1)S(1)} %combine.1), channel_id=1, replica_groups=mesh['grp'=16,'pair'=2,'z'=8,'core'=2] {'z'}, dimensions={0} | all-to-all | bytes 524288 | tf_op jit(solution)/shard_map/all_to_all | solution.py:385
  77.5 4.5 %collective-permute-start.5 = (bf16[8,64,256]{2,1,0:T(8,128)(2,1)S(1)}, bf16[8,64,256]{2,1,0:T(8,128)(2,1)S(1)}, u32[]{:S(2)}, u32[]{:S(2)}) collective-permute-start(bf16[8,64,256]{2,1,0:T(8,128)(2,1)S(1)} %all_to_all.16.rows_ref), channel_id=1, source_target_pairs={{0,1},{1,0},{2,3},{3,2},{4,5},{5,4},{6,7},{7,6},{8,9},{9,8},{10,11... | collective-permute-start | bytes 786440 | tf_op jit(solution)/shard_map/ppermute | solution.py:386
  82.0 0.0 copy-done
  82.0 0.9 %project_near.1.before_ref = f32[64,256]{1,0:T(8,128)S(1)} custom-call(s32[5]{0:T(128)S(1)} %stack.19.meta_ref, bf16[8,64,256]{2,1,0:T(8,128)(2,1)S(1)} %all_to_all.16.rows_ref, bf16[8,2,256,256]{3,2,1,0:T(8,128)(2,1)S(1)} %bitcast.10, f32[64,256]{1,0:T(8,128)S(1)} %get-tuple-element.24.before_ref), custom_call_target="tpu_custom_call" | custom-call | tf_op jit(solution)/shard_map/project_near/pallas_call | solution.py:388
  82.9 0.3 collective-permute-done.5.rows_ref
  83.1 1.5 %project_far.1 = bf16[64,256]{1,0:T(8,128)(2,1)} custom-call(s32[5]{0:T(128)S(1)} %stack.19.meta_ref, bf16[8,64,256]{2,1,0:T(8,128)(2,1)S(1)} %collective-permute-done.5.rows_ref, bf16[8,2,256,256]{3,2,1,0:T(8,128)(2,1)S(1)} %bitcast.11, f32[64,256]{1,0:T(8,128)S(1)} %project_near.1.before_ref), custom_call_target="tpu_custom_call" | custom-call | tf_op jit(solution)/shard_map/project_far/pallas_call | solution.py:391
Async XLA Ops:
  2.0 28.9 %collective-permute-start.3 = (bf16[1024,1024]{1,0:T(8,128)(2,1)}, bf16[1024,1024]{1,0:T(8,128)(2,1)S(1)}, u32[]{:S(2)}, u32[]{:S(2)}) collective-permute-start(bf16[1024,1024]{1,0:T(8,128)(2,1)} %bitcast.13), channel_id=1, source_target_pairs={{0,1},{1,0},{2,3},{3,2},{4,5},{5,4},{6,7},{7,6},{8,9},{9,8},{10,11... | collective-permute-start | bytes 6291464 | tf_op jit(solution)/shard_map/ppermute | solution.py:323
  4.6 26.4 %collective-permute-start.4 = (bf16[1024,1024]{1,0:T(8,128)(2,1)}, bf16[1024,1024]{1,0:T(8,128)(2,1)}, u32[]{:S(2)}, u32[]{:S(2)}) collective-permute-start(bf16[1024,1024]{1,0:T(8,128)(2,1)} %bitcast.15), channel_id=1, source_target_pairs={{0,1},{1,0},{2,3},{3,2},{4,5},{5,4},{6,7},{7,6},{8,9},{9,8},{10,11... | collective-permute-start | bytes 6291464 | tf_op jit(solution)/shard_map/ppermute | solution.py:324
  6.6 24.3 %all-to-all-start = ((bf16[16,64,256]{2,1,0:T(8,128)(2,1)}), bf16[16,64,256]{2,1,0:T(8,128)(2,1)S(1)}, u32[]{:S(2)}, u32[]{:S(2)}) async-start(bf16[16,64,256]{2,1,0:T(8,128)(2,1)} %get-tuple-element.15), calls=%async_computation | async-start | bytes 1048576 | tf_op jit(solution)/shard_map/all_to_all | solution.py:320
  17.6 4.4 %collective-permute-start = (s32[3,32]{1,0:T(4,128)S(1)}, s32[3,32]{1,0:T(4,128)S(1)}, u32[]{:S(2)}, u32[]{:S(2)}) collective-permute-start(s32[3,32]{1,0:T(4,128)S(1)} %get-tuple-element.17.mine_ref), channel_id=1, source_target_pairs={{0,16},{16,0},{1,17},{17,1},{2,18},{18,2},{3,19},{19,3},{4,20},{20... | collective-permute-start | bytes 1160 | tf_op jit(solution)/shard_map/ppermute | solution.py:322
  24.3 7.6 %collective-permute-start.1 = (bf16[128,128]{1,0:T(8,128)(2,1)S(1)}, bf16[128,128]{1,0:T(8,128)(2,1)S(1)}, u32[]{:S(2)}, u32[]{:S(2)}) collective-permute-start(bf16[128,128]{1,0:T(8,128)(2,1)S(1)} %get-tuple-element.20.kv_ref), channel_id=1, source_target_pairs={{17,16},{16,17},{19,18},{18,19},{21,20},{20,21},{23,22},{22,23},{4... | collective-permute-start | bytes 98312 | tf_op jit(solution)/shard_map/ppermute | solution.py:347
  25.0 10.3 %collective-permute-start.2 = (bf16[128,128]{1,0:T(8,128)(2,1)S(1)}, bf16[128,128]{1,0:T(8,128)(2,1)S(1)}, u32[]{:S(2)}, u32[]{:S(2)}) collective-permute-start(bf16[128,128]{1,0:T(8,128)(2,1)S(1)} %get-tuple-element.20.kv_ref), channel_id=1, source_target_pairs={{8,0},{9,1},{10,2},{11,3},{12,4},{13,5},{14,6},{15,7},{25,16},{24,... | collective-permute-start | bytes 98312 | tf_op jit(solution)/shard_map/ppermute | solution.py:344
  31.9 50.1 %copy-start = (bf16[4096,256]{1,0:T(8,128)(2,1)S(1)}, bf16[4096,256]{1,0:T(8,128)(2,1)}, u32[]{:S(2)}) copy-start(bf16[4096,256]{1,0:T(8,128)(2,1)} %param.19) | copy-start | bytes 6291460
  77.5 5.7 %collective-permute-start.5 = (bf16[8,64,256]{2,1,0:T(8,128)(2,1)S(1)}, bf16[8,64,256]{2,1,0:T(8,128)(2,1)S(1)}, u32[]{:S(2)}, u32[]{:S(2)}) collective-permute-start(bf16[8,64,256]{2,1,0:T(8,128)(2,1)S(1)} %all_to_all.16.rows_ref), channel_id=1, source_target_pairs={{0,1},{1,0},{2,3},{3,2},{4,5},{5,4},{6,7},{7,6},{8,9},{9,8},{10,11... | collective-permute-start | bytes 786440 | tf_op jit(solution)/shard_map/ppermute | solution.py:386

commit v10 on v9

--- a/solution.py
+++ b/solution.py
@@ -353,7 +353,7 @@
         "regroup",
         "v",
         4,
-        cost_estimate=pl.CostEstimate(flops=0, bytes_accessed=44 * 10**6, transcendentals=0),
+        cost_estimate=pl.CostEstimate(flops=10**12, bytes_accessed=0, transcendentals=0),
     )(queries)
     partial_shape = (2, z_count, CHUNK, 2 * half)
     partials = call(

time: 85.9 us -> 83.9 us (0.977)
  waiting for transfers between devices: 9.22 us -> 6.83 us
  starting transfers between devices: 25.4 us -> 26.8 us
  blocking collectives: 41 us -> 40 us
    all_to_all x1, waiting for transfers between devices: 4.59 us -> 0.05 us  [shards(): lax.all_to_all(query_rows, ('pair', 'z'), split_axis=0, concat_axis=0, ti...]
    ppermute x1, waiting for transfers between devices: 3.32 us -> 6.5 us  [shards(): lax.ppermute(kv_rows, ('pair', 'z', 'core'), [(at(p, k + z_count // 2, c...]
    ppermute x1, waiting for transfers between devices: 1.03 us -> 0.01 us  [shards(): other = lax.ppermute(mine, 'pair', swap)]
    all_to_all x1, blocking collectives: 26.9 us -> 25.9 us  [shards(): lax.all_to_all(partials.reshape(shape), ('pair', 'z'), split_axis=0, conc...]
  transfers between devices with their start and end apart: 7 -> 7, of which waited for: 4 -> 2; matrix products, arithmetic and copies ran while one was open for 0% -> 0% of each run, Pallas kernels for 5% -> 5%
where the time goes in v10:
time: 83.9 us; the launch traced here: 83 us
  blocking collectives  40 us (48%)
  starting transfers between devices  26.8 us (32%)
  Pallas kernels  9.17 us (11%)
  waiting for transfers between devices  6.83 us (8%)
    all_to_all x1, blocking collectives, shards(): lax.all_to_all(partials.reshape(shape), ('pair', 'z'), split_axis=0, conc...  25.9 us
    all_to_all x1, blocking collectives, shards(): lax.all_to_all(attention, 'z', split_axis=0, concat_axis=0, tiled=True)  14 us
    all_to_all x1, starting transfers between devices, shards(): lax.all_to_all(query_rows, ('pair', 'z'), split_axis=0, concat_axis=0, ti...  11.1 us
    ppermute x1, waiting for transfers between devices, shards(): lax.ppermute(kv_rows, ('pair', 'z', 'core'), [(at(p, k + z_count // 2, c...  6.5 us
    ppermute x1, starting transfers between devices, shards(): far_rows = lax.ppermute(near_rows, 'core', swap)  4.54 us
    ppermute x1, starting transfers between devices, shards(): far_keys = lax.ppermute(near_keys, 'core', swap)  3.43 us
    ppermute x1, starting transfers between devices, shards(): other = lax.ppermute(mine, 'pair', swap)  3.27 us
    pallas_call x1, Pallas kernels, shards(): call(generated_kernel, (array((rows, HEAD), bf16), array((half, width), f...  2.38 us
  transfers between devices with their start and end apart: 7, of which 2 were waited for; matrix products, arithmetic and copies ran while one was open for 0% of the time, Pallas kernels for 5%

profile of v10, /device:TPU:57, one launch (start us, length us, event | category | flops | bytes accessed | tf_op | source)
XLA Modules:
  0.0 83.0 jit_solution(10753086017626379258)
XLA Ops:
  0.0 2.0 %look.1 = (bf16[16,64,256]{2,1,0:T(8,128)(2,1)}, s32[3,32]{1,0:T(4,128)S(1)}) custom-call(s32[2,32]{1,0:T(2,128)} %codes_hbm.1, s32[1,32]{1,0:T(1,128)} %bitcast.17, bf16[2,256,256]{2,1,0:T(8,128)(2,1)} %query_hbm.1), custom_call_target="tpu_custom_call" | custom-call | tf_op jit(solution)/shard_map/look/pallas_call | solution.py:311
  2.0 11.1 %all-to-all-start = ((bf16[16,64,256]{2,1,0:T(8,128)(2,1)}), bf16[16,64,256]{2,1,0:T(8,128)(2,1)S(1)}, u32[]{:S(2)}, u32[]{:S(2)}) async-start(bf16[16,64,256]{2,1,0:T(8,128)(2,1)} %get-tuple-element.15), calls=%async_computation | async-start | bytes 1048576 | tf_op jit(solution)/shard_map/all_to_all | solution.py:320
  13.1 3.3 %collective-permute-start = (s32[3,32]{1,0:T(4,128)S(1)}, s32[3,32]{1,0:T(4,128)S(1)}, u32[]{:S(2)}, u32[]{:S(2)}) collective-permute-start(s32[3,32]{1,0:T(4,128)S(1)} %get-tuple-element.17.mine_ref), channel_id=1, source_target_pairs={{0,16},{16,0},{1,17},{17,1},{2,18},{18,2},{3,19},{19,3},{4,20},{20... | collective-permute-start | bytes 1160 | tf_op jit(solution)/shard_map/ppermute | solution.py:322
  16.4 3.4 %collective-permute-start.3 = (bf16[1024,1024]{1,0:T(8,128)(2,1)}, bf16[1024,1024]{1,0:T(8,128)(2,1)}, u32[]{:S(2)}, u32[]{:S(2)}) collective-permute-start(bf16[1024,1024]{1,0:T(8,128)(2,1)} %bitcast.13), channel_id=1, source_target_pairs={{0,1},{1,0},{2,3},{3,2},{4,5},{5,4},{6,7},{7,6},{8,9},{9,8},{10,11... | collective-permute-start | bytes 6291464 | tf_op jit(solution)/shard_map/ppermute | solution.py:323
  19.8 1.9 %collective-permute-start.4 = (bf16[1024,1024]{1,0:T(8,128)(2,1)}, bf16[1024,1024]{1,0:T(8,128)(2,1)}, u32[]{:S(2)}, u32[]{:S(2)}) collective-permute-start(bf16[1024,1024]{1,0:T(8,128)(2,1)} %bitcast.15), channel_id=1, source_target_pairs={{0,1},{1,0},{2,3},{3,2},{4,5},{5,4},{6,7},{7,6},{8,9},{9,8},{10,11... | collective-permute-start | bytes 6291464 | tf_op jit(solution)/shard_map/ppermute | solution.py:324
  21.8 0.1 stack.19.meta_ref
  21.9 0.0 collective-permute-done.other_ref
  21.9 2.4 %generated.1 = (bf16[128,128]{1,0:T(8,128)(2,1)}, f32[64,256]{1,0:T(8,128)S(1)}, s32[2]{0:T(128)S(1)}) custom-call(s32[5]{0:T(128)S(1)} %stack.19.meta_ref, s32[3,32]{1,0:T(4,128)S(1)} %get-tuple-element.17.mine_ref, s32[3,32]{1,0:T(4,128)S(1)} %collective-permute-done.other_ref, bf16[2,256,128]{2,1,0:T(8,128)(2,1)} %kv_hbm.1, ...), custom_call_target="tpu_custom_call" | custom-call | tf_op jit(solution)/shard_map/generated/pallas_call | solution.py:327
  24.2 1.3 %collective-permute-start.1 = (bf16[128,128]{1,0:T(8,128)(2,1)}, bf16[128,128]{1,0:T(8,128)(2,1)}, u32[]{:S(2)}, u32[]{:S(2)}) collective-permute-start(bf16[128,128]{1,0:T(8,128)(2,1)} %get-tuple-element.20.kv_ref), channel_id=1, source_target_pairs={{17,16},{16,17},{19,18},{18,19},{21,20},{20,21},{23,22},{22,23},{4... | collective-permute-start | bytes 98312 | tf_op jit(solution)/shard_map/ppermute | solution.py:347
  25.5 1.3 %collective-permute-start.2 = (bf16[128,128]{1,0:T(8,128)(2,1)}, bf16[128,128]{1,0:T(8,128)(2,1)}, u32[]{:S(2)}, u32[]{:S(2)}) collective-permute-start(bf16[128,128]{1,0:T(8,128)(2,1)} %get-tuple-element.20.kv_ref), channel_id=1, source_target_pairs={{8,0},{9,1},{10,2},{11,3},{12,4},{13,5},{14,6},{15,7},{25,16},{24,... | collective-permute-start | bytes 98312 | tf_op jit(solution)/shard_map/ppermute | solution.py:344
  26.8 0.0 all-to-all-done.query_ref
  26.9 0.1 regroup.1.query_ref
  27.0 0.0 collective-permute-done.3.far_key
  27.0 0.0 collective-permute-done.4.far_value
  27.0 0.9 %attend.1.before_ref = bf16[2,8,144,128]{3,2,1,0:T(8,128)(2,1)S(1)} custom-call(s32[2]{0:T(128)S(1)} %get-tuple-element.21.live_ref, bf16[8,256,128]{2,1,0:T(8,128)(2,1)S(1)} %regroup.1.query_ref, bf16[1024,1024]{1,0:T(8,128)(2,1)} %bitcast.14, bf16[1024,1024]{1,0:T(8,128)(2,1)} %bitcast.16, bf16[1024,1024]{1,0:T(8,128)(2,1)} %collective-permute-done.3.far_key, ...), custom_call_target="tpu_custom_call" | custom-call | flops 2147483648 | bytes 4194304 | tf_op jit(solution)/shard_map/attend/pallas_call | solution.py:359
  27.9 0.0 copy-start
  27.9 0.0 collective-permute-done.1.far_kv_ref
  27.9 6.5 %collective-permute-done.2.gen_value_ref = bf16[128,128]{1,0:T(8,128)(2,1)} collective-permute-done((bf16[128,128]{1,0:T(8,128)(2,1)}, bf16[128,128]{1,0:T(8,128)(2,1)}, u32[]{:S(2)}, u32[]{:S(2)}) %collective-permute-start.2) | collective-permute-done | bytes 32800 | tf_op jit(solution)/shard_map/ppermute | solution.py:344
  34.4 1.2 %add_generated.1 = bf16[2,8,144,128]{3,2,1,0:T(8,128)(2,1)S(1)} custom-call(s32[5]{0:T(128)S(1)} %stack.19.meta_ref, bf16[8,256,128]{2,1,0:T(8,128)(2,1)S(1)} %regroup.1.query_ref, bf16[128,128]{1,0:T(8,128)(2,1)} %get-tuple-element.20.kv_ref, bf16[128,128]{1,0:T(8,128)(2,1)} %collective-permute-done.1.far_kv_ref, ...), custom_call_target="tpu_custom_call", output_to_operand_aliasing={{}: (7, {})} | custom-call | tf_op jit(solution)/shard_map/add_generated/pallas_call | solution.py:378
  35.7 25.9 %all_to_all.15.parts_ref = bf16[16,144,128]{2,1,0:T(8,128)(2,1)S(1)} all-to-all(bf16[16,144,128]{2,1,0:T(8,128)(2,1)S(1)} %bitcast.12), channel_id=1, replica_groups=mesh['grp'=16,'pair'=2,'z'=8,'core'=2] {'pair','z'}, dimensions={0} | all-to-all | bytes 1179648 | tf_op jit(solution)/shard_map/all_to_all | solution.py:383
  61.6 0.2 combine.1
  61.8 14.0 %all_to_all.16.rows_ref = bf16[8,64,256]{2,1,0:T(8,128)(2,1)S(1)} all-to-all(bf16[8,64,256]{2,1,0:T(8,128)(2,1)S(1)} %combine.1), channel_id=1, replica_groups=mesh['grp'=16,'pair'=2,'z'=8,'core'=2] {'z'}, dimensions={0} | all-to-all | bytes 524288 | tf_op jit(solution)/shard_map/all_to_all | solution.py:385
  75.8 4.5 %collective-permute-start.5 = (bf16[8,64,256]{2,1,0:T(8,128)(2,1)S(1)}, bf16[8,64,256]{2,1,0:T(8,128)(2,1)S(1)}, u32[]{:S(2)}, u32[]{:S(2)}) collective-permute-start(bf16[8,64,256]{2,1,0:T(8,128)(2,1)S(1)} %all_to_all.16.rows_ref), channel_id=1, source_target_pairs={{0,1},{1,0},{2,3},{3,2},{4,5},{5,4},{6,7},{7,6},{8,9},{9,8},{10,11... | collective-permute-start | bytes 786440 | tf_op jit(solution)/shard_map/ppermute | solution.py:386
  80.4 0.0 copy-done
  80.4 0.9 %project_near.1.before_ref = f32[64,256]{1,0:T(8,128)S(1)} custom-call(s32[5]{0:T(128)S(1)} %stack.19.meta_ref, bf16[8,64,256]{2,1,0:T(8,128)(2,1)S(1)} %all_to_all.16.rows_ref, bf16[8,2,256,256]{3,2,1,0:T(8,128)(2,1)S(1)} %bitcast.10, f32[64,256]{1,0:T(8,128)S(1)} %get-tuple-element.24.before_ref), custom_call_target="tpu_custom_call" | custom-call | tf_op jit(solution)/shard_map/project_near/pallas_call | solution.py:388
  81.3 0.3 collective-permute-done.5.rows_ref
  81.5 1.5 %project_far.1 = bf16[64,256]{1,0:T(8,128)(2,1)} custom-call(s32[5]{0:T(128)S(1)} %stack.19.meta_ref, bf16[8,64,256]{2,1,0:T(8,128)(2,1)S(1)} %collective-permute-done.5.rows_ref, bf16[8,2,256,256]{3,2,1,0:T(8,128)(2,1)S(1)} %bitcast.11, f32[64,256]{1,0:T(8,128)S(1)} %project_near.1.before_ref), custom_call_target="tpu_custom_call" | custom-call | tf_op jit(solution)/shard_map/project_far/pallas_call | solution.py:391
Async XLA Ops:
  2.0 24.8 %all-to-all-start = ((bf16[16,64,256]{2,1,0:T(8,128)(2,1)}), bf16[16,64,256]{2,1,0:T(8,128)(2,1)S(1)}, u32[]{:S(2)}, u32[]{:S(2)}) async-start(bf16[16,64,256]{2,1,0:T(8,128)(2,1)} %get-tuple-element.15), calls=%async_computation | async-start | bytes 1048576 | tf_op jit(solution)/shard_map/all_to_all | solution.py:320
  13.1 8.7 %collective-permute-start = (s32[3,32]{1,0:T(4,128)S(1)}, s32[3,32]{1,0:T(4,128)S(1)}, u32[]{:S(2)}, u32[]{:S(2)}) collective-permute-start(s32[3,32]{1,0:T(4,128)S(1)} %get-tuple-element.17.mine_ref), channel_id=1, source_target_pairs={{0,16},{16,0},{1,17},{17,1},{2,18},{18,2},{3,19},{19,3},{4,20},{20... | collective-permute-start | bytes 1160 | tf_op jit(solution)/shard_map/ppermute | solution.py:322
  16.4 10.6 %collective-permute-start.3 = (bf16[1024,1024]{1,0:T(8,128)(2,1)}, bf16[1024,1024]{1,0:T(8,128)(2,1)}, u32[]{:S(2)}, u32[]{:S(2)}) collective-permute-start(bf16[1024,1024]{1,0:T(8,128)(2,1)} %bitcast.13), channel_id=1, source_target_pairs={{0,1},{1,0},{2,3},{3,2},{4,5},{5,4},{6,7},{7,6},{8,9},{9,8},{10,11... | collective-permute-start | bytes 6291464 | tf_op jit(solution)/shard_map/ppermute | solution.py:323
  19.8 7.1 %collective-permute-start.4 = (bf16[1024,1024]{1,0:T(8,128)(2,1)}, bf16[1024,1024]{1,0:T(8,128)(2,1)}, u32[]{:S(2)}, u32[]{:S(2)}) collective-permute-start(bf16[1024,1024]{1,0:T(8,128)(2,1)} %bitcast.15), channel_id=1, source_target_pairs={{0,1},{1,0},{2,3},{3,2},{4,5},{5,4},{6,7},{7,6},{8,9},{9,8},{10,11... | collective-permute-start | bytes 6291464 | tf_op jit(solution)/shard_map/ppermute | solution.py:324
  24.2 3.7 %collective-permute-start.1 = (bf16[128,128]{1,0:T(8,128)(2,1)}, bf16[128,128]{1,0:T(8,128)(2,1)}, u32[]{:S(2)}, u32[]{:S(2)}) collective-permute-start(bf16[128,128]{1,0:T(8,128)(2,1)} %get-tuple-element.20.kv_ref), channel_id=1, source_target_pairs={{17,16},{16,17},{19,18},{18,19},{21,20},{20,21},{23,22},{22,23},{4... | collective-permute-start | bytes 98312 | tf_op jit(solution)/shard_map/ppermute | solution.py:347
  25.5 8.9 %collective-permute-start.2 = (bf16[128,128]{1,0:T(8,128)(2,1)}, bf16[128,128]{1,0:T(8,128)(2,1)}, u32[]{:S(2)}, u32[]{:S(2)}) collective-permute-start(bf16[128,128]{1,0:T(8,128)(2,1)} %get-tuple-element.20.kv_ref), channel_id=1, source_target_pairs={{8,0},{9,1},{10,2},{11,3},{12,4},{13,5},{14,6},{15,7},{25,16},{24,... | collective-permute-start | bytes 98312 | tf_op jit(solution)/shard_map/ppermute | solution.py:344
  27.9 52.5 %copy-start = (bf16[4096,256]{1,0:T(8,128)(2,1)S(1)}, bf16[4096,256]{1,0:T(8,128)(2,1)}, u32[]{:S(2)}) copy-start(bf16[4096,256]{1,0:T(8,128)(2,1)} %param.19) | copy-start | bytes 6291460
  75.8 5.7 %collective-permute-start.5 = (bf16[8,64,256]{2,1,0:T(8,128)(2,1)S(1)}, bf16[8,64,256]{2,1,0:T(8,128)(2,1)S(1)}, u32[]{:S(2)}, u32[]{:S(2)}) collective-permute-start(bf16[8,64,256]{2,1,0:T(8,128)(2,1)S(1)} %all_to_all.16.rows_ref), channel_id=1, source_target_pairs={{0,1},{1,0},{2,3},{3,2},{4,5},{5,4},{6,7},{7,6},{8,9},{9,8},{10,11... | collective-permute-start | bytes 786440 | tf_op jit(solution)/shard_map/ppermute | solution.py:386

commit v11 on v10

--- a/solution.py
+++ b/solution.py
@@ -139,7 +139,8 @@
 
     def copies(head, keys):
         sources, target, sem = ((near_key, far_key), key_ref, key_sem) if keys else ((near_value, far_value), value_ref, value_sem)
-        lanes = pl.ds(pl.multiple_of(head * HEAD, HEAD), HEAD)
+        start = head * HEAD
+        lanes = pl.ds(start if isinstance(start, int) else pl.multiple_of(start, HEAD), HEAD)
         return [
             pltpu.make_async_copy(
                 source.at[:, lanes], target.at[head, pl.ds(block * block_slots, block_slots)], sem.at[block * heads + head]
@@ -152,13 +153,13 @@
             copy.wait()
 
     def attend(masked):
-        def begin(head, _):
-            for keys in (True, False):
-                for copy in copies(head, keys):
-                    copy.start()
-            return 0
-
-        lax.fori_loop(0, heads, begin, 0)
+        def begin(start, stop):
+            for head in range(start, stop):
+                for keys in (True, False):
+                    for copy in copies(head, keys):
+                        copy.start()
+
+        begin(0, 2)
 
         def score(head, at):
             scores = scores_of(key_ref[head], query_ref[head])
@@ -186,7 +187,9 @@
             return top
 
         wait(0, True)
-        top = lax.fori_loop(0, heads // 2 - 1, step, score(0, 0))
+        top = score(0, 0)
+        begin(2, heads)
+        top = lax.fori_loop(0, heads // 2 - 1, step, top)
         wait(heads - 1, True)
         wait(heads - 2, False)
         wait(heads - 1, False)
@@ -216,7 +219,7 @@
 
 
 def add_generated_kernel(
-    meta_ref, query_ref, kv_ref, far_kv_ref, gen_value_ref, mine_ref, other_ref, before_ref, out_ref
+    meta_ref, query_ref, kv_ref, far_kv_ref, gen_value_ref, mine_ref, other_ref, before_ref, out_ref, chunk_ref, sem
 ):
     width = query_ref.shape[1]
     half = width // 4
@@ -224,6 +227,10 @@
 
     @pl.when(head >= 0)
     def _():
+        loads = [pltpu.make_async_copy(before_ref.at[x, head], chunk_ref.at[x, 0], sem.at[x]) for x in range(2)]
+        stores = [pltpu.make_async_copy(chunk_ref.at[x, 0], out_ref.at[x, head], sem.at[2 + x]) for x in range(2)]
+        for copy in loads:
+            copy.start()
         values = extended(gen_value_ref[...])
         row = lax.broadcasted_iota(jnp.int32, (2 * half, width), 0)
         lane = lax.broadcasted_iota(jnp.int32, (2 * half, width), 1)
@@ -238,7 +245,9 @@
         allowed = (row == own) | (row == jnp.concatenate(pieces, axis=1))
         keys = jnp.where(swapped, far_kv_ref[...], kv_ref[...])
         scores = jnp.where(allowed, scores_of(keys, query_ref[head]), DEAD)
-        before = jnp.concatenate([before_ref[x, head] for x in range(2)], axis=1)
+        for copy in loads:
+            copy.wait()
+        before = jnp.concatenate([chunk_ref[x, 0] for x in range(2)], axis=1)
         old_top, old_total = read_stats(before[HEAD:CHUNK])
         top = jnp.maximum(old_top, jnp.max(scores, axis=0, keepdims=True))
         weights = jnp.where(allowed, jnp.exp2((scores - top) * EXP2_SCALE), 0.0)
@@ -248,7 +257,11 @@
         added = added + jnp.dot(values, low, preferred_element_type=jnp.float32)
         factor = jnp.exp2((old_top - top) * EXP2_SCALE)
         sums = before[0:HEAD].astype(jnp.float32) * factor + added[0:HEAD]
-        write(out_ref, head, sums, old_total * factor + added[HEAD : HEAD + 1], top)
+        write(chunk_ref, 0, sums, old_total * factor + added[HEAD : HEAD + 1], top)
+        for copy in stores:
+            copy.start()
+        for copy in stores:
+            copy.wait()
 
 
 def combine_kernel(parts_ref, out_ref):
@@ -376,7 +389,14 @@
         ),
     )(live, queries, hbm(near_keys), hbm(near_values), far_keys, far_values)
     partials = call(
-        add_generated_kernel, array(partial_shape, bf16), "add_generated", "svvvvvvv", 4, input_output_aliases={7: 0}
+        add_generated_kernel,
+        array(partial_shape, bf16),
+        "add_generated",
+        "svvvvvva",
+        4,
+        "a",
+        input_output_aliases={7: 0},
+        scratch_shapes=[pltpu.VMEM((2, 1, CHUNK, 2 * half), bf16), dma((4,))],
     )(meta, queries, kv_rows, far_kv, gen_values, mine, other, partials)
 
     shape = (2 * z_count, CHUNK, 2 * half)

time: 83.9 us -> 84.3 us (level)
  Pallas kernels: 9.17 us -> 17 us
  waiting for transfers between devices: 6.83 us -> 0.33 us
    pallas_call x1, Pallas kernels: 0.92 us -> 8.36 us  [shards(): call(attend_kernel, array(partial_shape, bf16), 'attend', 'svhhaa', 24, s...]
    ppermute x1, waiting for transfers between devices: 6.5 us -> 0.01 us  [shards(): lax.ppermute(kv_rows, ('pair', 'z', 'core'), [(at(p, k + z_count // 2, c...]
  transfers between devices with their start and end apart: 7 -> 7, of which waited for: 2 -> 1; matrix products, arithmetic and copies ran while one was open for 0% -> 0% of each run, Pallas kernels for 5% -> 14%
where the time goes in v11:
time: 84.3 us; the launch traced here: 83.8 us
  blocking collectives  39.4 us (47%)
  starting transfers between devices  26.8 us (32%)
  Pallas kernels  17 us (20%)
    all_to_all x1, blocking collectives, shards(): lax.all_to_all(partials.reshape(shape), ('pair', 'z'), split_axis=0, conc...  25.4 us
    all_to_all x1, blocking collectives, shards(): lax.all_to_all(attention, 'z', split_axis=0, concat_axis=0, tiled=True)  14 us
    all_to_all x1, starting transfers between devices, shards(): lax.all_to_all(query_rows, ('pair', 'z'), split_axis=0, concat_axis=0, ti...  11.1 us
    pallas_call x1, Pallas kernels, shards(): call(attend_kernel, array(partial_shape, bf16), 'attend', 'svhhaa', 24, s...  8.36 us
    ppermute x1, starting transfers between devices, shards(): far_rows = lax.ppermute(near_rows, 'core', swap)  4.54 us
    ppermute x1, starting transfers between devices, shards(): far_keys = lax.ppermute(near_keys, 'core', swap)  3.43 us
    ppermute x1, starting transfers between devices, shards(): other = lax.ppermute(mine, 'pair', swap)  3.27 us
    pallas_call x1, Pallas kernels, shards(): call(generated_kernel, (array((rows, HEAD), bf16), array((half, width), f...  2.38 us
  transfers between devices with their start and end apart: 7, of which 1 were waited for; matrix products, arithmetic and copies ran while one was open for 0% of the time, Pallas kernels for 14%

profile of v11, /device:TPU:57, one launch (start us, length us, event | category | flops | bytes accessed | tf_op | source)
XLA Modules:
  0.0 83.8 jit_solution(8773394802283388247)
XLA Ops:
  0.0 2.0 %look.1 = (bf16[16,64,256]{2,1,0:T(8,128)(2,1)}, s32[3,32]{1,0:T(4,128)S(1)}) custom-call(s32[2,32]{1,0:T(2,128)} %codes_hbm.1, s32[1,32]{1,0:T(1,128)} %bitcast.17, bf16[2,256,256]{2,1,0:T(8,128)(2,1)} %query_hbm.1), custom_call_target="tpu_custom_call" | custom-call | tf_op jit(solution)/shard_map/look/pallas_call | solution.py:324
  2.0 11.1 %all-to-all-start = ((bf16[16,64,256]{2,1,0:T(8,128)(2,1)}), bf16[16,64,256]{2,1,0:T(8,128)(2,1)S(1)}, u32[]{:S(2)}, u32[]{:S(2)}) async-start(bf16[16,64,256]{2,1,0:T(8,128)(2,1)} %get-tuple-element.15), calls=%async_computation | async-start | bytes 1048576 | tf_op jit(solution)/shard_map/all_to_all | solution.py:333
  13.1 3.3 %collective-permute-start = (s32[3,32]{1,0:T(4,128)S(1)}, s32[3,32]{1,0:T(4,128)S(1)}, u32[]{:S(2)}, u32[]{:S(2)}) collective-permute-start(s32[3,32]{1,0:T(4,128)S(1)} %get-tuple-element.17.mine_ref), channel_id=1, source_target_pairs={{0,16},{16,0},{1,17},{17,1},{2,18},{18,2},{3,19},{19,3},{4,20},{20... | collective-permute-start | bytes 1160 | tf_op jit(solution)/shard_map/ppermute | solution.py:335
  16.4 3.4 %collective-permute-start.3 = (bf16[1024,1024]{1,0:T(8,128)(2,1)}, bf16[1024,1024]{1,0:T(8,128)(2,1)}, u32[]{:S(2)}, u32[]{:S(2)}) collective-permute-start(bf16[1024,1024]{1,0:T(8,128)(2,1)} %bitcast.13), channel_id=1, source_target_pairs={{0,1},{1,0},{2,3},{3,2},{4,5},{5,4},{6,7},{7,6},{8,9},{9,8},{10,11... | collective-permute-start | bytes 6291464 | tf_op jit(solution)/shard_map/ppermute | solution.py:336
  19.8 1.9 %collective-permute-start.4 = (bf16[1024,1024]{1,0:T(8,128)(2,1)}, bf16[1024,1024]{1,0:T(8,128)(2,1)}, u32[]{:S(2)}, u32[]{:S(2)}) collective-permute-start(bf16[1024,1024]{1,0:T(8,128)(2,1)} %bitcast.15), channel_id=1, source_target_pairs={{0,1},{1,0},{2,3},{3,2},{4,5},{5,4},{6,7},{7,6},{8,9},{9,8},{10,11... | collective-permute-start | bytes 6291464 | tf_op jit(solution)/shard_map/ppermute | solution.py:337
  21.8 0.1 stack.19.meta_ref
  21.9 0.0 collective-permute-done.other_ref
  21.9 2.4 %generated.1 = (bf16[128,128]{1,0:T(8,128)(2,1)}, f32[64,256]{1,0:T(8,128)S(1)}, s32[2]{0:T(128)S(1)}) custom-call(s32[5]{0:T(128)S(1)} %stack.19.meta_ref, s32[3,32]{1,0:T(4,128)S(1)} %get-tuple-element.17.mine_ref, s32[3,32]{1,0:T(4,128)S(1)} %collective-permute-done.other_ref, bf16[2,256,128]{2,1,0:T(8,128)(2,1)} %kv_hbm.1, ...), custom_call_target="tpu_custom_call" | custom-call | tf_op jit(solution)/shard_map/generated/pallas_call | solution.py:340
  24.2 1.3 %collective-permute-start.1 = (bf16[128,128]{1,0:T(8,128)(2,1)}, bf16[128,128]{1,0:T(8,128)(2,1)}, u32[]{:S(2)}, u32[]{:S(2)}) collective-permute-start(bf16[128,128]{1,0:T(8,128)(2,1)} %get-tuple-element.20.kv_ref), channel_id=1, source_target_pairs={{17,16},{16,17},{19,18},{18,19},{21,20},{20,21},{23,22},{22,23},{4... | collective-permute-start | bytes 98312 | tf_op jit(solution)/shard_map/ppermute | solution.py:360
  25.5 1.3 %collective-permute-start.2 = (bf16[128,128]{1,0:T(8,128)(2,1)}, bf16[128,128]{1,0:T(8,128)(2,1)}, u32[]{:S(2)}, u32[]{:S(2)}) collective-permute-start(bf16[128,128]{1,0:T(8,128)(2,1)} %get-tuple-element.20.kv_ref), channel_id=1, source_target_pairs={{8,0},{9,1},{10,2},{11,3},{12,4},{13,5},{14,6},{15,7},{25,16},{24,... | collective-permute-start | bytes 98312 | tf_op jit(solution)/shard_map/ppermute | solution.py:357
  26.8 0.0 all-to-all-done.query_ref
  26.9 0.1 regroup.1.query_ref
  27.0 0.0 collective-permute-done.3.far_key
  27.0 0.0 collective-permute-done.4.far_value
  27.0 8.4 %attend.1.before_ref = bf16[2,8,144,128]{3,2,1,0:T(8,128)(2,1)S(1)} custom-call(s32[2]{0:T(128)S(1)} %get-tuple-element.21.live_ref, bf16[8,256,128]{2,1,0:T(8,128)(2,1)S(1)} %regroup.1.query_ref, bf16[1024,1024]{1,0:T(8,128)(2,1)} %bitcast.14, bf16[1024,1024]{1,0:T(8,128)(2,1)} %bitcast.16, bf16[1024,1024]{1,0:T(8,128)(2,1)} %collective-permute-done.3.far_key, ...), custom_call_target="tpu_custom_call" | custom-call | flops 2147483648 | bytes 4194304 | tf_op jit(solution)/shard_map/attend/pallas_call | solution.py:372
  35.3 0.0 copy-start
  35.3 0.0 collective-permute-done.1.far_kv_ref
  35.4 0.0 collective-permute-done.2.gen_value_ref
  35.4 1.6 %add_generated.1 = bf16[2,8,144,128]{3,2,1,0:T(8,128)(2,1)S(1)} custom-call(s32[5]{0:T(128)S(1)} %stack.19.meta_ref, bf16[8,256,128]{2,1,0:T(8,128)(2,1)S(1)} %regroup.1.query_ref, bf16[128,128]{1,0:T(8,128)(2,1)} %get-tuple-element.20.kv_ref, bf16[128,128]{1,0:T(8,128)(2,1)} %collective-permute-done.1.far_kv_ref, ...), custom_call_target="tpu_custom_call", output_to_operand_aliasing={{}: (7, {})} | custom-call | tf_op jit(solution)/shard_map/add_generated/pallas_call | solution.py:391
  37.0 25.4 %all_to_all.15.parts_ref = bf16[16,144,128]{2,1,0:T(8,128)(2,1)S(1)} all-to-all(bf16[16,144,128]{2,1,0:T(8,128)(2,1)S(1)} %bitcast.12), channel_id=1, replica_groups=mesh['grp'=16,'pair'=2,'z'=8,'core'=2] {'pair','z'}, dimensions={0} | all-to-all | bytes 1179648 | tf_op jit(solution)/shard_map/all_to_all | solution.py:403
  62.3 0.2 combine.1
  62.6 14.0 %all_to_all.16.rows_ref = bf16[8,64,256]{2,1,0:T(8,128)(2,1)S(1)} all-to-all(bf16[8,64,256]{2,1,0:T(8,128)(2,1)S(1)} %combine.1), channel_id=1, replica_groups=mesh['grp'=16,'pair'=2,'z'=8,'core'=2] {'z'}, dimensions={0} | all-to-all | bytes 524288 | tf_op jit(solution)/shard_map/all_to_all | solution.py:405
  76.6 4.5 %collective-permute-start.5 = (bf16[8,64,256]{2,1,0:T(8,128)(2,1)S(1)}, bf16[8,64,256]{2,1,0:T(8,128)(2,1)S(1)}, u32[]{:S(2)}, u32[]{:S(2)}) collective-permute-start(bf16[8,64,256]{2,1,0:T(8,128)(2,1)S(1)} %all_to_all.16.rows_ref), channel_id=1, source_target_pairs={{0,1},{1,0},{2,3},{3,2},{4,5},{5,4},{6,7},{7,6},{8,9},{9,8},{10,11... | collective-permute-start | bytes 786440 | tf_op jit(solution)/shard_map/ppermute | solution.py:406
  81.2 0.0 copy-done
  81.2 0.8 %project_near.1.before_ref = f32[64,256]{1,0:T(8,128)S(1)} custom-call(s32[5]{0:T(128)S(1)} %stack.19.meta_ref, bf16[8,64,256]{2,1,0:T(8,128)(2,1)S(1)} %all_to_all.16.rows_ref, bf16[8,2,256,256]{3,2,1,0:T(8,128)(2,1)S(1)} %bitcast.10, f32[64,256]{1,0:T(8,128)S(1)} %get-tuple-element.24.before_ref), custom_call_target="tpu_custom_call" | custom-call | tf_op jit(solution)/shard_map/project_near/pallas_call | solution.py:408
  82.0 0.3 collective-permute-done.5.rows_ref
  82.3 1.5 %project_far.1 = bf16[64,256]{1,0:T(8,128)(2,1)} custom-call(s32[5]{0:T(128)S(1)} %stack.19.meta_ref, bf16[8,64,256]{2,1,0:T(8,128)(2,1)S(1)} %collective-permute-done.5.rows_ref, bf16[8,2,256,256]{3,2,1,0:T(8,128)(2,1)S(1)} %bitcast.11, f32[64,256]{1,0:T(8,128)S(1)} %project_near.1.before_ref), custom_call_target="tpu_custom_call" | custom-call | tf_op jit(solution)/shard_map/project_far/pallas_call | solution.py:411
Async XLA Ops:
  2.0 24.8 %all-to-all-start = ((bf16[16,64,256]{2,1,0:T(8,128)(2,1)}), bf16[16,64,256]{2,1,0:T(8,128)(2,1)S(1)}, u32[]{:S(2)}, u32[]{:S(2)}) async-start(bf16[16,64,256]{2,1,0:T(8,128)(2,1)} %get-tuple-element.15), calls=%async_computation | async-start | bytes 1048576 | tf_op jit(solution)/shard_map/all_to_all | solution.py:333
  13.1 8.7 %collective-permute-start = (s32[3,32]{1,0:T(4,128)S(1)}, s32[3,32]{1,0:T(4,128)S(1)}, u32[]{:S(2)}, u32[]{:S(2)}) collective-permute-start(s32[3,32]{1,0:T(4,128)S(1)} %get-tuple-element.17.mine_ref), channel_id=1, source_target_pairs={{0,16},{16,0},{1,17},{17,1},{2,18},{18,2},{3,19},{19,3},{4,20},{20... | collective-permute-start | bytes 1160 | tf_op jit(solution)/shard_map/ppermute | solution.py:335
  16.4 10.6 %collective-permute-start.3 = (bf16[1024,1024]{1,0:T(8,128)(2,1)}, bf16[1024,1024]{1,0:T(8,128)(2,1)}, u32[]{:S(2)}, u32[]{:S(2)}) collective-permute-start(bf16[1024,1024]{1,0:T(8,128)(2,1)} %bitcast.13), channel_id=1, source_target_pairs={{0,1},{1,0},{2,3},{3,2},{4,5},{5,4},{6,7},{7,6},{8,9},{9,8},{10,11... | collective-permute-start | bytes 6291464 | tf_op jit(solution)/shard_map/ppermute | solution.py:336
  19.8 7.1 %collective-permute-start.4 = (bf16[1024,1024]{1,0:T(8,128)(2,1)}, bf16[1024,1024]{1,0:T(8,128)(2,1)}, u32[]{:S(2)}, u32[]{:S(2)}) collective-permute-start(bf16[1024,1024]{1,0:T(8,128)(2,1)} %bitcast.15), channel_id=1, source_target_pairs={{0,1},{1,0},{2,3},{3,2},{4,5},{5,4},{6,7},{7,6},{8,9},{9,8},{10,11... | collective-permute-start | bytes 6291464 | tf_op jit(solution)/shard_map/ppermute | solution.py:337
  24.2 11.1 %collective-permute-start.1 = (bf16[128,128]{1,0:T(8,128)(2,1)}, bf16[128,128]{1,0:T(8,128)(2,1)}, u32[]{:S(2)}, u32[]{:S(2)}) collective-permute-start(bf16[128,128]{1,0:T(8,128)(2,1)} %get-tuple-element.20.kv_ref), channel_id=1, source_target_pairs={{17,16},{16,17},{19,18},{18,19},{21,20},{20,21},{23,22},{22,23},{4... | collective-permute-start | bytes 98312 | tf_op jit(solution)/shard_map/ppermute | solution.py:360
  25.5 9.8 %collective-permute-start.2 = (bf16[128,128]{1,0:T(8,128)(2,1)}, bf16[128,128]{1,0:T(8,128)(2,1)}, u32[]{:S(2)}, u32[]{:S(2)}) collective-permute-start(bf16[128,128]{1,0:T(8,128)(2,1)} %get-tuple-element.20.kv_ref), channel_id=1, source_target_pairs={{8,0},{9,1},{10,2},{11,3},{12,4},{13,5},{14,6},{15,7},{25,16},{24,... | collective-permute-start | bytes 98312 | tf_op jit(solution)/shard_map/ppermute | solution.py:357
  35.3 45.8 %copy-start = (bf16[4096,256]{1,0:T(8,128)(2,1)S(1)}, bf16[4096,256]{1,0:T(8,128)(2,1)}, u32[]{:S(2)}) copy-start(bf16[4096,256]{1,0:T(8,128)(2,1)} %param.19) | copy-start | bytes 6291460
  76.6 5.7 %collective-permute-start.5 = (bf16[8,64,256]{2,1,0:T(8,128)(2,1)S(1)}, bf16[8,64,256]{2,1,0:T(8,128)(2,1)S(1)}, u32[]{:S(2)}, u32[]{:S(2)}) collective-permute-start(bf16[8,64,256]{2,1,0:T(8,128)(2,1)S(1)} %all_to_all.16.rows_ref), channel_id=1, source_target_pairs={{0,1},{1,0},{2,3},{3,2},{4,5},{5,4},{6,7},{7,6},{8,9},{9,8},{10,11... | collective-permute-start | bytes 786440 | tf_op jit(solution)/shard_map/ppermute | solution.py:406

commit v12 on v10

--- a/solution.py
+++ b/solution.py
@@ -216,7 +216,7 @@
 
 
 def add_generated_kernel(
-    meta_ref, query_ref, kv_ref, far_kv_ref, gen_value_ref, mine_ref, other_ref, before_ref, out_ref
+    meta_ref, query_ref, kv_ref, far_kv_ref, gen_value_ref, mine_ref, other_ref, before_ref, out_ref, own_query_ref, sem
 ):
     width = query_ref.shape[1]
     half = width // 4
@@ -224,6 +224,8 @@
 
     @pl.when(head >= 0)
     def _():
+        copy = pltpu.make_async_copy(query_ref.at[head], own_query_ref, sem.at[0])
+        copy.start()
         values = extended(gen_value_ref[...])
         row = lax.broadcasted_iota(jnp.int32, (2 * half, width), 0)
         lane = lax.broadcasted_iota(jnp.int32, (2 * half, width), 1)
@@ -237,7 +239,8 @@
             pieces += [jnp.full_like(parents, -1), parents] * 2
         allowed = (row == own) | (row == jnp.concatenate(pieces, axis=1))
         keys = jnp.where(swapped, far_kv_ref[...], kv_ref[...])
-        scores = jnp.where(allowed, scores_of(keys, query_ref[head]), DEAD)
+        copy.wait()
+        scores = jnp.where(allowed, scores_of(keys, own_query_ref[...]), DEAD)
         before = jnp.concatenate([before_ref[x, head] for x in range(2)], axis=1)
         old_top, old_total = read_stats(before[HEAD:CHUNK])
         top = jnp.maximum(old_top, jnp.max(scores, axis=0, keepdims=True))
@@ -376,7 +379,13 @@
         ),
     )(live, queries, hbm(near_keys), hbm(near_values), far_keys, far_values)
     partials = call(
-        add_generated_kernel, array(partial_shape, bf16), "add_generated", "svvvvvvv", 4, input_output_aliases={7: 0}
+        add_generated_kernel,
+        array(partial_shape, bf16),
+        "add_generated",
+        "savvvvvv",
+        4,
+        input_output_aliases={7: 0},
+        scratch_shapes=[pltpu.VMEM((2 * rows, HEAD), bf16), dma((1,))],
     )(meta, queries, kv_rows, far_kv, gen_values, mine, other, partials)
 
     shape = (2 * z_count, CHUNK, 2 * half)

time: 83.9 us -> 84.2 us (level)
  Pallas kernels: 9.17 us -> 16 us
  waiting for transfers between devices: 6.83 us -> 0.33 us
    pallas_call x1, Pallas kernels: 0.92 us -> 7.42 us  [shards(): call(attend_kernel, array(partial_shape, bf16), 'attend', 'svhhaa', 24, s...]
    ppermute x1, waiting for transfers between devices: 6.5 us -> 0.01 us  [shards(): lax.ppermute(kv_rows, ('pair', 'z', 'core'), [(at(p, k + z_count // 2, c...]
  transfers between devices with their start and end apart: 7 -> 7, of which waited for: 2 -> 1; matrix products, arithmetic and copies ran while one was open for 0% -> 0% of each run, Pallas kernels for 5% -> 13%
where the time goes in v12:
time: 84.2 us; the launch traced here: 83 us
  blocking collectives  39.6 us (47%)
  starting transfers between devices  26.8 us (32%)
  Pallas kernels  16 us (19%)
    all_to_all x1, blocking collectives, shards(): lax.all_to_all(partials.reshape(shape), ('pair', 'z'), split_axis=0, conc...  25.6 us
    all_to_all x1, blocking collectives, shards(): lax.all_to_all(attention, 'z', split_axis=0, concat_axis=0, tiled=True)  14 us
    all_to_all x1, starting transfers between devices, shards(): lax.all_to_all(query_rows, ('pair', 'z'), split_axis=0, concat_axis=0, ti...  11.1 us
    pallas_call x1, Pallas kernels, shards(): call(attend_kernel, array(partial_shape, bf16), 'attend', 'svhhaa', 24, s...  7.42 us
    ppermute x1, starting transfers between devices, shards(): far_rows = lax.ppermute(near_rows, 'core', swap)  4.54 us
    ppermute x1, starting transfers between devices, shards(): far_keys = lax.ppermute(near_keys, 'core', swap)  3.43 us
    ppermute x1, starting transfers between devices, shards(): other = lax.ppermute(mine, 'pair', swap)  3.27 us
    pallas_call x1, Pallas kernels, shards(): call(generated_kernel, (array((rows, HEAD), bf16), array((half, width), f...  2.38 us
  transfers between devices with their start and end apart: 7, of which 1 were waited for; matrix products, arithmetic and copies ran while one was open for 0% of the time, Pallas kernels for 13%

profile of v12, /device:TPU:57, one launch (start us, length us, event | category | flops | bytes accessed | tf_op | source)
XLA Modules:
  0.0 83.0 jit_solution(2237191602128782796)
XLA Ops:
  0.0 2.0 %look.1 = (bf16[16,64,256]{2,1,0:T(8,128)(2,1)}, s32[3,32]{1,0:T(4,128)S(1)}) custom-call(s32[2,32]{1,0:T(2,128)} %codes_hbm.1, s32[1,32]{1,0:T(1,128)} %bitcast.17, bf16[2,256,256]{2,1,0:T(8,128)(2,1)} %query_hbm.1), custom_call_target="tpu_custom_call" | custom-call | tf_op jit(solution)/shard_map/look/pallas_call | solution.py:314
  2.0 11.1 %all-to-all-start = ((bf16[16,64,256]{2,1,0:T(8,128)(2,1)}), bf16[16,64,256]{2,1,0:T(8,128)(2,1)S(1)}, u32[]{:S(2)}, u32[]{:S(2)}) async-start(bf16[16,64,256]{2,1,0:T(8,128)(2,1)} %get-tuple-element.15), calls=%async_computation | async-start | bytes 1048576 | tf_op jit(solution)/shard_map/all_to_all | solution.py:323
  13.1 3.3 %collective-permute-start = (s32[3,32]{1,0:T(4,128)S(1)}, s32[3,32]{1,0:T(4,128)S(1)}, u32[]{:S(2)}, u32[]{:S(2)}) collective-permute-start(s32[3,32]{1,0:T(4,128)S(1)} %get-tuple-element.17.mine_ref), channel_id=1, source_target_pairs={{0,16},{16,0},{1,17},{17,1},{2,18},{18,2},{3,19},{19,3},{4,20},{20... | collective-permute-start | bytes 1160 | tf_op jit(solution)/shard_map/ppermute | solution.py:325
  16.4 3.4 %collective-permute-start.3 = (bf16[1024,1024]{1,0:T(8,128)(2,1)}, bf16[1024,1024]{1,0:T(8,128)(2,1)}, u32[]{:S(2)}, u32[]{:S(2)}) collective-permute-start(bf16[1024,1024]{1,0:T(8,128)(2,1)} %bitcast.13), channel_id=1, source_target_pairs={{0,1},{1,0},{2,3},{3,2},{4,5},{5,4},{6,7},{7,6},{8,9},{9,8},{10,11... | collective-permute-start | bytes 6291464 | tf_op jit(solution)/shard_map/ppermute | solution.py:326
  19.8 1.9 %collective-permute-start.4 = (bf16[1024,1024]{1,0:T(8,128)(2,1)}, bf16[1024,1024]{1,0:T(8,128)(2,1)}, u32[]{:S(2)}, u32[]{:S(2)}) collective-permute-start(bf16[1024,1024]{1,0:T(8,128)(2,1)} %bitcast.15), channel_id=1, source_target_pairs={{0,1},{1,0},{2,3},{3,2},{4,5},{5,4},{6,7},{7,6},{8,9},{9,8},{10,11... | collective-permute-start | bytes 6291464 | tf_op jit(solution)/shard_map/ppermute | solution.py:327
  21.8 0.1 stack.19.meta_ref
  21.9 0.0 collective-permute-done.other_ref
  21.9 2.4 %generated.1 = (bf16[128,128]{1,0:T(8,128)(2,1)}, f32[64,256]{1,0:T(8,128)S(1)}, s32[2]{0:T(128)S(1)}) custom-call(s32[5]{0:T(128)S(1)} %stack.19.meta_ref, s32[3,32]{1,0:T(4,128)S(1)} %get-tuple-element.17.mine_ref, s32[3,32]{1,0:T(4,128)S(1)} %collective-permute-done.other_ref, bf16[2,256,128]{2,1,0:T(8,128)(2,1)} %kv_hbm.1, ...), custom_call_target="tpu_custom_call" | custom-call | tf_op jit(solution)/shard_map/generated/pallas_call | solution.py:330
  24.2 1.3 %collective-permute-start.1 = (bf16[128,128]{1,0:T(8,128)(2,1)}, bf16[128,128]{1,0:T(8,128)(2,1)}, u32[]{:S(2)}, u32[]{:S(2)}) collective-permute-start(bf16[128,128]{1,0:T(8,128)(2,1)} %get-tuple-element.20.kv_ref), channel_id=1, source_target_pairs={{17,16},{16,17},{19,18},{18,19},{21,20},{20,21},{23,22},{22,23},{4... | collective-permute-start | bytes 98312 | tf_op jit(solution)/shard_map/ppermute | solution.py:350
  25.5 1.3 %collective-permute-start.2 = (bf16[128,128]{1,0:T(8,128)(2,1)}, bf16[128,128]{1,0:T(8,128)(2,1)}, u32[]{:S(2)}, u32[]{:S(2)}) collective-permute-start(bf16[128,128]{1,0:T(8,128)(2,1)} %get-tuple-element.20.kv_ref), channel_id=1, source_target_pairs={{8,0},{9,1},{10,2},{11,3},{12,4},{13,5},{14,6},{15,7},{25,16},{24,... | collective-permute-start | bytes 98312 | tf_op jit(solution)/shard_map/ppermute | solution.py:347
  26.8 0.0 all-to-all-done.query_ref
  26.9 0.1 regroup.1.query_ref
  27.0 0.0 collective-permute-done.3.far_key
  27.0 0.0 collective-permute-done.4.far_value
  27.0 7.4 %attend.1.before_ref = bf16[2,8,144,128]{3,2,1,0:T(8,128)(2,1)S(1)} custom-call(s32[2]{0:T(128)S(1)} %get-tuple-element.21.live_ref, bf16[8,256,128]{2,1,0:T(8,128)(2,1)S(1)} %regroup.1.query_ref, bf16[1024,1024]{1,0:T(8,128)(2,1)} %bitcast.14, bf16[1024,1024]{1,0:T(8,128)(2,1)} %bitcast.16, bf16[1024,1024]{1,0:T(8,128)(2,1)} %collective-permute-done.3.far_key, ...), custom_call_target="tpu_custom_call" | custom-call | flops 2147483648 | bytes 4194304 | tf_op jit(solution)/shard_map/attend/pallas_call | solution.py:362
  34.4 0.0 copy-start
  34.4 0.0 collective-permute-done.1.far_kv_ref
  34.4 0.0 collective-permute-done.2.gen_value_ref
  34.4 1.6 %add_generated.1 = bf16[2,8,144,128]{3,2,1,0:T(8,128)(2,1)S(1)} custom-call(s32[5]{0:T(128)S(1)} %stack.19.meta_ref, bf16[8,256,128]{2,1,0:T(8,128)(2,1)S(1)} %regroup.1.query_ref, bf16[128,128]{1,0:T(8,128)(2,1)} %get-tuple-element.20.kv_ref, bf16[128,128]{1,0:T(8,128)(2,1)} %collective-permute-done.1.far_kv_ref, ...), custom_call_target="tpu_custom_call", output_to_operand_aliasing={{}: (7, {})} | custom-call | tf_op jit(solution)/shard_map/add_generated/pallas_call | solution.py:381
  36.0 25.6 %all_to_all.15.parts_ref = bf16[16,144,128]{2,1,0:T(8,128)(2,1)S(1)} all-to-all(bf16[16,144,128]{2,1,0:T(8,128)(2,1)S(1)} %bitcast.12), channel_id=1, replica_groups=mesh['grp'=16,'pair'=2,'z'=8,'core'=2] {'pair','z'}, dimensions={0} | all-to-all | bytes 1179648 | tf_op jit(solution)/shard_map/all_to_all | solution.py:392
  61.6 0.2 combine.1
  61.8 14.0 %all_to_all.16.rows_ref = bf16[8,64,256]{2,1,0:T(8,128)(2,1)S(1)} all-to-all(bf16[8,64,256]{2,1,0:T(8,128)(2,1)S(1)} %combine.1), channel_id=1, replica_groups=mesh['grp'=16,'pair'=2,'z'=8,'core'=2] {'z'}, dimensions={0} | all-to-all | bytes 524288 | tf_op jit(solution)/shard_map/all_to_all | solution.py:394
  75.9 4.5 %collective-permute-start.5 = (bf16[8,64,256]{2,1,0:T(8,128)(2,1)S(1)}, bf16[8,64,256]{2,1,0:T(8,128)(2,1)S(1)}, u32[]{:S(2)}, u32[]{:S(2)}) collective-permute-start(bf16[8,64,256]{2,1,0:T(8,128)(2,1)S(1)} %all_to_all.16.rows_ref), channel_id=1, source_target_pairs={{0,1},{1,0},{2,3},{3,2},{4,5},{5,4},{6,7},{7,6},{8,9},{9,8},{10,11... | collective-permute-start | bytes 786440 | tf_op jit(solution)/shard_map/ppermute | solution.py:395
  80.4 0.0 copy-done
  80.4 0.8 %project_near.1.before_ref = f32[64,256]{1,0:T(8,128)S(1)} custom-call(s32[5]{0:T(128)S(1)} %stack.19.meta_ref, bf16[8,64,256]{2,1,0:T(8,128)(2,1)S(1)} %all_to_all.16.rows_ref, bf16[8,2,256,256]{3,2,1,0:T(8,128)(2,1)S(1)} %bitcast.10, f32[64,256]{1,0:T(8,128)S(1)} %get-tuple-element.24.before_ref), custom_call_target="tpu_custom_call" | custom-call | tf_op jit(solution)/shard_map/project_near/pallas_call | solution.py:397
  81.3 0.3 collective-permute-done.5.rows_ref
  81.6 1.5 %project_far.1 = bf16[64,256]{1,0:T(8,128)(2,1)} custom-call(s32[5]{0:T(128)S(1)} %stack.19.meta_ref, bf16[8,64,256]{2,1,0:T(8,128)(2,1)S(1)} %collective-permute-done.5.rows_ref, bf16[8,2,256,256]{3,2,1,0:T(8,128)(2,1)S(1)} %bitcast.11, f32[64,256]{1,0:T(8,128)S(1)} %project_near.1.before_ref), custom_call_target="tpu_custom_call" | custom-call | tf_op jit(solution)/shard_map/project_far/pallas_call | solution.py:400
Async XLA Ops:
  2.0 24.8 %all-to-all-start = ((bf16[16,64,256]{2,1,0:T(8,128)(2,1)}), bf16[16,64,256]{2,1,0:T(8,128)(2,1)S(1)}, u32[]{:S(2)}, u32[]{:S(2)}) async-start(bf16[16,64,256]{2,1,0:T(8,128)(2,1)} %get-tuple-element.15), calls=%async_computation | async-start | bytes 1048576 | tf_op jit(solution)/shard_map/all_to_all | solution.py:323
  13.1 8.7 %collective-permute-start = (s32[3,32]{1,0:T(4,128)S(1)}, s32[3,32]{1,0:T(4,128)S(1)}, u32[]{:S(2)}, u32[]{:S(2)}) collective-permute-start(s32[3,32]{1,0:T(4,128)S(1)} %get-tuple-element.17.mine_ref), channel_id=1, source_target_pairs={{0,16},{16,0},{1,17},{17,1},{2,18},{18,2},{3,19},{19,3},{4,20},{20... | collective-permute-start | bytes 1160 | tf_op jit(solution)/shard_map/ppermute | solution.py:325
  16.4 10.6 %collective-permute-start.3 = (bf16[1024,1024]{1,0:T(8,128)(2,1)}, bf16[1024,1024]{1,0:T(8,128)(2,1)}, u32[]{:S(2)}, u32[]{:S(2)}) collective-permute-start(bf16[1024,1024]{1,0:T(8,128)(2,1)} %bitcast.13), channel_id=1, source_target_pairs={{0,1},{1,0},{2,3},{3,2},{4,5},{5,4},{6,7},{7,6},{8,9},{9,8},{10,11... | collective-permute-start | bytes 6291464 | tf_op jit(solution)/shard_map/ppermute | solution.py:326
  19.8 7.1 %collective-permute-start.4 = (bf16[1024,1024]{1,0:T(8,128)(2,1)}, bf16[1024,1024]{1,0:T(8,128)(2,1)}, u32[]{:S(2)}, u32[]{:S(2)}) collective-permute-start(bf16[1024,1024]{1,0:T(8,128)(2,1)} %bitcast.15), channel_id=1, source_target_pairs={{0,1},{1,0},{2,3},{3,2},{4,5},{5,4},{6,7},{7,6},{8,9},{9,8},{10,11... | collective-permute-start | bytes 6291464 | tf_op jit(solution)/shard_map/ppermute | solution.py:327
  24.2 10.2 %collective-permute-start.1 = (bf16[128,128]{1,0:T(8,128)(2,1)}, bf16[128,128]{1,0:T(8,128)(2,1)}, u32[]{:S(2)}, u32[]{:S(2)}) collective-permute-start(bf16[128,128]{1,0:T(8,128)(2,1)} %get-tuple-element.20.kv_ref), channel_id=1, source_target_pairs={{17,16},{16,17},{19,18},{18,19},{21,20},{20,21},{23,22},{22,23},{4... | collective-permute-start | bytes 98312 | tf_op jit(solution)/shard_map/ppermute | solution.py:350
  25.5 8.9 %collective-permute-start.2 = (bf16[128,128]{1,0:T(8,128)(2,1)}, bf16[128,128]{1,0:T(8,128)(2,1)}, u32[]{:S(2)}, u32[]{:S(2)}) collective-permute-start(bf16[128,128]{1,0:T(8,128)(2,1)} %get-tuple-element.20.kv_ref), channel_id=1, source_target_pairs={{8,0},{9,1},{10,2},{11,3},{12,4},{13,5},{14,6},{15,7},{25,16},{24,... | collective-permute-start | bytes 98312 | tf_op jit(solution)/shard_map/ppermute | solution.py:347
  34.4 46.0 %copy-start = (bf16[4096,256]{1,0:T(8,128)(2,1)S(1)}, bf16[4096,256]{1,0:T(8,128)(2,1)}, u32[]{:S(2)}) copy-start(bf16[4096,256]{1,0:T(8,128)(2,1)} %param.19) | copy-start | bytes 6291460
  75.9 5.7 %collective-permute-start.5 = (bf16[8,64,256]{2,1,0:T(8,128)(2,1)S(1)}, bf16[8,64,256]{2,1,0:T(8,128)(2,1)S(1)}, u32[]{:S(2)}, u32[]{:S(2)}) collective-permute-start(bf16[8,64,256]{2,1,0:T(8,128)(2,1)S(1)} %all_to_all.16.rows_ref), channel_id=1, source_target_pairs={{0,1},{1,0},{2,3},{3,2},{4,5},{5,4},{6,7},{7,6},{8,9},{9,8},{10,11... | collective-permute-start | bytes 786440 | tf_op jit(solution)/shard_map/ppermute | solution.py:395
